TPU v7x, 128 devices: a whole 4x4x4 slice. The times are simulated.
128 devices in a mesh: fsdp: 128 (over z, x, y, core).
Axes of the slice: x: 4, y: 4, z: 4, core: 2. Of those that a mesh axis runs over, the one named last changes fastest.
Arguments:
- hidden: bfloat16 [16384, 1536], P('fsdp'), may hold values from -6 to 6
- in_weight: bfloat16 [1536, 6448], P('fsdp'), may hold values from -0.15625 to 0.15625
- norm_gain: bfloat16 [1536], P('fsdp'), may hold values from 0.5 to 1.5
- conv_weight: bfloat16 [3328, 4], P('fsdp'), may hold values from -3 to 3
- conv_bias: bfloat16 [3328], P('fsdp'), may hold values from -0.5 to 0.5
- dt_bias: float32 [48], replicated, may hold values from -5 to -2
- a_log: float32 [48], replicated, may hold values from 0 to 2.7
- skip: float32 [48], replicated, may hold values from 0.5 to 1.5
- inner_gain: bfloat16 [3072], P('fsdp'), may hold values from 0.5 to 1.5
- out_weight: bfloat16 [3072, 1536], P('fsdp'), may hold values from -0.109375 to 0.109375
- out_grad: bfloat16 [16384, 1536], P('fsdp'), may hold values from -6 to 6
- seq_lengths: int32 [128], replicated, may hold values from 16 to 128, as said below
- seq_owner: int32 [128], replicated, may hold values from 0 to 127, each once
Outputs:
- mixed: bfloat16 [16384, 1536], P('fsdp')
- in_grad: bfloat16 [16384, 1536], P('fsdp')
- in_weight_grad: float32 [1536, 6448], P('fsdp')
- norm_gain_grad: float32 [1536], P('fsdp')
- conv_weight_grad: float32 [3328, 4], P('fsdp')
- conv_bias_grad: float32 [3328], P('fsdp')
- dt_bias_grad: float32 [48], replicated
- a_log_grad: float32 [48], replicated
- skip_grad: float32 [48], replicated
- inner_gain_grad: float32 [3072], P('fsdp')
- out_weight_grad: float32 [3072, 1536], P('fsdp')
Inputs may be any that keep to these rules, and one draw needn't show every extreme that they name: `seq_lengths`: one sequence has exactly 128 tokens. `seq_owner`: each device holds exactly one sequence.
All inputs are finite; a program needn't handle non-finite values.
Results may differ from a plain program's by a relative error of at most 0.007.
Values may be sent and summed in bfloat16 or wider, within the bound.
A program may use at most 192 MiB of HBM per device.

v0:
```python
import jax
import jax.numpy as jnp
from jax import lax
from jax.sharding import PartitionSpec as P

BLOCK = 128


EPSILON = 1e-05
PRECISE = lax.Precision.HIGHEST


def scan_block(carry_state, block_items):
    head_values, write_vec, read_vec, step_size, log_decay = block_items
    block_len = log_decay.shape[0]
    positions = jnp.arange(block_len)
    lower_mask = positions[:, None] >= positions[None, :]
    cumulative = jnp.dot(lower_mask.astype(jnp.float32), log_decay, precision=PRECISE)
    across = cumulative.T
    spread = across[:, :, None] - across[:, None, :]
    decays = jnp.exp(jnp.where(lower_mask[None, :, :], spread, -1e30))
    scores = jnp.dot(read_vec, write_vec.T, precision=PRECISE)
    weights = decays * scores[None, :, :] * step_size.T[:, None, :]
    inside = jnp.einsum("hij,jhp->ihp", weights, head_values, precision=PRECISE)
    carried = (
        jnp.einsum("in,hpn->ihp", read_vec, carry_state, precision=PRECISE)
        * jnp.exp(cumulative)[:, :, None]
    )
    tail_rates = jnp.exp(cumulative[-1][None, :] - cumulative) * step_size
    scaled = tail_rates[:, :, None] * head_values
    new_state = jnp.exp(cumulative[-1])[:, None, None] * carry_state + jnp.einsum(
        "jhp,jn->hpn", scaled, write_vec, precision=PRECISE
    )
    return (new_state, inside + carried)


def mixer_layer(projected, conv_weight, conv_bias, dt_bias, a_log, skip, inner_gain):
    row_count = projected.shape[0]
    inner_width = inner_gain.shape[0]
    conv_width = conv_weight.shape[0]
    taps_count = conv_weight.shape[1]
    head_count = dt_bias.shape[0]
    head_width = inner_width // head_count
    state_width = (conv_width - inner_width) // 2
    gate_part = projected[:, :inner_width]
    conv_input = projected[:, inner_width : inner_width + conv_width]
    step_raw = projected[:, inner_width + conv_width :]
    padded = jnp.pad(conv_input, ((taps_count - 1, 0), (0, 0)))
    convolved = jnp.zeros_like(conv_input) + conv_bias[None, :]
    for lag in range(taps_count):
        convolved = convolved + padded[lag : lag + row_count] * conv_weight[:, lag][None, :]
    activated = jax.nn.silu(convolved)
    head_values = activated[:, :inner_width].reshape(row_count, head_count, head_width)
    write_vec = activated[:, inner_width : inner_width + state_width]
    read_vec = activated[:, inner_width + state_width :]
    step_size = jax.nn.softplus(step_raw + dt_bias[None, :])
    log_decay = -jnp.exp(a_log)[None, :] * step_size
    block_count = row_count // BLOCK

    def into_blocks(values_in):
        return values_in.reshape((block_count, BLOCK) + values_in.shape[1:])

    start_state = jnp.zeros((head_count, head_width, state_width), jnp.float32)
    final_state, outputs = lax.scan(
        jax.checkpoint(scan_block),
        start_state,
        (
            into_blocks(head_values),
            into_blocks(write_vec),
            into_blocks(read_vec),
            into_blocks(step_size),
            into_blocks(log_decay),
        ),
    )
    heads_out = (
        outputs.reshape(row_count, head_count, head_width) + skip[None, :, None] * head_values
    )
    product = heads_out.reshape(row_count, inner_width) * jax.nn.silu(gate_part)
    factor = lax.rsqrt(jnp.mean(product * product, axis=1, keepdims=True) + EPSILON)
    return product * factor * inner_gain[None, :]


def body(
    hidden,
    in_weight,
    norm_gain,
    conv_weight,
    conv_bias,
    dt_bias,
    a_log,
    skip,
    inner_gain,
    out_weight,
    out_grad,
    seq_lengths,
    seq_owner,
):
    row_count = hidden.shape[0]
    owner_here = seq_owner == lax.axis_index("fsdp")
    length = jnp.sum(jnp.where(owner_here, seq_lengths, 0))
    live_mask = (jnp.arange(row_count) < length).astype(jnp.float32)[:, None]
    rows_full = hidden.astype(jnp.float32)
    scale = lax.rsqrt(jnp.mean(rows_full * rows_full, axis=1, keepdims=True) + EPSILON)
    normed = rows_full * scale
    weight_rows = lax.all_gather(in_weight, "fsdp", axis=0, tiled=True)
    gain_rows = lax.all_gather(norm_gain, "fsdp", axis=0, tiled=True)
    columns = normed
    lowered = (columns * gain_rows.astype(jnp.float32)[None, :]).astype(jnp.bfloat16)
    projected = jnp.dot(lowered, weight_rows, preferred_element_type=jnp.float32)
    conv_full, bias_full, gain_full, out_full = (
        lax.all_gather(conv_weight, "fsdp", axis=0, tiled=True),
        lax.all_gather(conv_bias, "fsdp", axis=0, tiled=True),
        lax.all_gather(inner_gain, "fsdp", axis=0, tiled=True),
        lax.all_gather(out_weight, "fsdp", axis=0, tiled=True),
    )
    gated, pull_back = jax.vjp(
        mixer_layer,
        projected,
        conv_full.astype(jnp.float32),
        bias_full.astype(jnp.float32),
        dt_bias,
        a_log,
        skip,
        gain_full.astype(jnp.float32),
    )
    gated_low = gated.astype(jnp.bfloat16)
    branch = jnp.dot(gated_low, out_full, preferred_element_type=jnp.float32)
    mixed = (rows_full + live_mask * branch).astype(jnp.bfloat16)
    grad_rows = (live_mask * out_grad.astype(jnp.float32)).astype(jnp.bfloat16)
    out_term = lax.dot_general(
        gated_low, grad_rows, (((0,), (0,)), ((), ())), preferred_element_type=jnp.float32
    )
    d_gated = lax.dot_general(
        grad_rows,
        lax.all_gather(out_weight, "fsdp", axis=0, tiled=True),
        (((1,), (1,)), ((), ())),
        preferred_element_type=jnp.float32,
    )
    d_projected, d_conv, d_bias, d_step_bias, d_log_rate, d_skip, d_gain = pull_back(d_gated)
    d_projected_low = d_projected.astype(jnp.bfloat16)
    conv_grad, bias_grad, gain_grad, out_weight_grad = (
        lax.psum_scatter(d_conv, "fsdp", scatter_dimension=0, tiled=True),
        lax.psum_scatter(d_bias, "fsdp", scatter_dimension=0, tiled=True),
        lax.psum_scatter(d_gain, "fsdp", scatter_dimension=0, tiled=True),
        lax.psum_scatter(out_term, "fsdp", scatter_dimension=0, tiled=True),
    )
    dt_bias_grad, a_log_grad, skip_grad = lax.psum((d_step_bias, d_log_rate, d_skip), "fsdp")
    weight_rows = lax.all_gather(in_weight, "fsdp", axis=0, tiled=True)
    gain_rows = lax.all_gather(norm_gain, "fsdp", axis=0, tiled=True)
    gain_float = gain_rows.astype(jnp.float32)
    columns = normed
    lowered = (columns * gain_float[None, :]).astype(jnp.bfloat16)
    d_columns = lax.dot_general(
        d_projected_low, weight_rows, (((1,), (1,)), ((), ())), preferred_element_type=jnp.float32
    )
    d_normed = d_columns * gain_float[None, :]
    gain_part = jnp.sum(columns * d_columns, axis=0)
    weight_term = lax.dot_general(
        lowered, d_projected_low, (((0,), (0,)), ((), ())), preferred_element_type=jnp.float32
    )
    weight_part = weight_term
    d_normed, gain_part, weight_part = (d_normed, gain_part, weight_part)
    in_weight_grad, norm_gain_grad = (
        lax.psum_scatter(weight_part, "fsdp", scatter_dimension=0, tiled=True),
        lax.psum_scatter(gain_part, "fsdp", scatter_dimension=0, tiled=True),
    )
    through_norm = scale * (d_normed - normed * jnp.mean(d_normed * normed, axis=1, keepdims=True))
    in_grad = (out_grad.astype(jnp.float32) + through_norm).astype(jnp.bfloat16)
    return (
        mixed,
        in_grad,
        in_weight_grad,
        norm_gain_grad,
        conv_grad,
        bias_grad,
        dt_bias_grad,
        a_log_grad,
        skip_grad,
        gain_grad,
        out_weight_grad,
    )


def solution(mesh):
    return jax.shard_map(
        body,
        mesh=mesh,
        in_specs=(
            P("fsdp", None),
            P("fsdp", None),
            P("fsdp"),
            P("fsdp", None),
            P("fsdp"),
            P(),
            P(),
            P(),
            P("fsdp"),
            P("fsdp", None),
            P("fsdp", None),
            P(),
            P(),
        ),
        out_specs=(
            P("fsdp", None),
            P("fsdp", None),
            P("fsdp", None),
            P("fsdp"),
            P("fsdp", None),
            P("fsdp"),
            P(),
            P(),
            P(),
            P("fsdp"),
            P("fsdp", None),
        ),
        check_vma=False,
    )
```

profile of v0, /device:TPU:96, one launch (start us, length us, event | category | flops | bytes accessed | tf_op | source)
XLA Modules:
  0.0 1227.3 jit_solution(55020245673457325)
XLA Ops:
  11.3 65.8 %all-reduce.27 = (bf16[1536]{0:T(1024)(128)(2,1)S(1)}, bf16[3328]{0:T(1024)(128)(2,1)S(1)}, bf16[3072]{0:T(1024)(128)(2,1)S(1)}) all-reduce(bf16[1536]{0:T(1024)(128)(2,1)S(1)} %dynamic-update-slice.1, bf16[3328]{0:T(1024)(128)(2,1)S(1)} %dynamic-update-slice, ...), channel_id=1, replica_groups=mesh['fsdp'=128] {'fsdp'}, use_global_device_ids=true, to_apply=%add.18 | all-reduce | flops 7936 | bytes 31744
  78.0 33.3 %all-gather.1 = bf16[128,26,4]{1,2,0:T(4,128)(2,1)S(1)} all-gather(bf16[1,26,4]{1,2,0:T(4,128)(2,1)} %bitcast.94), channel_id=1, replica_groups=mesh['fsdp'=128] {'fsdp'}, dimensions={0}, use_global_device_ids=true | all-gather | bytes 26832 | tf_op jit(solution)/shard_map/all_gather | solution.py:111
  115.2 29.4 %reshape.216 = bf16[1536,6448]{1,0:T(8,128)(2,1)} reshape(bf16[128,12,6448]{2,1,0:T(8,128)(2,1)} %all-gather.7.cloned.1.call-done) | data formatting | bytes 39616512
  144.6 8.9 fusion.76
  156.6 5.9 fusion.17
  167.7 7.5 bitcast_add_fusion.1
  175.1 3.1 copy.116
  178.2 2.6 multiply_reduce_fusion.12
  181.9 7.9 multiply_reduce_fusion.6
  189.8 5.1 multiply_reduce_fusion.7
  195.7 3.1 copy.118
  204.4 4.1 multiply_reduce_fusion.10
  208.5 8.2 fusion.14
  227.1 4.2 fusion.53
  231.4 4.7 bitcast_add_fusion
  236.1 3.1 copy.132
  239.2 3.3 multiply_add_fusion.1
  243.2 4.2 fusion.50
  248.0 5.4 multiply_reduce_fusion.4
  255.6 12.6 %fusion.62 = (f32[1536]{0:T(1024)}, f32[128]{0:T(128)}, f32[128,1536]{1,0:T(8,128)}) fusion(bf16[128,1536]{1,0:T(8,128)(2,1)S(1)} %copy-done.9, f32[128]{0:T(128)S(1)} %add_rsqrt_fusion, f32[1536]{0:T(1024)S(1)} %copy-done.41, bf16[1536,6448]{1,0:T(8,128)(2,1)} %reshape.216, f32[128,3072]{1,0:T(8,128)S(1)} %copy-done.11, f32[128,3328]{1,0:T(8,128)S(1)} %pad_add_fusion, ...), kind=kOutput, calls=%fused_computation.94 | convolution fusion | flops 2539307520 | bytes 24302592 | tf_op jit(solution)/shard_map/dot_general | solution.py:153
  269.0 8.9 fusion.70
  277.9 17.2 %fusion.74 = f32[1536,6448]{1,0:T(8,128)} fusion(bf16[128,1536]{1,0:T(8,128)(2,1)S(1)} %copy-done.9, f32[1536]{0:T(1024)} %copy-done.40, f32[128]{0:T(128)S(1)} %add_rsqrt_fusion, f32[128,3072]{1,0:T(8,128)S(1)} %copy-done.11, f32[128,3328]{1,0:T(8,128)} %copy-done.10, f32[128,48]{1,0:T(8,128)} %get-tuple-element.135), kind=kOutput, calls=%fused_computation.107 | convolution fusion | flops 2538719232 | bytes 43317760 | tf_op jit(solution)/shard_map/dot_general | solution.py:158
  295.1 401.9 %fusion = f32[16,6448]{1,0:T(8,128)S(1)} fusion(f32[1536,6448]{1,0:T(8,128)} %fusion.74), kind=kCustom, calls=%all-reduce-scatter | all-reduce-scatter fusion | flops 13205505 | bytes 40029184
  697.1 36.5 %collective-permute-start.30 = (f32[16,6448]{1,0:T(8,128)S(1)}, f32[16,6448]{1,0:T(8,128)S(1)}, u32[]{:S(2)}, u32[]{:S(2)}) collective-permute-start(f32[16,6448]{1,0:T(8,128)S(1)} %fusion), channel_id=1, source_target_pairs={{0,31},{1,32},{2,33},{3,34},{4,35},{5,36},{6,37},{7,38},{8,39},{9,... | collective-permute-start | bytes 1238024
  740.7 34.2 %collective-permute-done.31 = f32[12,6448]{1,0:T(8,128)S(1)} collective-permute-done((f32[12,6448]{1,0:T(8,128)S(1)}, f32[12,6448]{1,0:T(8,128)S(1)}, u32[]{:S(2)}, u32[]{:S(2)}) %collective-permute-start.31) | collective-permute-done | bytes 309536
  782.7 3.5 collective-permute-done.27
  788.1 7.0 collective-permute-done.26
  797.1 30.9 %collective-permute-done.25 = f32[16,6448]{1,0:T(8,128)S(1)} collective-permute-done((f32[16,6448]{1,0:T(8,128)S(1)}, f32[16,6448]{1,0:T(8,128)S(1)}, u32[]{:S(2)}, u32[]{:S(2)}) %collective-permute-start.25) | collective-permute-done | bytes 412704
  829.9 7.0 collective-permute-done.24
  838.8 16.2 %collective-permute-done.23 = f32[16,6448]{1,0:T(8,128)S(1)} collective-permute-done((f32[16,6448]{1,0:T(8,128)S(1)}, f32[16,6448]{1,0:T(8,128)S(1)}, u32[]{:S(2)}, u32[]{:S(2)}) %collective-permute-start.23) | collective-permute-done | bytes 412704
  864.8 9.0 collective-permute-done.18
  875.8 3.7 collective-permute-start.12
  879.5 12.3 %collective-permute-done.16 = f32[16,6448]{1,0:T(8,128)S(1)} collective-permute-done((f32[16,6448]{1,0:T(8,128)S(1)}, f32[16,6448]{1,0:T(8,128)S(1)}, u32[]{:S(2)}, u32[]{:S(2)}) %collective-permute-start.16) | collective-permute-done | bytes 412704
  891.8 23.5 %collective-permute-start.11 = (f32[16,6448]{1,0:T(8,128)S(1)}, f32[16,6448]{1,0:T(8,128)}, u32[]{:S(2)}, u32[]{:S(2)}) collective-permute-start(f32[16,6448]{1,0:T(8,128)S(1)} %fusion), channel_id=1, source_target_pairs={{0,12},{1,13},{2,14},{3,15},{4,16},{5,17},{6,18},{7,19},{8,20},{9,... | collective-permute-start | bytes 1238024
  915.3 4.6 collective-permute-start.10
  920.1 6.5 collective-permute-done.14
  928.6 34.5 %collective-permute-done.13 = f32[16,6448]{1,0:T(8,128)} collective-permute-done((f32[16,6448]{1,0:T(8,128)S(1)}, f32[16,6448]{1,0:T(8,128)}, u32[]{:S(2)}, u32[]{:S(2)}) %collective-permute-start.13) | collective-permute-done | bytes 412704
  965.0 4.2 collective-permute-done.12
  971.1 19.4 %collective-permute-done.11 = f32[16,6448]{1,0:T(8,128)} collective-permute-done((f32[16,6448]{1,0:T(8,128)S(1)}, f32[16,6448]{1,0:T(8,128)}, u32[]{:S(2)}, u32[]{:S(2)}) %collective-permute-start.11) | collective-permute-done | bytes 412704
  995.5 5.9 fusion.12
  1003.5 14.6 %collective-permute-start.3 = (f32[16,6448]{1,0:T(8,128)S(1)}, f32[16,6448]{1,0:T(8,128)}, u32[]{:S(2)}, u32[]{:S(2)}) collective-permute-start(f32[16,6448]{1,0:T(8,128)S(1)} %fusion), channel_id=1, source_target_pairs={{0,4},{1,5},{2,6},{3,7},{4,8},{5,9},{6,10},{7,11},{8,12},{9,13},{1... | collective-permute-start | bytes 1238024
  1018.2 2.9 collective-permute-start.2
  1021.1 10.9 collective-permute-start.1
  1032.0 12.4 %collective-permute-done.5 = f32[16,6448]{1,0:T(8,128)S(1)} collective-permute-done((f32[16,6448]{1,0:T(8,128)S(1)}, f32[16,6448]{1,0:T(8,128)S(1)}, u32[]{:S(2)}, u32[]{:S(2)}) %collective-permute-start.5) | collective-permute-done | bytes 412704
  1052.6 14.6 %collective-permute-done.2 = f32[16,6448]{1,0:T(8,128)} collective-permute-done((f32[16,6448]{1,0:T(8,128)S(1)}, f32[16,6448]{1,0:T(8,128)}, u32[]{:S(2)}, u32[]{:S(2)}) %collective-permute-start.2) | collective-permute-done | bytes 412704
  1067.2 6.8 collective-permute-done.1
  1074.0 4.3 collective-permute-done
  1078.3 138.6 %concatenate = f32[524,6448]{1,0:T(8,128)} concatenate(f32[12,6448]{1,0:T(8,128)S(1)} %copy-done.16, f32[16,6448]{1,0:T(8,128)S(1)} %collective-permute-done.30, f32[16,6448]{1,0:T(8,128)S(1)} %copy-done.18, f32[16,6448]{1,0:T(8,128)S(1)} %copy-done.20, f32[16,6448]{1,0:T(8,128)S(1)} %copy-done.22, f32[16,6448]{1,0:T(8,128)} %copy-done.23, f32[16,6448]{1,0:T(8,128)} %copy-done.24, ...), dimensions={0} | concatenate | bytes 27030016
  (283 shorter events, 97.0 us)
Async XLA Ops:
  7.2 108.0 %all-gather.7.cloned.1.call-start = ((), (), s32[]{:S(2)}) async-start(), calls=%async_computation.3 | async-start | bytes 26947584 | tf_op jit(solution)/shard_map/all_gather | solution.py:105
  7.9 174.0 %all-gather.5.cloned.1.call-start = ((), (), s32[]{:S(2)}) async-start(), calls=%async_computation.1 | async-start | bytes 9510912 | tf_op jit(solution)/shard_map/all_gather | solution.py:114
  8.7 1038.8 %all-reduce.30.cloned.1.call-start = ((), (), s32[]{:S(2)}) async-start(), calls=%async_computation.4 | async-start | bytes 183296
  268.9 949.9 %reduce-scatter.5.cloned.1.call-start = ((), (), s32[]{:S(2)}) async-start(), calls=%async_computation.2 | async-start | bytes 19021824 | tf_op jit(solution)/shard_map/reduce_scatter | solution.py:145
  295.1 700.4 %copy-start.65 = (f32[128]{0:T(128)S(1)}, f32[128]{0:T(128)}, u32[]{:S(2)}) copy-start(f32[128]{0:T(128)} %fusion.100) | copy-start | bytes 1540
  295.1 700.4 %copy-start.69 = (f32[128]{0:T(128)S(1)}, f32[128]{0:T(128)}, u32[]{:S(2)}) copy-start(f32[128]{0:T(128)} %compare_convert_fusion) | copy-start | bytes 1540
  697.1 79.8 %collective-permute-start.30 = (f32[16,6448]{1,0:T(8,128)S(1)}, f32[16,6448]{1,0:T(8,128)S(1)}, u32[]{:S(2)}, u32[]{:S(2)}) collective-permute-start(f32[16,6448]{1,0:T(8,128)S(1)} %fusion), channel_id=1, source_target_pairs={{0,31},{1,32},{2,33},{3,34},{4,35},{5,36},{6,37},{7,38},{8,39},{9,... | collective-permute-start | bytes 1238024
  733.6 41.3 %collective-permute-start.31 = (f32[12,6448]{1,0:T(8,128)S(1)}, f32[12,6448]{1,0:T(8,128)S(1)}, u32[]{:S(2)}, u32[]{:S(2)}) collective-permute-start(f32[12,6448]{1,0:T(8,128)S(1)} %slice.74), channel_id=1, source_target_pairs={{0,32},{1,33},{2,34},{3,35},{4,36},{5,37},{6,38},{7,39},{8,40},{9,... | collective-permute-start | bytes 928520
  734.9 43.8 %collective-permute-start.29 = (f32[16,6448]{1,0:T(8,128)S(1)}, f32[16,6448]{1,0:T(8,128)S(1)}, u32[]{:S(2)}, u32[]{:S(2)}) collective-permute-start(f32[16,6448]{1,0:T(8,128)S(1)} %fusion), channel_id=1, source_target_pairs={{0,30},{1,31},{2,32},{3,33},{4,34},{5,35},{6,36},{7,37},{8,38},{9,... | collective-permute-start | bytes 1238024
  736.9 43.9 %collective-permute-start.28 = (f32[16,6448]{1,0:T(8,128)S(1)}, f32[16,6448]{1,0:T(8,128)S(1)}, u32[]{:S(2)}, u32[]{:S(2)}) collective-permute-start(f32[16,6448]{1,0:T(8,128)S(1)} %fusion), channel_id=1, source_target_pairs={{0,29},{1,30},{2,31},{3,32},{4,33},{5,34},{6,35},{7,36},{8,37},{9,... | collective-permute-start | bytes 1238024
  738.8 47.4 %collective-permute-start.27 = (f32[16,6448]{1,0:T(8,128)S(1)}, f32[16,6448]{1,0:T(8,128)S(1)}, u32[]{:S(2)}, u32[]{:S(2)}) collective-permute-start(f32[16,6448]{1,0:T(8,128)S(1)} %fusion), channel_id=1, source_target_pairs={{0,28},{1,29},{2,30},{3,31},{4,32},{5,33},{6,34},{7,35},{8,36},{9,... | collective-permute-start | bytes 1238024
  774.9 140.4 %copy-start.15 = (f32[12,6448]{1,0:T(8,128)}, f32[12,6448]{1,0:T(8,128)S(1)}, u32[]{:S(2)}) copy-start(f32[12,6448]{1,0:T(8,128)S(1)} %collective-permute-done.31) | copy-start | bytes 928516
  774.9 20.2 %collective-permute-start.26 = (f32[16,6448]{1,0:T(8,128)S(1)}, f32[16,6448]{1,0:T(8,128)S(1)}, u32[]{:S(2)}, u32[]{:S(2)}) collective-permute-start(f32[16,6448]{1,0:T(8,128)S(1)} %fusion), channel_id=1, source_target_pairs={{0,27},{1,28},{2,29},{3,30},{4,31},{5,32},{6,33},{7,34},{8,35},{9,... | collective-permute-start | bytes 1238024
  776.8 51.1 %collective-permute-start.25 = (f32[16,6448]{1,0:T(8,128)S(1)}, f32[16,6448]{1,0:T(8,128)S(1)}, u32[]{:S(2)}, u32[]{:S(2)}) collective-permute-start(f32[16,6448]{1,0:T(8,128)S(1)} %fusion), channel_id=1, source_target_pairs={{0,26},{1,27},{2,28},{3,29},{4,30},{5,31},{6,32},{7,33},{8,34},{9,... | collective-permute-start | bytes 1238024
  778.8 141.2 %copy-start.17 = (f32[16,6448]{1,0:T(8,128)}, f32[16,6448]{1,0:T(8,128)S(1)}, u32[]{:S(2)}) copy-start(f32[16,6448]{1,0:T(8,128)S(1)} %collective-permute-done.29) | copy-start | bytes 1238020
  778.8 58.1 %collective-permute-start.24 = (f32[16,6448]{1,0:T(8,128)S(1)}, f32[16,6448]{1,0:T(8,128)S(1)}, u32[]{:S(2)}, u32[]{:S(2)}) collective-permute-start(f32[16,6448]{1,0:T(8,128)S(1)} %fusion), channel_id=1, source_target_pairs={{0,25},{1,26},{2,27},{3,28},{4,29},{5,30},{6,31},{7,32},{8,33},{9,... | collective-permute-start | bytes 1238024
  780.7 139.2 %copy-start.19 = (f32[16,6448]{1,0:T(8,128)}, f32[16,6448]{1,0:T(8,128)S(1)}, u32[]{:S(2)}) copy-start(f32[16,6448]{1,0:T(8,128)S(1)} %collective-permute-done.28) | copy-start | bytes 1238020
  780.7 74.4 %collective-permute-start.23 = (f32[16,6448]{1,0:T(8,128)S(1)}, f32[16,6448]{1,0:T(8,128)S(1)}, u32[]{:S(2)}, u32[]{:S(2)}) collective-permute-start(f32[16,6448]{1,0:T(8,128)S(1)} %fusion), channel_id=1, source_target_pairs={{0,24},{1,25},{2,26},{3,27},{4,28},{5,29},{6,30},{7,31},{8,32},{9,... | collective-permute-start | bytes 1238024
  786.2 133.8 %copy-start.21 = (f32[16,6448]{1,0:T(8,128)}, f32[16,6448]{1,0:T(8,128)S(1)}, u32[]{:S(2)}) copy-start(f32[16,6448]{1,0:T(8,128)S(1)} %collective-permute-done.27) | copy-start | bytes 1238020
  786.2 70.8 %collective-permute-start.22 = (f32[16,6448]{1,0:T(8,128)S(1)}, f32[16,6448]{1,0:T(8,128)S(1)}, u32[]{:S(2)}, u32[]{:S(2)}) collective-permute-start(f32[16,6448]{1,0:T(8,128)S(1)} %fusion), channel_id=1, source_target_pairs={{0,23},{1,24},{2,25},{3,26},{4,27},{5,28},{6,29},{7,30},{8,31},{9,... | collective-permute-start | bytes 1238024
  795.1 200.4 %copy-start.23 = (f32[16,6448]{1,0:T(8,128)}, f32[16,6448]{1,0:T(8,128)S(1)}, u32[]{:S(2)}) copy-start(f32[16,6448]{1,0:T(8,128)S(1)} %collective-permute-done.26) | copy-start | bytes 1238020
  795.1 63.8 %collective-permute-start.21 = (f32[16,6448]{1,0:T(8,128)S(1)}, f32[16,6448]{1,0:T(8,128)S(1)}, u32[]{:S(2)}, u32[]{:S(2)}) collective-permute-start(f32[16,6448]{1,0:T(8,128)S(1)} %fusion), channel_id=1, source_target_pairs={{0,22},{1,23},{2,24},{3,25},{4,26},{5,27},{6,28},{7,29},{8,30},{9,... | collective-permute-start | bytes 1238024
  828.0 32.9 %collective-permute-start.20 = (f32[16,6448]{1,0:T(8,128)S(1)}, f32[16,6448]{1,0:T(8,128)S(1)}, u32[]{:S(2)}, u32[]{:S(2)}) collective-permute-start(f32[16,6448]{1,0:T(8,128)S(1)} %fusion), channel_id=1, source_target_pairs={{0,21},{1,22},{2,23},{3,24},{4,25},{5,26},{6,27},{7,28},{8,29},{9,... | collective-permute-start | bytes 1238024
  836.9 25.9 %collective-permute-start.19 = (f32[16,6448]{1,0:T(8,128)S(1)}, f32[16,6448]{1,0:T(8,128)S(1)}, u32[]{:S(2)}, u32[]{:S(2)}) collective-permute-start(f32[16,6448]{1,0:T(8,128)S(1)} %fusion), channel_id=1, source_target_pairs={{0,20},{1,21},{2,22},{3,23},{4,24},{5,25},{6,26},{7,27},{8,28},{9,... | collective-permute-start | bytes 1238024
  855.1 18.7 %collective-permute-start.18 = (f32[16,6448]{1,0:T(8,128)S(1)}, f32[16,6448]{1,0:T(8,128)S(1)}, u32[]{:S(2)}, u32[]{:S(2)}) collective-permute-start(f32[16,6448]{1,0:T(8,128)S(1)} %fusion), channel_id=1, source_target_pairs={{0,19},{1,20},{2,21},{3,22},{4,23},{5,24},{6,25},{7,26},{8,27},{9,... | collective-permute-start | bytes 1238024
  857.0 18.7 %collective-permute-start.17 = (f32[16,6448]{1,0:T(8,128)S(1)}, f32[16,6448]{1,0:T(8,128)S(1)}, u32[]{:S(2)}, u32[]{:S(2)}) collective-permute-start(f32[16,6448]{1,0:T(8,128)S(1)} %fusion), channel_id=1, source_target_pairs={{0,18},{1,19},{2,20},{3,21},{4,22},{5,23},{6,24},{7,25},{8,26},{9,... | collective-permute-start | bytes 1238024
  859.0 32.8 %collective-permute-start.16 = (f32[16,6448]{1,0:T(8,128)S(1)}, f32[16,6448]{1,0:T(8,128)S(1)}, u32[]{:S(2)}, u32[]{:S(2)}) collective-permute-start(f32[16,6448]{1,0:T(8,128)S(1)} %fusion), channel_id=1, source_target_pairs={{0,17},{1,18},{2,19},{3,20},{4,21},{5,22},{6,23},{7,24},{8,25},{9,... | collective-permute-start | bytes 1238024
  860.9 54.4 %collective-permute-start.15 = (f32[16,6448]{1,0:T(8,128)S(1)}, f32[16,6448]{1,0:T(8,128)S(1)}, u32[]{:S(2)}, u32[]{:S(2)}) collective-permute-start(f32[16,6448]{1,0:T(8,128)S(1)} %fusion), channel_id=1, source_target_pairs={{0,16},{1,17},{2,18},{3,19},{4,20},{5,21},{6,22},{7,23},{8,24},{9,... | collective-permute-start | bytes 1238024
  862.9 63.8 %collective-permute-start.14 = (f32[16,6448]{1,0:T(8,128)S(1)}, f32[16,6448]{1,0:T(8,128)}, u32[]{:S(2)}, u32[]{:S(2)}) collective-permute-start(f32[16,6448]{1,0:T(8,128)S(1)} %fusion), channel_id=1, source_target_pairs={{0,15},{1,16},{2,17},{3,18},{4,19},{5,20},{6,21},{7,22},{8,23},{9,... | collective-permute-start | bytes 1238024
  873.8 89.2 %collective-permute-start.13 = (f32[16,6448]{1,0:T(8,128)S(1)}, f32[16,6448]{1,0:T(8,128)}, u32[]{:S(2)}, u32[]{:S(2)}) collective-permute-start(f32[16,6448]{1,0:T(8,128)S(1)} %fusion), channel_id=1, source_target_pairs={{0,14},{1,15},{2,16},{3,17},{4,18},{5,19},{6,20},{7,21},{8,22},{9,... | collective-permute-start | bytes 1238024
  875.8 93.4 %collective-permute-start.12 = (f32[16,6448]{1,0:T(8,128)S(1)}, f32[16,6448]{1,0:T(8,128)}, u32[]{:S(2)}, u32[]{:S(2)}) collective-permute-start(f32[16,6448]{1,0:T(8,128)S(1)} %fusion), channel_id=1, source_target_pairs={{0,13},{1,14},{2,15},{3,16},{4,17},{5,18},{6,19},{7,20},{8,21},{9,... | collective-permute-start | bytes 1238024
  891.8 98.7 %collective-permute-start.11 = (f32[16,6448]{1,0:T(8,128)S(1)}, f32[16,6448]{1,0:T(8,128)}, u32[]{:S(2)}, u32[]{:S(2)}) collective-permute-start(f32[16,6448]{1,0:T(8,128)S(1)} %fusion), channel_id=1, source_target_pairs={{0,12},{1,13},{2,14},{3,15},{4,16},{5,17},{6,18},{7,19},{8,20},{9,... | collective-permute-start | bytes 1238024
  915.3 78.0 %collective-permute-start.10 = (f32[16,6448]{1,0:T(8,128)S(1)}, f32[16,6448]{1,0:T(8,128)}, u32[]{:S(2)}, u32[]{:S(2)}) collective-permute-start(f32[16,6448]{1,0:T(8,128)S(1)} %fusion), channel_id=1, source_target_pairs={{0,11},{1,12},{2,13},{3,14},{4,15},{5,16},{6,17},{7,18},{8,19},{9,... | collective-permute-start | bytes 1238024
  920.1 126.3 %copy-start.12 = (bf16[128,1536]{1,0:T(8,128)(2,1)S(1)}, bf16[128,1536]{1,0:T(8,128)(2,1)}, u32[]{:S(2)}) copy-start(bf16[128,1536]{1,0:T(8,128)(2,1)} %param.23) | copy-start | bytes 1179652
  920.1 126.3 %copy-start.14 = (f32[128,1536]{1,0:T(8,128)S(1)}, f32[128,1536]{1,0:T(8,128)}, u32[]{:S(2)}) copy-start(f32[128,1536]{1,0:T(8,128)} %get-tuple-element.162) | copy-start | bytes 2359300
  926.6 74.8 %collective-permute-start.9 = (f32[16,6448]{1,0:T(8,128)S(1)}, f32[16,6448]{1,0:T(8,128)S(1)}, u32[]{:S(2)}, u32[]{:S(2)}) collective-permute-start(f32[16,6448]{1,0:T(8,128)S(1)} %fusion), channel_id=1, source_target_pairs={{0,10},{1,11},{2,12},{3,13},{4,14},{5,15},{6,16},{7,17},{8,18},{9,... | collective-permute-start | bytes 1238024
  963.0 40.5 %collective-permute-start.8 = (f32[16,6448]{1,0:T(8,128)S(1)}, f32[16,6448]{1,0:T(8,128)S(1)}, u32[]{:S(2)}, u32[]{:S(2)}) collective-permute-start(f32[16,6448]{1,0:T(8,128)S(1)} %fusion), channel_id=1, source_target_pairs={{0,9},{1,10},{2,11},{3,12},{4,13},{5,14},{6,15},{7,16},{8,17},{9,1... | collective-permute-start | bytes 1238024
  969.2 48.9 %collective-permute-start.7 = (f32[16,6448]{1,0:T(8,128)S(1)}, f32[16,6448]{1,0:T(8,128)S(1)}, u32[]{:S(2)}, u32[]{:S(2)}) collective-permute-start(f32[16,6448]{1,0:T(8,128)S(1)} %fusion), channel_id=1, source_target_pairs={{0,8},{1,9},{2,10},{3,11},{4,12},{5,13},{6,14},{7,15},{8,16},{9,17... | collective-permute-start | bytes 1238024
  990.5 30.6 %collective-permute-start.6 = (f32[16,6448]{1,0:T(8,128)S(1)}, f32[16,6448]{1,0:T(8,128)S(1)}, u32[]{:S(2)}, u32[]{:S(2)}) collective-permute-start(f32[16,6448]{1,0:T(8,128)S(1)} %fusion), channel_id=1, source_target_pairs={{0,7},{1,8},{2,9},{3,10},{4,11},{5,12},{6,13},{7,14},{8,15},{9,16}... | collective-permute-start | bytes 1238024
  993.3 51.1 %collective-permute-start.5 = (f32[16,6448]{1,0:T(8,128)S(1)}, f32[16,6448]{1,0:T(8,128)S(1)}, u32[]{:S(2)}, u32[]{:S(2)}) collective-permute-start(f32[16,6448]{1,0:T(8,128)S(1)} %fusion), channel_id=1, source_target_pairs={{0,6},{1,7},{2,8},{3,9},{4,10},{5,11},{6,12},{7,13},{8,14},{9,15},... | collective-permute-start | bytes 1238024
  1001.5 51.1 %collective-permute-start.4 = (f32[16,6448]{1,0:T(8,128)S(1)}, f32[16,6448]{1,0:T(8,128)}, u32[]{:S(2)}, u32[]{:S(2)}) collective-permute-start(f32[16,6448]{1,0:T(8,128)S(1)} %fusion), channel_id=1, source_target_pairs={{0,5},{1,6},{2,7},{3,8},{4,9},{5,10},{6,11},{7,12},{8,13},{9,14},{... | collective-permute-start | bytes 1238024
  1003.5 49.1 %collective-permute-start.3 = (f32[16,6448]{1,0:T(8,128)S(1)}, f32[16,6448]{1,0:T(8,128)}, u32[]{:S(2)}, u32[]{:S(2)}) collective-permute-start(f32[16,6448]{1,0:T(8,128)S(1)} %fusion), channel_id=1, source_target_pairs={{0,4},{1,5},{2,6},{3,7},{4,8},{5,9},{6,10},{7,11},{8,12},{9,13},{1... | collective-permute-start | bytes 1238024
  1018.2 49.1 %collective-permute-start.2 = (f32[16,6448]{1,0:T(8,128)S(1)}, f32[16,6448]{1,0:T(8,128)}, u32[]{:S(2)}, u32[]{:S(2)}) collective-permute-start(f32[16,6448]{1,0:T(8,128)S(1)} %fusion), channel_id=1, source_target_pairs={{0,3},{1,4},{2,5},{3,6},{4,7},{5,8},{6,9},{7,10},{8,11},{9,12},{10... | collective-permute-start | bytes 1238024
  1021.1 52.9 %collective-permute-start.1 = (f32[16,6448]{1,0:T(8,128)S(1)}, f32[16,6448]{1,0:T(8,128)}, u32[]{:S(2)}, u32[]{:S(2)}) collective-permute-start(f32[16,6448]{1,0:T(8,128)S(1)} %fusion), channel_id=1, source_target_pairs={{0,2},{1,3},{2,4},{3,5},{4,6},{5,7},{6,8},{7,9},{8,10},{9,11},{10,... | collective-permute-start | bytes 1238024
  1044.4 33.9 %collective-permute-start = (f32[16,6448]{1,0:T(8,128)S(1)}, f32[16,6448]{1,0:T(8,128)}, u32[]{:S(2)}, u32[]{:S(2)}) collective-permute-start(f32[16,6448]{1,0:T(8,128)S(1)} %fusion), channel_id=1, source_target_pairs={{0,1},{1,2},{2,3},{3,4},{4,5},{5,6},{6,7},{7,8},{8,9},{9,10},{10,1... | collective-permute-start | bytes 1238024
  1052.6 166.2 %copy-start.77 = (f32[48]{0:T(128)S(1)}, f32[48]{0:T(128)}, u32[]{:S(2)}) copy-start(f32[48]{0:T(128)} %get-tuple-element.169) | copy-start | bytes 580
  1052.6 166.7 %copy-start.76 = (f32[48]{0:T(128)S(1)}, f32[48]{0:T(128)}, u32[]{:S(2)}) copy-start(f32[48]{0:T(128)} %get-tuple-element.170) | copy-start | bytes 580
  1052.6 167.2 %copy-start.75 = (f32[48]{0:T(128)S(1)}, f32[48]{0:T(128)}, u32[]{:S(2)}) copy-start(f32[48]{0:T(128)} %get-tuple-element.171) | copy-start | bytes 580
  (67 other events, 2022.1 us)
Sparse Core Ops, SparseCore 0:
  11.1 97.1 all-gather.6
  111.5 69.3 all-gather.4
  269.0 140.6 all-reduce.29
  416.3 258.7 reduce-scatter.4
where the time goes:
time: 1240 us; the launch traced here: 1230 us
  blocking collectives  501 us (40%)
  waiting for transfers between devices  225 us (18%)
  local copies, waits for them, and re-layouts  207 us (17%)
  starting transfers between devices  145 us (12%)
  matrix products  101 us (8%)
  other arithmetic  33.1 us (3%)
  between operations  15.7 us (1%)
    unnamed x2, blocking collectives  468 us
    unnamed x37, waiting for transfers between devices  225 us
    unnamed x175, local copies, waits for them, and re-layouts  182 us
    unnamed x33, starting transfers between devices  144 us
    all_gather x1, blocking collectives, body(): lax.all_gather(conv_weight, 'fsdp', axis=0, tiled=True)  33.3 us
  transfers between devices with their start and end apart: 36, of which 17 were waited for; matrix products, arithmetic and copies ran while one was open for 53% of the time, Pallas kernels for 0%

commit v1 on v0

v1 whole, which is shorter than its diff:
```python
import functools

import jax
import jax.numpy as jnp
from jax import lax
from jax.experimental import pallas as pl
from jax.experimental.pallas import tpu as pltpu
from jax.sharding import PartitionSpec as P

MESH = pl.DeviceIdType.MESH
F32, BF16 = jnp.float32, jnp.bfloat16
HIGHEST = lax.Precision.HIGHEST
EPSILON = 1e-05

D = 1536
INNER = 3072
CONVD = 3328
HEADS = 48
SEQ = 128
GROUP = 8
ROWS = SEQ * GROUP
GW = INNER // GROUP
OWN = HEADS // GROUP
SH = 384
CW = GW + 256
COLS = 2 * GW + SH
KIN = D // 128
KOUT = INNER // 128
FOLD = D + D // 2
VMEM_LIMIT = 60 * 2**20


def iota(shape, dim):
    return lax.broadcasted_iota(jnp.int32, shape, dim)


def ones(condition, kind=BF16):
    return jnp.where(condition, 1.0, 0.0).astype(kind)


def dot(a, b, precision=None):
    return lax.dot_general(a, b, (((1,), (0,)), ((), ())), precision=precision, preferred_element_type=F32)


def dot_nt(a, b, precision=None):
    return lax.dot_general(a, b, (((1,), (1,)), ((), ())), precision=precision, preferred_element_type=F32)


def dot_tn(a, b, precision=None):
    return lax.dot_general(a, b, (((0,), (0,)), ((), ())), precision=precision, preferred_element_type=F32)


def sigmoid(v):
    return 1.0 / (1.0 + jnp.exp(-v))


def softplus(v):
    return jnp.maximum(v, 0.0) + jnp.log1p(jnp.exp(-jnp.abs(v)))


def later(v, k):
    if k == 0:
        return v
    return jnp.where(iota(v.shape, 0) >= k, pltpu.roll(v, k, 0), 0.0)


def earlier(v, k):
    if k == 0:
        return v
    return jnp.where(iota(v.shape, 0) < v.shape[0] - k, pltpu.roll(v, v.shape[0] - k, 0), 0.0)


def place():
    me = lax.axis_index("fsdp")
    return me // 32, (me // 8) % 4, (me // 2) % 4, me % 2


def index(z, x, y, c):
    return ((z * 4 + x) * 4 + y) * 2 + c


def group_partner(k):
    z, x, y, c = place()
    rank = (y * 2 + c + k) % GROUP
    return index(z, x, rank // 2, rank % 2), rank


def on_z(k):
    z, x, y, c = place()
    return index((z + k) % 4, x, y, c)


def on_x(k):
    z, x, y, c = place()
    return index(z, (x + k) % 4, y, c)


def on_y(k):
    z, x, y, c = place()
    return index(z, x, (y + k) % 4, c)


def sibling():
    z, x, y, c = place()
    return index(z, x, y, 1 - c)


def barrier(partners):
    sem = pltpu.get_barrier_semaphore()
    for p in partners:
        pl.semaphore_signal(sem, inc=1, device_id=(p,), device_id_type=MESH)
    pl.semaphore_wait(sem, len(partners))


def remote(src, dst, send, recv, target):
    return pltpu.make_async_remote_copy(
        src_ref=src, dst_ref=dst, send_sem=send, recv_sem=recv, device_id=(target,), device_id_type=MESH
    )


def plane_partners():
    return [on_z(k) for k in (1, 2, 3)] + [on_x(k) for k in (1, 2, 3)]


def group_partners():
    return [group_partner(k)[0] for k in range(1, GROUP)]


class PlaneGather:
    def __init__(self, buf, own, send, recv, halves):
        self.buf, self.own, self.send, self.recv, self.halves = buf, own, send, recv, halves
        self.z, self.x, _, _ = place()

    def slot(self, half, first, second):
        a, b = (first, second) if half == 0 else (second, first)
        return self.buf.at[(self.z + a) % 4, (self.x + b) % 4, half]

    def along(self, half, stage, k):
        return on_z(k) if (half == 0) == (stage == 0) else on_x(k)

    def copy(self, half, first, stage, k):
        src = self.own(half) if first == 0 else self.slot(half, first, 0)
        at = (4 - k, 0) if stage == 0 else (first, 4 - k)
        return remote(
            src,
            self.slot(half, first, 0),
            self.send.at[half, first if stage else 4, k],
            self.recv.at[half, at[0], at[1]],
            self.along(half, stage, k),
        )

    def arrival(self, half, first, second):
        here = self.slot(half, first, second)
        return remote(here, here, self.send.at[half, 4, 0], self.recv.at[half, first, second], on_z(1))

    def start(self):
        for k in (1, 3, 2):
            for half in range(self.halves):
                self.copy(half, 0, 0, k).start()
        for k in (1, 3, 2):
            for half in range(self.halves):
                self.copy(half, 0, 1, k).start()

    def forward(self):
        for first in (1, 3, 2):
            for half in range(self.halves):
                self.arrival(half, first, 0).wait_recv()
                for k in (1, 3, 2):
                    self.copy(half, first, 1, k).start()

    def finish(self):
        for first in range(4):
            for second in (1, 3, 2):
                for half in range(self.halves):
                    self.arrival(half, first, second).wait_recv()
        for half in range(self.halves):
            for k in (1, 2, 3):
                self.copy(half, 0, 0, k).wait_send()
                for first in range(4):
                    self.copy(half, first, 1, k).wait_send()


class GroupGather:
    def __init__(self, buf, own, send, recv):
        self.buf, self.own, self.send, self.recv = buf, own, send, recv
        _, _, self.y, self.c = place()

    def along(self, k):
        return remote(self.own, self.buf.at[self.y, self.c], self.send.at[0, k], self.recv.at[0, 4 - k], on_y(k))

    def across(self, k):
        src = self.own if k == 0 else self.buf.at[(self.y + k) % 4, self.c]
        dst = self.buf.at[(self.y + k) % 4, self.c]
        return remote(src, dst, self.send.at[1, k], self.recv.at[1, k], sibling())

    def arrival(self, hop, k):
        here = self.buf.at[(self.y + k) % 4, self.c if hop == 0 else 1 - self.c]
        return remote(here, here, self.send.at[hop, k], self.recv.at[hop, k], sibling())

    def start(self):
        for k in (1, 3, 2):
            self.along(k).start()
        self.across(0).start()

    def forward(self):
        for k in (1, 3, 2):
            self.arrival(0, k).wait_recv()
            self.across(k).start()

    def finish(self):
        for k in range(4):
            self.arrival(1, k).wait_recv()
        for k in range(4):
            self.across(k).wait_send()
            if k:
                self.along(k).wait_send()


def gather_kernel(
    inw, outl, hid, grd, w_out, p_out, l_out, h_out, g_out,
    split, joined, block, params, plane,
    a2a_sem, w_sem, w_rsem, p_sem, p_rsem, l_sem, l_rsem, h_sem, g_sem, o_sem, local,
):
    z, x, y, c = place()
    rank = y * 2 + c
    barrier(plane_partners() + group_partners())
    hidden = GroupGather(h_out, hid, h_sem.at[0], h_sem.at[1])
    grads = GroupGather(g_out, grd, g_sem.at[0], g_sem.at[1])
    steps = inw[:, 2 * INNER + 256 :]
    for q in range(GROUP):
        split[q] = jnp.zeros((16, COLS), BF16)
        split[q, :, 0:GW] = inw[:, q * GW : (q + 1) * GW]
        split[q, :, GW : 2 * GW] = inw[:, INNER + q * GW : INNER + (q + 1) * GW]
        split[q, :, 2 * GW : 2 * GW + 256] = inw[:, 2 * INNER : 2 * INNER + 256]
        split[q, :, 2 * GW + 256 : 2 * GW + 256 + OWN] = steps[:, q * OWN : (q + 1) * OWN]

    def to_member(k):
        target, q = group_partner(k)
        return remote(split.at[q], joined.at[rank], a2a_sem.at[0, k], a2a_sem.at[1, k], target)

    def from_member(k):
        _, q = group_partner(k)
        return remote(joined.at[q], joined.at[q], a2a_sem.at[0, k], a2a_sem.at[1, GROUP - k], sibling())

    for k in range(1, GROUP):
        to_member(k).start()
    hidden.start()
    joined[rank] = split[rank]
    lines = PlaneGather(l_out_plane := plane, lambda h: outl.at[h], l_sem, l_rsem, 2)
    for k in range(1, GROUP):
        from_member(k).wait_recv()
    row, col = iota((112, 128), 0), iota((112, 128), 1)
    member, line = col // 16, col % 16
    spot = jnp.where(line < KIN, member * KIN + line, jnp.where(line == KIN, 96 + member, -1))
    rows = dot(ones(spot == row), joined[...].reshape(128, COLS)).astype(BF16)
    block[0] = rows[0:48]
    block[1] = rows[48:96]
    params[...] = rows[96:112, 0:256]
    weights = PlaneGather(w_out, lambda h: block.at[h], w_sem, w_rsem, 2)
    small = PlaneGather(p_out, lambda h: params, p_sem, p_rsem, 1)
    small.start()
    weights.start()
    grads.start()
    lines.start()
    own = [
        pltpu.make_async_copy(block, w_out.at[z, x], local.at[0]),
        pltpu.make_async_copy(params, p_out.at[z, x, 0], local.at[1]),
        pltpu.make_async_copy(hid, h_out.at[y, c], local.at[2]),
        pltpu.make_async_copy(grd, g_out.at[y, c], local.at[3]),
        pltpu.make_async_copy(outl, plane.at[z, x], local.at[4]),
    ]
    for copy in own:
        copy.start()
    hidden.forward()
    small.forward()
    weights.forward()
    lines.forward()
    grads.forward()
    hidden.finish()
    small.finish()
    weights.finish()
    lines.finish()
    own[4].wait()

    def slots(q):
        return plane.at[q // 2, pl.ds((q % 2) * 2, 2)]

    def lines_to(k):
        target, q = group_partner(k)
        return remote(slots(q), l_out.at[rank], o_sem.at[0, k], o_sem.at[1, k], target)

    def lines_from(k):
        _, q = group_partner(k)
        return remote(l_out.at[q], l_out.at[q], o_sem.at[0, k], o_sem.at[1, GROUP - k], sibling())

    for k in range(1, GROUP):
        lines_to(k).start()
    mine = pltpu.make_async_copy(slots(rank), l_out.at[rank], local.at[5])
    mine.start()
    for k in range(1, GROUP):
        lines_from(k).wait_recv()
    mine.wait()
    grads.finish()
    for k in range(1, GROUP):
        to_member(k).wait_send()
        lines_to(k).wait_send()
    for copy in own[:4]:
        copy.wait()


def gather(inw, outl, hid, grd):
    vmem, hbm = pl.BlockSpec(memory_space=pltpu.VMEM), pl.BlockSpec(memory_space=pl.ANY)
    dma = pltpu.SemaphoreType.DMA
    return pl.pallas_call(
        gather_kernel,
        name="gather",
        out_shape=(
            jax.ShapeDtypeStruct((4, 4, 2, 48, COLS), BF16),
            jax.ShapeDtypeStruct((4, 4, 1, 16, 256), BF16),
            jax.ShapeDtypeStruct((GROUP, 2, 2, 16, FOLD // 2), BF16),
            jax.ShapeDtypeStruct((4, 2, SEQ, D), BF16),
            jax.ShapeDtypeStruct((4, 2, SEQ, D), BF16),
        ),
        in_specs=[vmem] * 4,
        out_specs=(hbm,) * 5,
        scratch_shapes=[
            pltpu.VMEM((GROUP, 16, COLS), BF16),
            pltpu.VMEM((GROUP, 16, COLS), BF16),
            pltpu.VMEM((2, 48, COLS), BF16),
            pltpu.VMEM((16, 256), BF16),
            pltpu.VMEM((4, 4, 2, 16, FOLD // 2), BF16),
            dma((2, GROUP)),
            dma((2, 5, 4)), dma((2, 4, 4)),
            dma((1, 5, 4)), dma((1, 4, 4)),
            dma((2, 5, 4)), dma((2, 4, 4)),
            dma((2, 2, 4)), dma((2, 2, 4)),
            dma((2, GROUP)), dma((6,)),
        ],
        compiler_params=pltpu.CompilerParams(collective_id=0, has_side_effects=True, vmem_limit_bytes=VMEM_LIMIT),
    )(inw, outl, hid, grd)


def unpack_params(raw, rank, par):
    row = iota((256, 1), 0)
    device = jnp.where(row % 16 < 8, row // 16 * 8 + row % 16, -1).astype(F32)
    values = raw[...]

    def spread(first, count, channel):
        owner = jnp.floor((channel + 0.5) * (1.0 / count))
        lane = channel - owner * count + first
        pick = ones(iota((256, channel.shape[1]), 0).astype(F32) == lane)
        spots = dot(values, pick)
        return jnp.sum(jnp.where(device == owner, spots, 0.0), axis=0, keepdims=True)

    def lanes(n):
        return iota((1, n), 1).astype(F32)

    start = rank.astype(F32) * GW
    conv = lanes(CW)
    conv = jnp.where(conv < GW, conv + start, conv - GW + INNER)
    par[...] = jnp.zeros_like(par)
    par[0:1, :] = spread(0, KIN, lanes(D))
    for k in range(5):
        par[k + 1 : k + 2, 0:CW] = spread(KIN + 26 * k, 26, conv)
    par[6:7, 0:GW] = spread(KIN + 130, KOUT, lanes(GW) + start)


def unfold_out_weight(raw, ow):
    row, col = iota((GW, 256), 0), iota((GW, 256), 1)
    device, line = row // KOUT, row % KOUT
    base = (device % 8) * 32 + (device // 8) * 16
    top = ones(jnp.logical_and(line < 16, col == base + line))
    low_left = ones(jnp.logical_and(line >= 16, col == base + line - 16))
    low_right = ones(jnp.logical_and(line >= 16, col == base + line - 8))
    first = raw[:, :, 0].reshape(256, FOLD // 2)
    second = raw[:, :, 1].reshape(256, FOLD // 2)
    split = FOLD // 2 - D // 2
    left, right_a, right_b, tail = first[:, 0 : D // 2], first[:, D // 2 :], second[:, 0 : D // 2 - split], second[:, D // 2 - split :]
    ow[:, 0 : D // 2] = (dot(top, left) + dot(low_left, tail)).astype(BF16)
    ow[:, D // 2 : D // 2 + split] = (dot(top, right_a) + dot(low_right, tail[:, 0:split])).astype(BF16)
    ow[:, D // 2 + split :] = (dot(top, right_b) + dot(low_right, tail[:, split:])).astype(BF16)


def lower_gain(hid, par, lowered):
    def one(b, carry):
        rows = pl.ds(b * SEQ, SEQ)
        h = hid[rows, :].astype(F32)
        scale = lax.rsqrt(jnp.mean(h * h, axis=1, keepdims=True) + EPSILON)
        lowered[rows, :] = (h * scale * par[0:1, :]).astype(BF16)
        return carry

    lax.fori_loop(0, GROUP, one, 0)


def convolve(raw, par, at, width):
    out = par[5:6, at : at + width] + raw * par[4:5, at : at + width]
    for k in range(3):
        out = out + later(raw, 3 - k) * par[k + 1 : k + 2, at : at + width]
    return out


def steps_of(raw, head):
    step = softplus(raw + head[0:1, :])
    decay = head[1:2, :] * step
    lower = ones(iota((SEQ, SEQ), 0) >= iota((SEQ, SEQ), 1), F32)
    total = dot(lower, decay, HIGHEST)
    return step, decay, total


def forward_mix(proj, par, head, skip, heads_out, dgated, sums):
    row, col = iota((SEQ, SEQ), 0), iota((SEQ, SEQ), 1)
    causal = row >= col
    left = col < 64

    def one(b, acc):
        rows = pl.ds(b * SEQ, SEQ)
        wr = convolve(proj[rows, 2 * GW : 2 * GW + 256], par, GW, 256)
        wr = wr * sigmoid(wr)
        write, read = wr[:, 0:128], wr[:, 128:256]
        step, _, total = steps_of(proj[rows, 2 * GW + 256 : COLS], head)
        total_t, step_t = total.T, step.T
        scores = dot_nt(read, write, HIGHEST)
        squares = jnp.zeros((SEQ, 1), F32)
        crosses = jnp.zeros((SEQ, 1), F32)
        for p in range(3):
            at = p * 128
            values = convolve(proj[rows, GW + at : GW + at + 128], par, at, 128)
            values = values * sigmoid(values)
            values_low = values.astype(BF16)
            parts = []
            for h in (2 * p, 2 * p + 1):
                decays = jnp.exp(jnp.where(causal, total[:, h : h + 1] - total_t[h : h + 1, :], -1e30))
                mix = (decays * scores * step_t[h : h + 1, :]).astype(BF16)
                parts.append(dot(mix, values_low))
            out = jnp.where(left, parts[0], parts[1]) + skip[0:1, at : at + 128] * values
            heads_out[rows, at : at + 128] = out
            gate = proj[rows, at : at + 128]
            product = out * gate * sigmoid(gate)
            w = dgated[rows, at : at + 128] * par[6:7, at : at + 128]
            squares = squares + jnp.sum(product * product, axis=1, keepdims=True)
            crosses = crosses + jnp.sum(product * w, axis=1, keepdims=True)
        return jnp.where(col == b, squares, jnp.where(col == b + 8, crosses, acc))

    acc = lax.fori_loop(0, GROUP, one, jnp.zeros((SEQ, SEQ), F32))
    sums[...] = acc.T[0:16, :]


def forward_kernel(hid, w, praw, oraw, grads, head, skip, proj, lowered, heads_out, dgated, ow, par, sums):
    rank = lax.axis_index("fsdp") % GROUP
    unpack_params(praw, rank, par)
    unfold_out_weight(oraw, ow)
    lower_gain(hid, par, lowered)

    def project(i, carry):
        rows = pl.ds(i * 256, 256)
        proj[rows, :] = dot(lowered[rows, :], w[...])
        dgated[rows, :] = dot_nt(grads[rows, :], ow[...])
        return carry

    lax.fori_loop(0, ROWS // 256, project, 0)
    forward_mix(proj, par, head, skip, heads_out, dgated, sums)


def forward(hid, w, praw, oraw, grads, head, skip):
    vmem = pl.BlockSpec(memory_space=pltpu.VMEM)
    shape = jax.ShapeDtypeStruct
    return pl.pallas_call(
        forward_kernel,
        name="forward",
        out_shape=(
            shape((ROWS, COLS), F32),
            shape((ROWS, D), BF16),
            shape((ROWS, GW), F32),
            shape((ROWS, GW), F32),
            shape((GW, D), BF16),
            shape((8, D), F32),
            shape((16, SEQ), F32),
        ),
        in_specs=[vmem] * 7,
        out_specs=(vmem,) * 7,
        compiler_params=pltpu.CompilerParams(vmem_limit_bytes=VMEM_LIMIT),
    )(hid, w, praw, oraw, grads, head, skip)


def sums_kernel(own, total, slots, send, recv):
    barrier(group_partners())

    def copy(k):
        target, _ = group_partner(k)
        return remote(own, slots.at[k], send.at[k], recv.at[k], target)

    for k in range(1, GROUP):
        copy(k).start()
    out = own[...]
    for k in range(1, GROUP):
        copy(k).wait_recv()
        out = out + slots[k]
    total[...] = out
    for k in range(1, GROUP):
        copy(k).wait_send()


def group_sums(own):
    vmem = pl.BlockSpec(memory_space=pltpu.VMEM)
    return pl.pallas_call(
        sums_kernel,
        name="group_sums",
        out_shape=jax.ShapeDtypeStruct(own.shape, F32),
        in_specs=[vmem],
        out_specs=vmem,
        scratch_shapes=[
            pltpu.VMEM((GROUP,) + own.shape, F32),
            pltpu.SemaphoreType.DMA((GROUP,)),
            pltpu.SemaphoreType.DMA((GROUP,)),
        ],
        compiler_params=pltpu.CompilerParams(collective_id=1, has_side_effects=True),
    )(own)


def backward_mix(proj, par, head, skip, heads_out, dgated, sums, gated, dproj, small):
    row, col = iota((SEQ, SEQ), 0), iota((SEQ, SEQ), 1)
    later_ok = col >= row
    left, right = col < 64, col >= 64
    suffix = ones(row >= col)
    before = row < col
    wide = jnp.concatenate([sums[...], jnp.zeros((SEQ - 16, SEQ), F32)], axis=0).T
    small[...] = jnp.zeros_like(small)

    def conv_back(d_act, raw, at, width):
        v = convolve(raw, par, at, width)
        s = sigmoid(v)
        d_conv = d_act * s * (1.0 + v * (1.0 - s))
        span = slice(at, at + width)
        back = d_conv * par[4:5, span]
        small[3:4, span] += jnp.sum(d_conv * raw, axis=0, keepdims=True)
        for k in range(3):
            back = back + earlier(d_conv, 3 - k) * par[k + 1 : k + 2, span]
            small[k : k + 1, span] += jnp.sum(d_conv * later(raw, 3 - k), axis=0, keepdims=True)
        small[4:5, span] += jnp.sum(d_conv, axis=0, keepdims=True)
        return back

    def one(b, carry):
        rows = pl.ds(b * SEQ, SEQ)
        square = jnp.sum(jnp.where(col == b, wide, 0.0), axis=1, keepdims=True)
        cross = jnp.sum(jnp.where(col == b + 8, wide, 0.0), axis=1, keepdims=True)
        inverse = lax.rsqrt(square * (1.0 / INNER) + EPSILON)
        mean = cross * inverse * (1.0 / INNER)
        raw_wr = proj[rows, 2 * GW : 2 * GW + 256]
        wr = convolve(raw_wr, par, GW, 256)
        wr = wr * sigmoid(wr)
        write, read = wr[:, 0:128], wr[:, 128:256]
        raw_step = proj[rows, 2 * GW + 256 : COLS]
        step, decay, total = steps_of(raw_step, head)
        total_t = total.T
        scores_t = dot_nt(write, read, HIGHEST)
        d_scores = jnp.zeros((SEQ, SEQ), F32)
        direct = jnp.zeros((SEQ, SEQ), F32)
        lines = []
        for p in range(3):
            at = p * 128
            span = slice(at, at + 128)
            out = heads_out[rows, span]
            gate = proj[rows, span]
            s = sigmoid(gate)
            silu = gate * s
            unit = out * silu * inverse
            dg = dgated[rows, span]
            gain = par[6:7, span]
            gated[rows, span] = (unit * gain).astype(BF16)
            small[5:6, span] += jnp.sum(dg * unit, axis=0, keepdims=True)
            d_product = (dg * gain - unit * mean) * inverse
            d_out = d_product * silu
            dproj[rows, span] = (d_product * out * (s * (1.0 + gate * (1.0 - s)))).astype(BF16)
            raw = proj[rows, GW + at : GW + at + 128]
            values = convolve(raw, par, at, 128)
            values = values * sigmoid(values)
            small[6:7, span] += jnp.sum(d_out * values, axis=0, keepdims=True)
            values_low = values.astype(BF16)
            d_low = d_out.astype(BF16)
            parts = []
            for i, h in enumerate((2 * p, 2 * p + 1)):
                decays = jnp.exp(jnp.where(later_ok, total_t[h : h + 1, :] - total[:, h : h + 1], -1e30))
                size = step[:, h : h + 1]
                own = jnp.where(left if i == 0 else right, d_out, 0.0).astype(BF16)
                d_mix = decays * dot_nt(values_low, own)
                d_scores = d_scores + d_mix * size
                per_step = (d_mix * scores_t).astype(BF16)
                tail = dot(per_step, suffix)
                direct = jnp.where(col == h, tail[:, 0:1], direct)
                lines.append(jnp.sum(jnp.where(before, tail * size, 0.0), axis=0, keepdims=True))
                mix = (decays * scores_t * size).astype(BF16)
                parts.append(dot(mix, d_low))
            d_values = jnp.where(left, parts[0], parts[1]) + skip[0:1, span] * d_out
            dproj[rows, GW + at : GW + at + 128] = conv_back(d_values, raw, at, 128).astype(BF16)
        lines = jnp.concatenate(lines + [jnp.zeros((SEQ - OWN, SEQ), F32)], axis=0)
        d_decay = lines.T
        d_step = direct + head[1:2, :] * d_decay
        d_raw = d_step * sigmoid(raw_step + head[0:1, :])
        small[7:8, 0:128] += jnp.sum(d_raw, axis=0, keepdims=True)
        small[7:8, 128:256] += jnp.sum(d_decay * decay, axis=0, keepdims=True)
        d_low = d_scores.astype(BF16)
        d_write = dot(d_low, read.astype(BF16))
        d_read = dot_tn(d_low, write.astype(BF16))
        d_wr = jnp.concatenate([d_write, d_read], axis=1)
        dproj[rows, 2 * GW : 2 * GW + 256] = conv_back(d_wr, raw_wr, GW, 256).astype(BF16)
        dproj[rows, 2 * GW + 256 : COLS] = d_raw.astype(BF16)
        return carry

    lax.fori_loop(0, GROUP, one, 0)


def backward_kernel(
    w, grads, head, skip, proj, lowered, heads_out, dgated, ow, par, sums, branch, d_low, dw, dow, small, gated, dproj
):
    backward_mix(proj, par, head, skip, heads_out, dgated, sums, gated, dproj, small)

    def by_rows(i, carry):
        rows = pl.ds(i * 256, 256)
        branch[rows, :] = dot(gated[rows, :], ow[...]).astype(BF16)
        d_low[rows, :] = dot_nt(dproj[rows, :], w[...]).astype(BF16)
        return carry

    lax.fori_loop(0, ROWS // 256, by_rows, 0)
    for i in range(D // 384):
        span = slice(i * 384, (i + 1) * 384)
        dw[span, :] = dot_tn(lowered[:, span], dproj[...]).astype(BF16)
    out = dot_tn(gated[...], grads[...])
    for j in range(16):
        block = out[j * KOUT : (j + 1) * KOUT]
        tail = jnp.concatenate([block[16:24, 0 : D // 2], block[16:24, D // 2 :]], axis=0)
        fold = jnp.concatenate([block[0:16], tail], axis=1).astype(BF16)
        for half in range(2):
            dow[j % 8, j // 8, half] = fold[:, half * (FOLD // 2) : (half + 1) * (FOLD // 2)]


def backward(w, grads, head, skip, proj, lowered, heads_out, dgated, ow, par, sums):
    vmem = pl.BlockSpec(memory_space=pltpu.VMEM)
    shape = jax.ShapeDtypeStruct
    return pl.pallas_call(
        backward_kernel,
        name="backward",
        out_shape=(
            shape((ROWS, D), BF16),
            shape((ROWS, D), BF16),
            shape((D, COLS), BF16),
            shape((GROUP, 2, 2, 16, FOLD // 2), BF16),
            shape((8, CW), F32),
        ),
        in_specs=[vmem] * 11,
        out_specs=(vmem,) * 5,
        scratch_shapes=[pltpu.VMEM((ROWS, GW), BF16), pltpu.VMEM((ROWS, COLS), BF16)],
        compiler_params=pltpu.CompilerParams(vmem_limit_bytes=VMEM_LIMIT),
    )(w, grads, head, skip, proj, lowered, heads_out, dgated, ow, par, sums)


class PlaneReduce:
    def __init__(self, terms, got, mid, last, out, send, recv):
        self.terms, self.got, self.mid, self.last, self.out = terms, got, mid, last, out
        self.send, self.recv = send, recv
        self.z, self.x, _, _ = place()

    def line(self, half, k):
        return self.terms.at[:, (self.x + k) % 4, 0] if half == 0 else self.terms.at[(self.z + k) % 4, :, 1]

    def first(self, half, k):
        target = on_x(k) if half == 0 else on_z(k)
        return remote(self.line(half, k), self.got.at[half, k - 1], self.send.at[half, 0, k], self.recv.at[half, 0, k], target)

    def second(self, half, k):
        target = on_z(k) if half == 0 else on_x(k)
        return remote(self.mid.at[half, k - 1], self.last.at[half, k - 1], self.send.at[half, 1, k], self.recv.at[half, 1, k], target)

    def start(self):
        for k in (2, 1, 3):
            for half in range(2):
                self.first(half, k).start()

    def middle(self):
        for half in range(2):
            for k in (1, 2, 3):
                self.first(half, k).wait_recv()
            for k in (2, 1, 3, 0):
                if half == 0:
                    at = (self.z + k) % 4
                    total = self.terms[at, self.x, 0].astype(F32)
                else:
                    at = (self.x + k) % 4
                    total = self.terms[self.z, at, 1].astype(F32)
                for j in range(3):
                    total = total + self.got[half, j, at].astype(F32)
                if k:
                    self.mid[half, k - 1] = total.astype(BF16)
                    self.second(half, k).start()
                else:
                    self.out[half] = total

    def end(self):
        for half in range(2):
            for k in (1, 2, 3):
                self.second(half, k).wait_recv()
            total = self.out[half]
            for j in range(3):
                total = total + self.last[half, j].astype(F32)
            self.out[half] = total

    def finish(self):
        for half in range(2):
            for k in (1, 2, 3):
                self.first(half, k).wait_send()
                self.second(half, k).wait_send()


class GroupReduce:
    def __init__(self, terms, got, mid, last, out, send, recv):
        self.terms, self.got, self.mid, self.last, self.out = terms, got, mid, last, out
        self.send, self.recv = send, recv
        _, _, self.y, self.c = place()

    def across(self, k):
        src = self.terms.at[(self.y + k) % 4, 1 - self.c]
        return remote(src, self.got.at[k], self.send.at[0, k], self.recv.at[0, k], sibling())

    def along(self, k):
        return remote(self.mid.at[k - 1], self.last.at[k - 1], self.send.at[1, k], self.recv.at[1, k], on_y(k))

    def start(self):
        for k in (2, 1, 3, 0):
            self.across(k).start()

    def middle(self):
        for k in (2, 1, 3, 0):
            self.across(k).wait_recv()
            total = self.terms[(self.y + k) % 4, self.c].astype(F32) + self.got[k].astype(F32)
            if k:
                self.mid[k - 1] = total.astype(BF16)
                self.along(k).start()
            else:
                self.out[...] = total

    def end(self):
        for k in (1, 2, 3):
            self.along(k).wait_recv()
        total = self.out[...]
        for j in range(3):
            total = total + self.last[j].astype(F32)
        self.out[...] = total

    def finish(self):
        for k in range(4):
            self.across(k).wait_send()
            if k:
                self.along(k).wait_send()


def reduce_kernel(
    branch, d_low, dw, dow, small, branch_out, low_out, rows_out, lines_out, small_out,
    gb, mb, lb, gd, md, ld, gw, mw, lw, fw, tl, gl, ml, ll, cut, zs, xs, part,
    b_sem, b_rsem, d_sem, d_rsem, w_sem, w_rsem, l_sem, l_rsem, o_sem, r_sem, s_sem,
):
    z, x, y, c = place()
    rank = y * 2 + c
    barrier(plane_partners() + group_partners())
    first = GroupReduce(branch, gb, mb, lb, branch_out, b_sem, b_rsem)
    second = GroupReduce(d_low, gd, md, ld, low_out, d_sem, d_rsem)
    weights = PlaneReduce(dw, gw, mw, lw, fw, w_sem, w_rsem)
    lines = PlaneReduce(tl, gl, ml, ll, lines_out, l_sem, l_rsem)

    def to_owner(k):
        target, q = group_partner(k)
        return remote(dow.at[q], tl.at[rank // 2, pl.ds((rank % 2) * 2, 2)], o_sem.at[0, k], o_sem.at[1, k], target)

    def from_member(k):
        _, q = group_partner(k)
        here = tl.at[q // 2, pl.ds((q % 2) * 2, 2)]
        return remote(here, here, o_sem.at[0, k], o_sem.at[1, GROUP - k], sibling())

    def small_z(k):
        return remote(small, zs.at[z], s_sem.at[0, k], s_sem.at[1, k], on_z(k))

    def small_x(k):
        return remote(part, xs.at[x], s_sem.at[2, k], s_sem.at[3, k], on_x(k))

    def small_group(k):
        return remote(small_out.at[rank], small_out.at[rank], s_sem.at[4, k], s_sem.at[5, k], group_partner(k)[0])

    weights.start()
    first.start()
    second.start()
    for k in (1, 2, 3):
        small_z(k).start()
    for k in range(1, GROUP):
        to_owner(k).start()
    tl[rank // 2, pl.ds((rank % 2) * 2, 2)] = dow[rank]
    zs[z] = small[...]
    first.middle()
    second.middle()
    for k in (1, 2, 3):
        small_z(k).wait_recv()
    part[...] = ((zs[0] + zs[1]) + zs[2]) + zs[3]
    xs[x] = part[...]
    for k in (1, 2, 3):
        small_x(k).start()
    weights.middle()
    for k in range(1, GROUP):
        from_member(k).wait_recv()
    lines.start()
    for k in (1, 2, 3):
        small_x(k).wait_recv()
    small_out[rank] = ((xs[0] + xs[1]) + xs[2]) + xs[3]
    for k in range(1, GROUP):
        small_group(k).start()
    weights.end()

    def rows_to(k):
        target, q = group_partner(k)
        return remote(cut.at[q], rows_out.at[rank], r_sem.at[0, k], r_sem.at[1, k], target)

    for q in range(GROUP):
        cut[q] = jnp.zeros((16, COLS), BF16)
        cut[q, 0:KIN, :] = fw[q // 4, q % 4 * KIN : (q % 4 + 1) * KIN, :].astype(BF16)
    for k in range(1, GROUP):
        rows_to(k).start()
    rows_out[rank] = cut[rank]
    lines.middle()
    first.end()
    second.end()
    lines.end()
    for k in range(1, GROUP):
        rows_to(k).wait_recv()
        small_group(k).wait_recv()
    first.finish()
    second.finish()
    weights.finish()
    lines.finish()
    for k in range(1, GROUP):
        to_owner(k).wait_send()
        rows_to(k).wait_send()
        small_group(k).wait_send()
    for k in (1, 2, 3):
        small_z(k).wait_send()
        small_x(k).wait_send()


def reduce_all(branch, d_low, dw, dow, small):
    vmem, vm = pl.BlockSpec(memory_space=pltpu.VMEM), pltpu.VMEM
    dma = pltpu.SemaphoreType.DMA
    shape = jax.ShapeDtypeStruct
    wide = FOLD // 2
    return pl.pallas_call(
        reduce_kernel,
        name="reduce",
        out_shape=(
            shape((SEQ, D), F32),
            shape((SEQ, D), F32),
            shape((GROUP, 16, COLS), BF16),
            shape((2, 16, wide), F32),
            shape((GROUP, 8, CW), F32),
        ),
        in_specs=[vmem] * 5,
        out_specs=(vmem,) * 5,
        scratch_shapes=[
            vm((4, SEQ, D), BF16), vm((3, SEQ, D), BF16), vm((3, SEQ, D), BF16),
            vm((4, SEQ, D), BF16), vm((3, SEQ, D), BF16), vm((3, SEQ, D), BF16),
            vm((2, 3, 4, 48, COLS), BF16), vm((2, 3, 48, COLS), BF16), vm((2, 3, 48, COLS), BF16), vm((2, 48, COLS), F32),
            vm((4, 4, 2, 16, wide), BF16),
            vm((2, 3, 4, 16, wide), BF16), vm((2, 3, 16, wide), BF16), vm((2, 3, 16, wide), BF16),
            vm((GROUP, 16, COLS), BF16),
            vm((4, 8, CW), F32), vm((4, 8, CW), F32), vm((8, CW), F32),
            dma((2, 4)), dma((2, 4)), dma((2, 4)), dma((2, 4)),
            dma((2, 2, 4)), dma((2, 2, 4)), dma((2, 2, 4)), dma((2, 2, 4)),
            dma((2, GROUP)), dma((2, GROUP)), dma((6, GROUP)),
        ],
        compiler_params=pltpu.CompilerParams(collective_id=2, has_side_effects=True, vmem_limit_bytes=VMEM_LIMIT),
    )(branch, d_low, dw, dow, small)


def finish_kernel(
    hid, grd, live, inw, gain_own, par, branch, d_low, rows, lines, small,
    mixed, in_grad, dinw, dgain, dconv, dheads, dinner, doutw,
):
    alive = live[...]
    h = hid[...].astype(F32)
    mixed[...] = (h + alive * branch[...]).astype(BF16)
    scale = lax.rsqrt(jnp.mean(h * h, axis=1, keepdims=True) + EPSILON)
    normed = h * scale
    d_normed = d_low[...] * par[0:1, :]
    through = scale * (d_normed - normed * jnp.mean(d_normed * normed, axis=1, keepdims=True))
    in_grad[...] = (grd[...].astype(F32) + through).astype(BF16)
    shared = jnp.zeros((KIN, 256), F32)
    total = jnp.zeros((KIN, 1), F32)
    for q in range(GROUP):
        block = rows[q].astype(F32)[0:KIN]
        for at, span in ((q * GW, block[:, 0:GW]), (INNER + q * GW, block[:, GW : 2 * GW])):
            dinw[:, at : at + GW] = span
        at = 2 * INNER + 256 + q * OWN
        dinw[:, at : at + OWN] = block[:, 2 * GW + 256 : 2 * GW + 256 + OWN]
        shared = shared + block[:, 2 * GW : 2 * GW + 256]
    dinw[:, 2 * INNER : 2 * INNER + 256] = shared
    total = jnp.sum(dinw[...] * inw[...].astype(F32), axis=1, keepdims=True)
    dgain[...] = total / gain_own[...].astype(F32)
    me = lax.axis_index("fsdp")
    conv = jnp.zeros((32, 8), F32)
    inner = jnp.zeros((32, 8), F32)
    common = jnp.zeros((8, 256), F32)
    line = iota((32, GW), 0)
    heads = ones(iota((GW, 128), 0) // 64 == iota((GW, 128), 1), F32)
    dheads[...] = jnp.zeros_like(dheads)
    for q in range(GROUP):
        part = small[q, :, 0:GW]
        lane = iota((32, GW), 1) + q * GW
        conv = conv + dot_nt(ones(lane == line + 26 * me, F32), part, HIGHEST)
        inner = inner + dot_nt(ones(lane == line + KOUT * me, F32), part, HIGHEST)
        common = common + small[q, :, GW:CW]
        span = slice(q * OWN, (q + 1) * OWN)
        dheads[0:1, span] = small[q, 7:8, 0:OWN]
        dheads[1:2, span] = small[q, 7:8, 128 : 128 + OWN]
        dheads[2:3, span] = dot(part, heads, HIGHEST)[6:7, 0:OWN]
    lane = iota((32, 256), 1) + INNER
    conv = conv + dot_nt(ones(lane == iota((32, 256), 0) + 26 * me, F32), common, HIGHEST)
    dconv[...] = conv
    dinner[...] = inner
    wide = FOLD // 2
    first, second = lines[0], lines[1]
    doutw[0:16, 0:wide] = first
    doutw[0:16, wide:D] = second[:, 0 : D - wide]
    tail = second[:, D - wide :]
    doutw[16:24, 0 : D // 2] = tail[0:8]
    doutw[16:24, D // 2 : D] = tail[8:16]


def finish(*given):
    vmem = pl.BlockSpec(memory_space=pltpu.VMEM)
    shape = jax.ShapeDtypeStruct
    return pl.pallas_call(
        finish_kernel,
        name="finish",
        out_shape=(
            shape((SEQ, D), BF16),
            shape((SEQ, D), BF16),
            shape((KIN, 2 * INNER + 256 + HEADS), F32),
            shape((KIN, 1), F32),
            shape((32, 8), F32),
            shape((8, HEADS), F32),
            shape((32, 8), F32),
            shape((KOUT, D), F32),
        ),
        in_specs=[vmem] * len(given),
        out_specs=(vmem,) * 8,
        compiler_params=pltpu.CompilerParams(vmem_limit_bytes=VMEM_LIMIT),
    )(*given)


def body(
    hidden, in_weight, norm_gain, conv_weight, conv_bias, dt_bias, a_log, skip, inner_gain, out_weight, out_grad,
    seq_lengths, seq_owner,
):
    me = lax.axis_index("fsdp")
    rank = me % GROUP
    length = jnp.sum(jnp.where(seq_owner == me, seq_lengths, 0))
    live = jnp.arange(SEQ)[:, None] < length
    grads = jnp.where(live, out_grad, jnp.zeros_like(out_grad))
    params = jnp.concatenate([norm_gain, conv_weight.T.reshape(-1), conv_bias, inner_gain, jnp.zeros((GW - 166,), BF16)])
    extra = jnp.pad(jnp.tile(params, 8)[None, :], ((0, 3), (0, in_weight.shape[1] - INNER)))
    inw = jnp.concatenate([in_weight, extra], axis=0)
    tail = jnp.concatenate([out_weight[16:, : D // 2], out_weight[16:, D // 2 :]], axis=0)
    fold = jnp.concatenate([out_weight[:16], tail], axis=1)
    outl = jnp.stack([fold[:, : FOLD // 2], fold[:, FOLD // 2 :]])
    mine = lax.dynamic_slice(jnp.stack([dt_bias, -jnp.exp(a_log), skip]), (0, rank * OWN), (3, OWN))
    head = jnp.pad(mine, ((0, 5), (0, 128 - OWN)))
    skip_wide = jnp.broadcast_to(jnp.repeat(mine[2], 64)[None, :], (8, GW))
    w, praw, oraw, hid, grd = gather(inw, outl, hidden, grads)
    w = w.reshape(D, COLS)
    hid, grd = hid.reshape(ROWS, D), grd.reshape(ROWS, D)
    proj, lowered, heads_out, dgated, ow, par, sums = forward(hid, w, praw.reshape(256, 256), oraw, grd, head, skip_wide)
    sums = group_sums(sums)
    branch, d_low, dw, dow, small = backward(w, grd, head, skip_wide, proj, lowered, heads_out, dgated, ow, par, sums)
    branch, d_low, rows, lines, small = reduce_all(
        branch.reshape(4, 2, SEQ, D), d_low.reshape(4, 2, SEQ, D), dw.reshape(4, 4, 2, 48, COLS), dow, small
    )
    mixed, in_grad, dinw, dgain, dconv, dheads, dinner, doutw = finish(
        hidden, out_grad, live.astype(F32), in_weight, norm_gain[:, None], par, branch, d_low, rows, lines, small
    )
    return (
        mixed,
        in_grad,
        dinw,
        dgain[:, 0],
        dconv[:26, :4],
        dconv[:26, 4],
        dheads[0],
        dheads[1],
        dheads[2],
        dinner[:KOUT, 5],
        doutw,
    )


def solution(mesh):
    rows, line, whole = P("fsdp", None), P("fsdp"), P()
    return jax.shard_map(
        body,
        mesh=mesh,
        in_specs=(rows, rows, line, rows, line, whole, whole, whole, line, rows, rows, whole, whole),
        out_specs=(rows, rows, rows, line, rows, line, whole, whole, whole, line, rows),
        check_vma=False,
    )
```

time: 1240 us -> 226 us (0.18)
  the two profiles are of different devices: /device:TPU:96 before, /device:TPU:1 now
where the time goes in v1:
time: 226 us; the launch traced here: 225 us
  Pallas kernels  202 us (89%)
  local copies, waits for them, and re-layouts  12 us (5%)
  other arithmetic  10.8 us (5%)
    pallas_call x1, Pallas kernels, gather(): pl.pallas_call(gather_kernel, name='gather', out_shape=(jax.ShapeDtypeStr...  68.1 us
    pallas_call x1, Pallas kernels, reduce_all(): pl.pallas_call(reduce_kernel, name='reduce', out_shape=(shape((SEQ, D), F...  64.7 us
    pallas_call x1, Pallas kernels, backward(): pl.pallas_call(backward_kernel, name='backward', out_shape=(shape((ROWS,...  32 us
    pallas_call x1, Pallas kernels, forward(): pl.pallas_call(forward_kernel, name='forward', out_shape=(shape((ROWS, CO...  25.9 us
    pallas_call x1, Pallas kernels, group_sums(): pl.pallas_call(sums_kernel, name='group_sums', out_shape=jax.ShapeDtypeSt...  6.51 us
    pallas_call x1, Pallas kernels, finish(): pl.pallas_call(finish_kernel, name='finish', out_shape=(shape((SEQ, D), B...  4.64 us

profile of v1, /device:TPU:1, one launch (start us, length us, event | category | flops | bytes accessed | tf_op | source)
XLA Modules:
  0.0 225.4 jit_solution(16011895870828307865)
XLA Ops:
  0.7 0.7 negate_bitcast_fusion
  1.3 0.7 pad_maximum_fusion.3
  2.0 0.1 constant_dynamic-slice_fusion
  2.1 0.1 broadcast_in_dim.37
  2.2 0.1 broadcast_in_dim.38
  2.2 0.6 broadcast_in_dim.39.skip
  2.8 0.6 pad.9.head
  3.4 0.7 fusion.5
  4.2 0.8 slice.38
  5.0 0.8 fusion.3
  5.7 0.6 pad_maximum_fusion.outl
  6.4 1.3 fusion.4
  7.7 0.6 iota_compare_fusion.2
  8.4 1.8 broadcast_select_fusion.grd
  10.2 0.8 reshape.61
  11.0 2.1 concatenate.12
  13.1 1.7 fusion.1.inw
  14.7 68.1 %gather.1 = (bf16[4,4,2,48,1152]{4,3,2,1,0:T(8,128)(2,1)}, bf16[4,4,1,16,256]{4,3,2,1,0:T(8,128)(2,1)}, bf16[8,2,2,16,1152]{4,3,2,1,0:T(8,128)(2,1)}, bf16[4,2,1...) custom-call(bf16[16,6448]{1,0:T(8,128)(2,1)} %fusion.1.inw, bf16[2,16,1152]{2,1,0:T(8,128)(2,1)} %pad_maximum_fusion.outl, ...), custom_call_target="tpu_custom_call" | custom-call | tf_op jit(solution)/shard_map/gather/pallas_call | solution.py:314
  82.8 25.9 %forward.1 = (f32[1024,1152]{1,0:T(8,128)}, bf16[1024,1536]{1,0:T(8,128)(2,1)}, f32[1024,384]{1,0:T(8,128)}, f32[1024,384]{1,0:T(8,128)}, bf16[384,1536]{1,0:T(8...) custom-call(bf16[1024,1536]{1,0:T(8,128)(2,1)} %bitcast.37, bf16[1536,1152]{1,0:T(8,128)(2,1)} %bitcast.30, ...), custom_call_target="tpu_custom_call" | custom-call | tf_op jit(solution)/shard_map/forward/pallas_call | solution.py:467
  108.7 6.5 %group_sums.1.sums = f32[16,128]{1,0:T(8,128)} custom-call(f32[16,128]{1,0:T(8,128)} %get-tuple-element.52.own), custom_call_target="tpu_custom_call" | custom-call | tf_op jit(solution)/shard_map/group_sums/pallas_call | solution.py:505
  115.2 32.0 %backward.1 = (bf16[1024,1536]{1,0:T(8,128)(2,1)}, bf16[1024,1536]{1,0:T(8,128)(2,1)}, bf16[1536,1152]{1,0:T(8,128)(2,1)}, bf16[8,2,2,16,1152]{4,3,2,1,0:T(8,128)(2,1)}, f32[8,640]{1,0:T(8,128)}) custom-call(bf16[1536,1152]{1,0:T(8,128)(2,1)} %bitcast.31, bf16[1024,1536]{1,0:T(8,128)(2,1)} %bitcast.33, f32[8,128]{1,0:T(8,128)} %pad.9.head, ...), custom_call_target="tpu_custom_call" | custom-call | tf_op jit(solution)/shard_map/backward/pallas_call | solution.py:639
  147.3 0.0 copy-start
  147.3 64.7 %reduce.6 = (f32[128,1536]{1,0:T(8,128)}, f32[128,1536]{1,0:T(8,128)}, bf16[8,16,1152]{2,1,0:T(8,128)(2,1)}, f32[2,16,1152]{2,1,0:T(8,128)}, f32[8,8,640]{2,1,0:T(8,128)}) custom-call(bf16[4,2,128,1536]{3,2,1,0:T(8,128)(2,1)} %bitcast.35, bf16[4,2,128,1536]{3,2,1,0:T(8,128)(2,1)} %bitcast.36, bf16[4,4,2,48,1152]{4,3,2,1,0:T(8,128)(2,1)} %bitcast.34, ...), custom_call_target="tpu_custom_call" | custom-call | tf_op jit(solution)/shard_map/reduce/pallas_call | solution.py:849
  211.9 1.3 fusion.2.live
  213.2 0.0 copy-done
  213.2 0.7 copy.26.gain_own
  213.9 4.6 %finish.1 = (bf16[128,1536]{1,0:T(8,128)(2,1)}, bf16[128,1536]{1,0:T(8,128)(2,1)}, f32[12,6448]{1,0:T(8,128)}, f32[12,1]{1,0:T(8,128)}, f32[32,8]{1,0:T(8,128)},...) custom-call(bf16[128,1536]{1,0:T(8,128)(2,1)} %hid.3, bf16[128,1536]{1,0:T(8,128)(2,1)} %grd.1, ...), custom_call_target="tpu_custom_call" | custom-call | tf_op jit(solution)/shard_map/finish/pallas_call | solution.py:934
  218.5 1.4 copy.27
  219.9 1.3 slice_bitcast_fusion.1
  221.2 1.3 reduce.1
  222.5 1.4 slice_reduce_fusion
  224.0 1.4 slice_reduce_fusion.1
  (4 shorter events, 0.0 us)
Async XLA Ops:
  147.3 66.0 %copy-start = (bf16[12]{0:T(256)(128)(2,1)S(1)}, bf16[12]{0:T(256)(128)(2,1)}, u32[]{:S(2)}) copy-start(bf16[12]{0:T(256)(128)(2,1)} %param.15) | copy-start | bytes 76

commit v2 on v1

v2 whole, which is shorter than its diff:
```python
import functools

import jax
import jax.numpy as jnp
from jax import lax
from jax.experimental import pallas as pl
from jax.experimental.pallas import tpu as pltpu
from jax.sharding import PartitionSpec as P

MESH = pl.DeviceIdType.MESH
F32, BF16 = jnp.float32, jnp.bfloat16
HIGHEST = lax.Precision.HIGHEST
EPSILON = 1e-05

D = 1536
INNER = 3072
CONVD = 3328
HEADS = 48
SEQ = 128
GROUP = 8
ROWS = SEQ * GROUP
GW = INNER // GROUP
OWN = HEADS // GROUP
SH = 384
CW = GW + 256
COLS = 2 * GW + SH
WR, ST, GA = GW, GW + 256, GW + SH
KIN = D // 128
KOUT = INNER // 128
FOLD = D + D // 2
WIDE = FOLD // 2
VMEM_LIMIT = 60 * 2**20


def iota(shape, dim):
    return lax.broadcasted_iota(jnp.int32, shape, dim)


def ones(condition, kind=BF16):
    return jnp.where(condition, 1.0, 0.0).astype(kind)


def dot(a, b, precision=None):
    return lax.dot_general(a, b, (((1,), (0,)), ((), ())), precision=precision, preferred_element_type=F32)


def dot_nt(a, b, precision=None):
    return lax.dot_general(a, b, (((1,), (1,)), ((), ())), precision=precision, preferred_element_type=F32)


def dot_tn(a, b, precision=None):
    return lax.dot_general(a, b, (((0,), (0,)), ((), ())), precision=precision, preferred_element_type=F32)


def sigmoid(v):
    return 1.0 / (1.0 + jnp.exp(-v))


def softplus(v):
    return jnp.maximum(v, 0.0) + jnp.log1p(jnp.exp(-jnp.abs(v)))


def later(v, k):
    if k == 0:
        return v
    return jnp.where(iota(v.shape, 0) >= k, pltpu.roll(v, k, 0), 0.0)


def earlier(v, k):
    if k == 0:
        return v
    return jnp.where(iota(v.shape, 0) < v.shape[0] - k, pltpu.roll(v, v.shape[0] - k, 0), 0.0)


def place():
    me = lax.axis_index("fsdp")
    return me // 32, (me // 8) % 4, (me // 2) % 4, me % 2


def index(z, x, y, c):
    return ((z * 4 + x) * 4 + y) * 2 + c


def group_partner(k):
    z, x, y, c = place()
    rank = (y * 2 + c + k) % GROUP
    return index(z, x, rank // 2, rank % 2), rank


def on_z(k):
    z, x, y, c = place()
    return index((z + k) % 4, x, y, c)


def on_x(k):
    z, x, y, c = place()
    return index(z, (x + k) % 4, y, c)


def on_y(k):
    z, x, y, c = place()
    return index(z, x, (y + k) % 4, c)


def sibling():
    z, x, y, c = place()
    return index(z, x, y, 1 - c)


def barrier(partners):
    sem = pltpu.get_barrier_semaphore()
    for p in partners:
        pl.semaphore_signal(sem, inc=1, device_id=(p,), device_id_type=MESH)
    pl.semaphore_wait(sem, len(partners))


def remote(src, dst, send, recv, target):
    return pltpu.make_async_remote_copy(
        src_ref=src, dst_ref=dst, send_sem=send, recv_sem=recv, device_id=(target,), device_id_type=MESH
    )


def plane_partners():
    return [on_z(k) for k in (1, 2, 3)] + [on_x(k) for k in (1, 2, 3)]


def group_partners():
    return [group_partner(k)[0] for k in range(1, GROUP)]


class PlaneGather:
    def __init__(self, buf, own, send, recv, halves):
        self.buf, self.own, self.send, self.recv, self.halves = buf, own, send, recv, halves
        self.z, self.x, _, _ = place()

    def slot(self, half, first, second):
        a, b = (first, second) if half == 0 else (second, first)
        return self.buf.at[(self.z + a) % 4, (self.x + b) % 4, half]

    def along(self, half, stage, k):
        return on_z(k) if (half == 0) == (stage == 0) else on_x(k)

    def copy(self, half, first, stage, k):
        src = self.own(half) if first == 0 else self.slot(half, first, 0)
        at = (4 - k, 0) if stage == 0 else (first, 4 - k)
        return remote(
            src,
            self.slot(half, first, 0),
            self.send.at[half, first if stage else 4, k],
            self.recv.at[half, at[0], at[1]],
            self.along(half, stage, k),
        )

    def arrival(self, half, first, second):
        here = self.slot(half, first, second)
        return remote(here, here, self.send.at[half, 4, 0], self.recv.at[half, first, second], on_z(1))

    def start(self):
        for k in (1, 3, 2):
            for half in range(self.halves):
                self.copy(half, 0, 0, k).start()
        for k in (1, 3, 2):
            for half in range(self.halves):
                self.copy(half, 0, 1, k).start()

    def forward(self):
        for first in (1, 3, 2):
            for half in range(self.halves):
                self.arrival(half, first, 0).wait_recv()
                for k in (1, 3, 2):
                    self.copy(half, first, 1, k).start()

    def finish(self):
        for first in range(4):
            for second in (1, 3, 2):
                for half in range(self.halves):
                    self.arrival(half, first, second).wait_recv()

    def sent(self):
        for half in range(self.halves):
            for k in (1, 2, 3):
                self.copy(half, 0, 0, k).wait_send()
                for first in range(4):
                    self.copy(half, first, 1, k).wait_send()


class GroupGather:
    def __init__(self, buf, own, send, recv):
        self.buf, self.own, self.send, self.recv = buf, own, send, recv
        _, _, self.y, self.c = place()

    def along(self, k):
        return remote(self.own, self.buf.at[self.y, self.c], self.send.at[0, k], self.recv.at[0, 4 - k], on_y(k))

    def across(self, k):
        src = self.own if k == 0 else self.buf.at[(self.y + k) % 4, self.c]
        dst = self.buf.at[(self.y + k) % 4, self.c]
        return remote(src, dst, self.send.at[1, k], self.recv.at[1, k], sibling())

    def arrival(self, hop, k):
        here = self.buf.at[(self.y + k) % 4, self.c if hop == 0 else 1 - self.c]
        return remote(here, here, self.send.at[hop, k], self.recv.at[hop, k], sibling())

    def start(self):
        for k in (1, 3, 2):
            self.along(k).start()
        self.across(0).start()

    def forward(self):
        for k in (1, 3, 2):
            self.arrival(0, k).wait_recv()
            self.across(k).start()

    def finish(self):
        for k in range(4):
            self.arrival(1, k).wait_recv()

    def sent(self):
        for k in range(4):
            self.across(k).wait_send()
            if k:
                self.along(k).wait_send()


def unpack_params(raw, rank, par):
    row = iota((512, 1), 0)
    device = (row // 4).astype(F32)
    tap = row % 4
    values = raw[...].reshape(512, 256)

    def spots(span, first, count, channel):
        owner = jnp.floor((channel + 0.5) * (1.0 / count))
        lane = channel - owner * count + first
        pick = ones(iota((128, channel.shape[1]), 0).astype(F32) == lane)
        return jnp.where(device == owner, dot(values[:, span], pick), 0.0)

    def only(k, at):
        return jnp.sum(jnp.where(tap == k, at, 0.0), axis=0, keepdims=True)

    def lanes(n):
        return iota((1, n), 1).astype(F32)

    start = rank.astype(F32) * GW
    conv = lanes(CW)
    conv = jnp.where(conv < GW, conv + start, conv - GW + INNER)
    low, high = slice(0, 128), slice(128, 256)
    par[...] = jnp.zeros_like(par)
    par[0:1, :] = only(0, spots(high, 0, KIN, lanes(D)))
    taps = spots(low, 0, 26, conv)
    for k in range(4):
        par[k + 1 : k + 2, 0:CW] = only(k, taps)
    par[5:6, 0:CW] = only(0, spots(high, KIN, 26, conv))
    par[6:7, 0:GW] = only(0, spots(high, KIN + 26, KOUT, lanes(GW) + start))


def own_heads(raw, rank, head, skip):
    row = iota((128, 128), 0)
    col = iota((128, 128), 1)
    given = raw[...]
    mine = dot(given, ones(jnp.logical_and(row == col + OWN * rank, col < OWN), F32), HIGHEST)
    head[...] = jnp.where(iota((8, 128), 0) == 1, -jnp.exp(mine), mine)
    wide = iota((128, GW), 0) == iota((128, GW), 1) // 64 + OWN * rank
    skip[...] = dot(given, ones(wide, F32), HIGHEST)[2:3]


def unfold_out_weight(raw, ow):
    row, col = iota((GW, 256), 0), iota((GW, 256), 1)
    device, line = row // KOUT, row % KOUT
    base = (device % 8) * 32 + (device // 8) * 16
    top = ones(jnp.logical_and(line < 16, col == base + line))
    low_left = ones(jnp.logical_and(line >= 16, col == base + line - 16))
    low_right = ones(jnp.logical_and(line >= 16, col == base + line - 8))
    first = raw[:, :, 0].reshape(256, WIDE)
    second = raw[:, :, 1].reshape(256, WIDE)
    half, split = D // 2, WIDE - D // 2
    left, right_a = first[:, 0:half], first[:, half:]
    right_b, tail = second[:, 0 : half - split], second[:, half - split :]
    ow[:, 0:half] = (dot(top, left) + dot(low_left, tail)).astype(BF16)
    ow[:, half : half + split] = (dot(top, right_a) + dot(low_right, tail[:, 0:split])).astype(BF16)
    ow[:, half + split :] = (dot(top, right_b) + dot(low_right, tail[:, split:])).astype(BF16)


def convolve(raw, par, at, width):
    out = par[5:6, at : at + width] + raw * par[4:5, at : at + width]
    for k in range(3):
        out = out + later(raw, 3 - k) * par[k + 1 : k + 2, at : at + width]
    return out


def steps_of(raw, head):
    step = softplus(raw + head[0:1, :])
    decay = head[1:2, :] * step
    lower = ones(iota((SEQ, SEQ), 0) >= iota((SEQ, SEQ), 1), F32)
    total = dot(lower, decay, HIGHEST)
    return step, decay, total


def mix_forward(b, proj, par, head, skip, heads_out):
    row, col = iota((SEQ, SEQ), 0), iota((SEQ, SEQ), 1)
    causal = row >= col
    rows = pl.ds(pl.multiple_of(b * SEQ, SEQ), SEQ)
    wr = convolve(proj[rows, WR:ST], par, GW, 256)
    wr = wr * sigmoid(wr)
    write, read = wr[:, 0:128], wr[:, 128:256]
    step, _, total = steps_of(proj[rows, ST:GA], head)
    total_t, step_t = total.T, step.T
    scores = dot_nt(read, write, HIGHEST)
    for p in range(3):
        at = p * 128
        values = convolve(proj[rows, at : at + 128], par, at, 128)
        values = values * sigmoid(values)
        values_low = values.astype(BF16)
        parts = []
        for h in (2 * p, 2 * p + 1):
            decays = jnp.exp(jnp.where(causal, total[:, h : h + 1] - total_t[h : h + 1, :], -1e30))
            mix = (decays * scores * step_t[h : h + 1, :]).astype(BF16)
            parts.append(dot(mix, values_low))
        heads_out[rows, at : at + 128] = jnp.where(col < 64, parts[0], parts[1]) + skip[0:1, at : at + 128] * values


def norm_sums(b, proj, par, heads_out, dgated, acc):
    rows = pl.ds(pl.multiple_of(b * SEQ, SEQ), SEQ)
    gate = proj[rows, GA:COLS]
    product = heads_out[rows, :] * gate * sigmoid(gate)
    squares = jnp.sum(product * product, axis=1, keepdims=True)
    crosses = jnp.sum(product * dgated[rows, :] * par[6:7, 0:GW], axis=1, keepdims=True)
    col = iota((SEQ, SEQ), 1)
    return jnp.where(col == b, squares, jnp.where(col == b + 8, crosses, acc))


def norm_back(b, proj, par, wide, heads_out, dgated, gated, dproj, small):
    rows = pl.ds(pl.multiple_of(b * SEQ, SEQ), SEQ)
    col = iota((SEQ, SEQ), 1)
    square = jnp.sum(jnp.where(col == b, wide[...], 0.0), axis=1, keepdims=True)
    cross = jnp.sum(jnp.where(col == b + 8, wide[...], 0.0), axis=1, keepdims=True)
    inverse = lax.rsqrt(square * (1.0 / INNER) + EPSILON)
    mean = cross * inverse * (1.0 / INNER)
    out = heads_out[rows, :]
    gate = proj[rows, GA:COLS]
    s = sigmoid(gate)
    silu = gate * s
    unit = out * silu * inverse
    dg = dgated[rows, :]
    gain = par[6:7, 0:GW]
    gated[rows, :] = (unit * gain).astype(BF16)
    small[5:6, 0:GW] += jnp.sum(dg * unit, axis=0, keepdims=True)
    d_product = (dg * gain - unit * mean) * inverse
    dproj[rows, GA:COLS] = (d_product * out * (s * (1.0 + gate * (1.0 - s)))).astype(BF16)
    dgated[rows, :] = d_product * silu


def mix_back(b, proj, par, head, skip, d_heads, dproj, small):
    row, col = iota((SEQ, SEQ), 0), iota((SEQ, SEQ), 1)
    later_ok = col >= row
    left, right = col < 64, col >= 64
    suffix = ones(row >= col)
    before = row < col
    rows = pl.ds(pl.multiple_of(b * SEQ, SEQ), SEQ)

    def conv_back(d_act, raw, v, s, at, width):
        d_conv = d_act * s * (1.0 + v * (1.0 - s))
        span = slice(at, at + width)
        back = d_conv * par[4:5, span]
        small[3:4, span] += jnp.sum(d_conv * raw, axis=0, keepdims=True)
        for k in range(3):
            back = back + earlier(d_conv, 3 - k) * par[k + 1 : k + 2, span]
            small[k : k + 1, span] += jnp.sum(d_conv * later(raw, 3 - k), axis=0, keepdims=True)
        small[4:5, span] += jnp.sum(d_conv, axis=0, keepdims=True)
        return back

    raw_wr = proj[rows, WR:ST]
    pre_wr = convolve(raw_wr, par, GW, 256)
    sig_wr = sigmoid(pre_wr)
    wr = pre_wr * sig_wr
    write, read = wr[:, 0:128], wr[:, 128:256]
    raw_step = proj[rows, ST:GA]
    step, decay, total = steps_of(raw_step, head)
    total_t = total.T
    scores_t = dot_nt(write, read, HIGHEST)
    d_scores = jnp.zeros((SEQ, SEQ), F32)
    direct = jnp.zeros((SEQ, SEQ), F32)
    lines = []
    for p in range(3):
        at = p * 128
        span = slice(at, at + 128)
        d_out = d_heads[rows, span]
        raw = proj[rows, span]
        pre = convolve(raw, par, at, 128)
        sig = sigmoid(pre)
        values = pre * sig
        small[6:7, span] += jnp.sum(d_out * values, axis=0, keepdims=True)
        values_low = values.astype(BF16)
        d_low = d_out.astype(BF16)
        parts = []
        for i, h in enumerate((2 * p, 2 * p + 1)):
            decays = jnp.exp(jnp.where(later_ok, total_t[h : h + 1, :] - total[:, h : h + 1], -1e30))
            size = step[:, h : h + 1]
            own = jnp.where(left if i == 0 else right, d_out, 0.0).astype(BF16)
            d_mix = decays * dot_nt(values_low, own)
            d_scores = d_scores + d_mix * size
            per_step = (d_mix * scores_t).astype(BF16)
            tail = dot(per_step, suffix)
            direct = jnp.where(col == h, tail[:, 0:1], direct)
            lines.append(jnp.sum(jnp.where(before, tail * size, 0.0), axis=0, keepdims=True))
            mix = (decays * scores_t * size).astype(BF16)
            parts.append(dot(mix, d_low))
        d_values = jnp.where(left, parts[0], parts[1]) + skip[0:1, span] * d_out
        dproj[rows, span] = conv_back(d_values, raw, pre, sig, at, 128).astype(BF16)
    d_decay = jnp.concatenate(lines + [jnp.zeros((SEQ - OWN, SEQ), F32)], axis=0).T
    d_step = direct + head[1:2, :] * d_decay
    d_raw = d_step * sigmoid(raw_step + head[0:1, :])
    small[7:8, 0:128] += jnp.sum(d_raw, axis=0, keepdims=True)
    small[7:8, 128:256] += jnp.sum(d_decay * decay, axis=0, keepdims=True)
    d_low = d_scores.astype(BF16)
    d_write = dot(d_low, read.astype(BF16))
    d_read = dot_tn(d_low, write.astype(BF16))
    d_wr = jnp.concatenate([d_write, d_read], axis=1)
    dproj[rows, WR:ST] = conv_back(d_wr, raw_wr, pre_wr, sig_wr, GW, 256).astype(BF16)
    dproj[rows, ST:GA] = d_raw.astype(BF16)


class PlaneReduce:
    def __init__(self, terms, got, mid, last, out, send, recv):
        self.terms, self.got, self.mid, self.last, self.out = terms, got, mid, last, out
        self.send, self.recv = send, recv
        self.z, self.x, _, _ = place()

    def line(self, half, k):
        return self.terms.at[:, (self.x + k) % 4, 0] if half == 0 else self.terms.at[(self.z + k) % 4, :, 1]

    def first(self, half, k):
        target = on_x(k) if half == 0 else on_z(k)
        return remote(self.line(half, k), self.got.at[half, k - 1], self.send.at[half, 0, k], self.recv.at[half, 0, k], target)

    def second(self, half, k):
        target = on_z(k) if half == 0 else on_x(k)
        return remote(self.mid.at[half, k - 1], self.last.at[half, k - 1], self.send.at[half, 1, k], self.recv.at[half, 1, k], target)

    def start(self):
        for k in (2, 1, 3):
            for half in range(2):
                self.first(half, k).start()

    def middle(self):
        for half in range(2):
            for k in (1, 2, 3):
                self.first(half, k).wait_recv()
            for k in (2, 1, 3, 0):
                if half == 0:
                    at = (self.z + k) % 4
                    total = self.terms[at, self.x, 0].astype(F32)
                else:
                    at = (self.x + k) % 4
                    total = self.terms[self.z, at, 1].astype(F32)
                for j in range(3):
                    total = total + self.got[half, j, at].astype(F32)
                if k:
                    self.mid[half, k - 1] = total.astype(BF16)
                    self.second(half, k).start()
                else:
                    self.out[half] = total

    def end(self):
        for half in range(2):
            for k in (1, 2, 3):
                self.second(half, k).wait_recv()
            total = self.out[half]
            for j in range(3):
                total = total + self.last[half, j].astype(F32)
            self.out[half] = total

    def finish(self):
        for half in range(2):
            for k in (1, 2, 3):
                self.first(half, k).wait_send()
                self.second(half, k).wait_send()


class GroupReduce:
    def __init__(self, terms, got, mid, last, out, send, recv):
        self.terms, self.got, self.mid, self.last, self.out = terms, got, mid, last, out
        self.send, self.recv = send, recv
        _, _, self.y, self.c = place()

    def across(self, k):
        src = self.terms.at[(self.y + k) % 4, 1 - self.c]
        return remote(src, self.got.at[k], self.send.at[0, k], self.recv.at[0, k], sibling())

    def along(self, k):
        return remote(self.mid.at[k - 1], self.last.at[k - 1], self.send.at[1, k], self.recv.at[1, k], on_y(k))

    def start(self):
        for k in (2, 1, 3, 0):
            self.across(k).start()

    def middle(self):
        for k in (2, 1, 3, 0):
            self.across(k).wait_recv()
            total = self.terms[(self.y + k) % 4, self.c].astype(F32) + self.got[k].astype(F32)
            if k:
                self.mid[k - 1] = total.astype(BF16)
                self.along(k).start()
            else:
                self.out[...] = total

    def end(self):
        for k in (1, 2, 3):
            self.along(k).wait_recv()
        total = self.out[...]
        for j in range(3):
            total = total + self.last[j].astype(F32)
        self.out[...] = total

    def finish(self):
        for k in range(4):
            self.across(k).wait_send()
            if k:
                self.along(k).wait_send()


class Members:
    def __init__(self, src, dst, send, recv):
        self.src, self.dst, self.send, self.recv = src, dst, send, recv
        _, _, y, c = place()
        self.rank = y * 2 + c

    def copy(self, k):
        target, q = group_partner(k)
        return remote(self.src(q), self.dst(self.rank), self.send.at[k], self.recv.at[k], target)

    def arrival(self, k):
        _, q = group_partner(k)
        return remote(self.dst(q), self.dst(q), self.send.at[k], self.recv.at[GROUP - k], sibling())

    def start(self):
        for k in range(1, GROUP):
            self.copy(k).start()

    def finish(self):
        for k in range(1, GROUP):
            self.arrival(k).wait_recv()

    def sent(self):
        for k in range(1, GROUP):
            self.copy(k).wait_send()


def layer_kernel(
    hid, inw, vectors, taps, heads_in, outw, grd, lengths, owners,
    mixed, in_grad, dinw, dgain, dconv, dheads, dinner, doutw,
    split, joined, block, gblock, params, outl, live_grd,
    wx, wg, praw, plane, oraw, hall, gall, low, proj, heads_out, dgated, ow, par, head, skip, sums, slots, wide,
    gated, dproj, d_low, dw, dow, small,
    gb, mb, lb, fb, gd, md, ld, fd, gw, mw, lw, fw, tl, gl, ml, ll, fl, cut, rows_in, zs, xs, part, small_all,
    a_s, a_r, wx_s, wx_r, wg_s, wg_r, p_s, p_r, l_s, l_r, h_s, h_r, g_s, g_r, o_s, o_r, n_s, n_r,
    b_s, b_r, d_s, d_r, rw_s, rw_r, rl_s, rl_r, ro_s, ro_r, rr_s, rr_r, sz_s, sz_r, sx_s, sx_r, sg_s, sg_r, local,
):
    z, x, y, c = place()
    rank = y * 2 + c
    barrier(plane_partners() + group_partners())

    tap_rows = dot_tn(taps[...], ones(iota((26, 128), 0) == iota((26, 128), 1)))
    top = iota((4, 128), 0) == 0
    lines = [tap_rows, jnp.where(top, vectors[...].astype(F32), 0.0), jnp.zeros((4, 128), F32)]

    def padded(span, extra):
        return jnp.concatenate([inw[:, span].astype(F32), extra], axis=0).astype(BF16)

    extra = jnp.concatenate(lines, axis=1)
    rest, few = jnp.zeros((4, 256), F32), jnp.zeros((4, HEADS), F32)
    shared = padded(slice(2 * INNER, 2 * INNER + 256), rest)
    steps = padded(slice(2 * INNER + 256, 2 * INNER + 256 + HEADS), few)
    for q in range(GROUP):
        split[q, :, 0:GW] = padded(slice(INNER + q * GW, INNER + (q + 1) * GW), extra)
        split[q, :, WR:ST] = shared
        split[q, :, ST:GA] = jnp.zeros((16, 128), BF16)
        split[q, :, ST : ST + OWN] = steps[:, q * OWN : (q + 1) * OWN]
        split[q, :, GA:COLS] = padded(slice(q * GW, (q + 1) * GW), extra)
    cuts = Members(lambda q: split.at[q], lambda q: joined.at[q], a_s, a_r)
    cuts.start()
    joined[rank] = split[rank]
    length = jnp.sum(jnp.where(owners[...] == lax.axis_index("fsdp"), lengths[...], 0), axis=1, keepdims=True)
    live = iota((SEQ, 1), 0) < length
    live_grd[...] = jnp.where(live, grd[...].astype(F32), 0.0).astype(BF16)
    end = outw[16:24, :].astype(F32)
    tail = jnp.concatenate([end[:, 0 : D // 2], end[:, D // 2 :]], axis=0).astype(BF16)
    outl[0] = outw[0:16, 0:WIDE]
    outl[1, :, 0 : D - WIDE] = outw[0:16, WIDE:D]
    outl[1, :, D - WIDE :] = tail
    own_heads(heads_in, rank, head, skip)

    hidden = GroupGather(hall, hid, h_s, h_r)
    grads = GroupGather(gall, live_grd, g_s, g_r)
    first_w = PlaneGather(wx, lambda h: block.at[h], wx_s, wx_r, 2)
    gate_w = PlaneGather(wg, lambda h: gblock.at[h], wg_s, wg_r, 2)
    vecs = PlaneGather(praw, lambda h: params, p_s, p_r, 1)
    out_lines = PlaneGather(plane, lambda h: outl.at[h], l_s, l_r, 2)
    out_rows = Members(lambda q: plane.at[q // 2, pl.ds((q % 2) * 2, 2)], lambda q: oraw.at[q], o_s, o_r)

    cuts.finish()
    hidden.start()
    row, col = iota((128, 128), 0), iota((128, 128), 1)
    member, line = col // 16, col % 16
    spot = jnp.where(line < KIN, member * KIN + line, 96 + member * 4 + line - KIN)
    both = dot(ones(spot == row), joined[...].reshape(128, COLS)).astype(BF16)
    for h in range(2):
        block[h] = both[48 * h : 48 * h + 48, 0:GA]
        gblock[h] = both[48 * h : 48 * h + 48, GA:COLS]
    params[...] = both[96:128, 0:256]
    vecs.start()
    first_w.start()
    wx[z, x] = block[...]
    wg[z, x] = gblock[...]
    praw[z, x, 0] = params[...]
    hall[y, c] = hid[...]
    gall[y, c] = live_grd[...]
    plane[z, x] = outl[...]
    vecs.forward()
    first_w.forward()
    vecs.finish()
    unpack_params(praw, rank, par)
    hidden.forward()
    hidden.finish()

    def lower(b, carry):
        h = hall[b // 2, b % 2].astype(F32)
        scale = lax.rsqrt(jnp.mean(h * h, axis=1, keepdims=True) + EPSILON)
        low[pl.ds(pl.multiple_of(b * SEQ, SEQ), SEQ), :] = (h * scale * par[0:1, :]).astype(BF16)
        return carry

    lax.fori_loop(0, GROUP, lower, 0)
    grads.start()
    first_w.finish()
    gate_w.start()
    out_lines.start()

    def chunk(i):
        return pl.ds(pl.multiple_of(i * 256, 256), 256)

    def project(i, carry):
        proj[chunk(i), 0:GA] = dot(low[chunk(i), :], wx[...].reshape(D, GA))
        return carry

    lax.fori_loop(0, ROWS // 256, project, 0)
    gate_w.forward()
    out_lines.forward()

    def forward(b, carry):
        @pl.when(b == 4)
        def _():
            out_lines.finish()
            out_rows.start()
            oraw[rank] = plane[rank // 2, pl.ds((rank % 2) * 2, 2)]

        mix_forward(b, proj, par, head, skip, heads_out)
        return carry

    lax.fori_loop(0, GROUP, forward, 0)
    gate_w.finish()

    def project_gate(i, carry):
        proj[chunk(i), GA:COLS] = dot(low[chunk(i), :], wg[...].reshape(D, GW))
        return carry

    lax.fori_loop(0, ROWS // 256, project_gate, 0)
    grads.forward()
    out_rows.finish()
    unfold_out_weight(oraw, ow)
    grads.finish()

    def pull(i, carry):
        dgated[chunk(i), :] = dot_nt(gall[i].reshape(256, D), ow[...])
        return carry

    lax.fori_loop(0, ROWS // 256, pull, 0)
    acc = lax.fori_loop(
        0, GROUP, lambda b, acc: norm_sums(b, proj, par, heads_out, dgated, acc), jnp.zeros((SEQ, SEQ), F32)
    )
    sums[...] = acc.T[0:16, :]
    norms = Members(lambda q: sums, lambda q: slots.at[q], n_s, n_r)
    norms.start()
    slots[rank] = sums[...]
    small[...] = jnp.zeros_like(small)
    norms.finish()
    total = slots[0]
    for q in range(1, GROUP):
        total = total + slots[q]
    wide[...] = jnp.concatenate([total, jnp.zeros((SEQ - 16, SEQ), F32)], axis=0).T

    def norms_back(b, carry):
        norm_back(b, proj, par, wide, heads_out, dgated, gated, dproj, small)
        return carry

    lax.fori_loop(0, GROUP, norms_back, 0)

    branches = GroupReduce(hall, gb, mb, lb, fb, b_s, b_r)
    lowers = GroupReduce(d_low, gd, md, ld, fd, d_s, d_r)
    weights = PlaneReduce(dw, gw, mw, lw, fw, rw_s, rw_r)
    out_sums = PlaneReduce(tl, gl, ml, ll, fl, rl_s, rl_r)
    to_plane = Members(lambda q: dow.at[q], lambda q: tl.at[q // 2, pl.ds((q % 2) * 2, 2)], ro_s, ro_r)
    cut_rows = Members(lambda q: cut.at[q], lambda q: rows_in.at[q], rr_s, rr_r)
    all_small = Members(lambda q: small_all.at[rank], lambda q: small_all.at[q], sg_s, sg_r)

    def small_z(k):
        return remote(small, zs.at[z], sz_s.at[k], sz_r.at[k], on_z(k))

    def small_x(k):
        return remote(part, xs.at[x], sx_s.at[k], sx_r.at[k], on_x(k))

    hidden.sent()
    branch = hall

    def out_term(i, carry):
        branch[i] = dot(gated[chunk(i), :], ow[...]).astype(BF16).reshape(2, SEQ, D)
        return carry

    lax.fori_loop(0, ROWS // 256, out_term, 0)
    branches.start()
    out = dot_tn(gated[...], gall[...].reshape(ROWS, D))
    for j in range(16):
        piece = out[j * KOUT : (j + 1) * KOUT]
        tail = jnp.concatenate([piece[16:24, 0 : D // 2], piece[16:24, D // 2 :]], axis=0)
        fold = jnp.concatenate([piece[0:16], tail], axis=1).astype(BF16)
        for h in range(2):
            dow[j % 8, j // 8, h] = fold[:, h * WIDE : (h + 1) * WIDE]
    to_plane.start()
    tl[rank // 2, pl.ds((rank % 2) * 2, 2)] = dow[rank]

    def backward(b, carry):
        @pl.when(b == 2)
        def _():
            branches.middle()

        @pl.when(b == 6)
        def _():
            to_plane.finish()
            out_sums.start()

        mix_back(b, proj, par, head, skip, dgated, dproj, small)
        return carry

    lax.fori_loop(0, GROUP, backward, 0)
    for k in (1, 2, 3):
        small_z(k).start()
    zs[z] = small[...]

    def slab(k):
        at = (z + k) % 4
        rows = dot_tn(low[:, pl.ds(pl.multiple_of(at * GW, GW), GW)], dproj[...]).astype(BF16)
        dw[at] = rows.reshape(4, 2, 48, COLS)

    for k in (2, 1, 3, 0):
        slab(k)
        if k:
            weights.first(1, k).start()
    for k in (2, 1, 3):
        weights.first(0, k).start()
    out_sums.middle()

    def lower_back(i, carry):
        back = dot_nt(dproj[chunk(i), 0:GA], wx[...].reshape(D, GA))
        back = back + dot_nt(dproj[chunk(i), GA:COLS], wg[...].reshape(D, GW))
        d_low[i] = back.astype(BF16).reshape(2, SEQ, D)
        return carry

    lax.fori_loop(0, ROWS // 256, lower_back, 0)
    lowers.start()
    for k in (1, 2, 3):
        small_z(k).wait_recv()
    part[...] = ((zs[0] + zs[1]) + zs[2]) + zs[3]
    xs[x] = part[...]
    for k in (1, 2, 3):
        small_x(k).start()
    branches.end()
    h32 = hid[...].astype(F32)
    mixed[...] = (h32 + jnp.where(live, fb[...], 0.0)).astype(BF16)
    weights.middle()
    lowers.middle()
    for k in (1, 2, 3):
        small_x(k).wait_recv()
    small_all[rank] = ((xs[0] + xs[1]) + xs[2]) + xs[3]
    all_small.start()
    out_sums.end()
    doutw[0:16, 0:WIDE] = fl[0]
    doutw[0:16, WIDE:D] = fl[1, :, 0 : D - WIDE]
    doutw[16:24, 0 : D // 2] = fl[1, 0:8, D - WIDE :]
    doutw[16:24, D // 2 : D] = fl[1, 8:16, D - WIDE :]
    weights.end()
    for q in range(GROUP):
        cut[q] = jnp.zeros((16, COLS), BF16)
        cut[q, 0:KIN, :] = fw[q // 4, q % 4 * KIN : (q % 4 + 1) * KIN, :].astype(BF16)
    cut_rows.start()
    rows_in[rank] = cut[rank]
    all_small.finish()
    finish_small(small_all, dconv, dheads, dinner)
    lowers.end()
    scale = lax.rsqrt(jnp.mean(h32 * h32, axis=1, keepdims=True) + EPSILON)
    normed = h32 * scale
    d_normed = fd[...] * par[0:1, :]
    through = scale * (d_normed - normed * jnp.mean(d_normed * normed, axis=1, keepdims=True))
    in_grad[...] = (grd[...].astype(F32) + through).astype(BF16)
    cut_rows.finish()
    finish_rows(rows_in, inw, vectors, dinw, dgain)
    for gone in (grads, first_w, gate_w, vecs, out_lines, cuts, out_rows, norms, to_plane, cut_rows, all_small):
        gone.sent()
    for gone in (branches, lowers, weights, out_sums):
        gone.finish()
    for k in (1, 2, 3):
        small_z(k).wait_send()
        small_x(k).wait_send()


def finish_small(small, dconv, dheads, dinner):
    me = lax.axis_index("fsdp")
    conv = jnp.zeros((32, 8), F32)
    inner = jnp.zeros((32, 8), F32)
    common = jnp.zeros((8, 256), F32)
    line = iota((32, GW), 0)
    heads = ones(iota((GW, 128), 0) // 64 == iota((GW, 128), 1), F32)
    dheads[...] = jnp.zeros_like(dheads)
    for q in range(GROUP):
        part = small[q, :, 0:GW]
        lane = iota((32, GW), 1) + q * GW
        conv = conv + dot_nt(ones(lane == line + 26 * me, F32), part, HIGHEST)
        inner = inner + dot_nt(ones(lane == line + KOUT * me, F32), part, HIGHEST)
        common = common + small[q, :, GW:CW]
        span = slice(q * OWN, (q + 1) * OWN)
        dheads[0:1, span] = small[q, 7:8, 0:OWN]
        dheads[1:2, span] = small[q, 7:8, 128 : 128 + OWN]
        dheads[2:3, span] = dot(part, heads, HIGHEST)[6:7, 0:OWN]
    lane = iota((32, 256), 1) + INNER
    dconv[...] = conv + dot_nt(ones(lane == iota((32, 256), 0) + 26 * me, F32), common, HIGHEST)
    dinner[...] = inner


def finish_rows(rows, inw, vectors, dinw, dgain):
    shared = jnp.zeros((KIN, 256), F32)
    for q in range(GROUP):
        own = rows[q].astype(F32)[0:KIN]
        dinw[:, INNER + q * GW : INNER + (q + 1) * GW] = own[:, 0:GW]
        dinw[:, q * GW : (q + 1) * GW] = own[:, GA:COLS]
        at = 2 * INNER + 256 + q * OWN
        dinw[:, at : at + OWN] = own[:, ST : ST + OWN]
        shared = shared + own[:, WR:ST]
    dinw[:, 2 * INNER : 2 * INNER + 256] = shared
    total = jnp.sum(dinw[...] * inw[...].astype(F32), axis=1, keepdims=True)
    gain = jnp.where(iota((KIN, 128), 0) == iota((KIN, 128), 1), vectors[...].astype(F32), 0.0)
    dgain[...] = total / jnp.sum(gain, axis=1, keepdims=True)


def layer(*given):
    vmem, vm = pl.BlockSpec(memory_space=pltpu.VMEM), pltpu.VMEM
    shape = jax.ShapeDtypeStruct

    def dma(*dims):
        return pltpu.SemaphoreType.DMA(dims)

    seven, pair = [dma(GROUP)] * 2, [dma(2, 4)] * 2
    return pl.pallas_call(
        layer_kernel,
        name="layer",
        out_shape=OUT_SHAPES,
        in_specs=[vmem] * len(given),
        out_specs=(vmem,) * len(OUT_SHAPES),
        scratch_shapes=[
            vm((GROUP, 16, COLS), BF16), vm((GROUP, 16, COLS), BF16), vm((2, 48, GA), BF16), vm((2, 48, GW), BF16),
            vm((32, 256), BF16), vm((2, 16, WIDE), BF16), vm((SEQ, D), BF16),
            vm((4, 4, 2, 48, GA), BF16), vm((4, 4, 2, 48, GW), BF16), vm((4, 4, 1, 32, 256), BF16),
            vm((4, 4, 2, 16, WIDE), BF16), vm((GROUP, 2, 2, 16, WIDE), BF16),
            vm((4, 2, SEQ, D), BF16), vm((4, 2, SEQ, D), BF16),
            vm((ROWS, D), BF16), vm((ROWS, COLS), F32), vm((ROWS, GW), F32), vm((ROWS, GW), F32), vm((GW, D), BF16),
            vm((8, D), F32), vm((8, 128), F32), vm((1, GW), F32),
            vm((16, SEQ), F32), vm((GROUP, 16, SEQ), F32), vm((SEQ, SEQ), F32),
            vm((ROWS, GW), BF16), vm((ROWS, COLS), BF16), vm((4, 2, SEQ, D), BF16),
            vm((4, 4, 2, 48, COLS), BF16), vm((GROUP, 2, 2, 16, WIDE), BF16), vm((8, CW), F32),
            vm((4, SEQ, D), BF16), vm((3, SEQ, D), BF16), vm((3, SEQ, D), BF16), vm((SEQ, D), F32),
            vm((4, SEQ, D), BF16), vm((3, SEQ, D), BF16), vm((3, SEQ, D), BF16), vm((SEQ, D), F32),
            vm((2, 3, 4, 48, COLS), BF16), vm((2, 3, 48, COLS), BF16), vm((2, 3, 48, COLS), BF16), vm((2, 48, COLS), F32),
            vm((4, 4, 2, 16, WIDE), BF16),
            vm((2, 3, 4, 16, WIDE), BF16), vm((2, 3, 16, WIDE), BF16), vm((2, 3, 16, WIDE), BF16), vm((2, 16, WIDE), F32),
            vm((GROUP, 16, COLS), BF16), vm((GROUP, 16, COLS), BF16),
            vm((4, 8, CW), F32), vm((4, 8, CW), F32), vm((8, CW), F32), vm((GROUP, 8, CW), F32),
            *seven,
            dma(2, 5, 4), dma(2, 4, 4), dma(2, 5, 4), dma(2, 4, 4), dma(1, 5, 4), dma(1, 4, 4), dma(2, 5, 4), dma(2, 4, 4),
            *pair, *pair, *seven, *seven,
            *pair, *pair, *[dma(2, 2, 4)] * 4, *seven, *seven, *[dma(4)] * 4, *seven, dma(8),
        ],
        compiler_params=pltpu.CompilerParams(collective_id=0, has_side_effects=True, vmem_limit_bytes=VMEM_LIMIT),
    )(*given)


OUT_SHAPES = (
    jax.ShapeDtypeStruct((SEQ, D), BF16),
    jax.ShapeDtypeStruct((SEQ, D), BF16),
    jax.ShapeDtypeStruct((KIN, 2 * INNER + 256 + HEADS), F32),
    jax.ShapeDtypeStruct((KIN, 1), F32),
    jax.ShapeDtypeStruct((32, 8), F32),
    jax.ShapeDtypeStruct((8, HEADS), F32),
    jax.ShapeDtypeStruct((32, 8), F32),
    jax.ShapeDtypeStruct((KOUT, D), F32),
)


def body(
    hidden, in_weight, norm_gain, conv_weight, conv_bias, dt_bias, a_log, skip, inner_gain, out_weight, out_grad,
    seq_lengths, seq_owner,
):
    vectors = jnp.concatenate([norm_gain, conv_bias, inner_gain, jnp.zeros((66,), BF16)])[None, :]
    heads = jnp.pad(jnp.stack([dt_bias, a_log, skip]), ((0, 5), (0, 128 - HEADS)))
    mixed, in_grad, dinw, dgain, dconv, dheads, dinner, doutw = layer(
        hidden, in_weight, vectors, conv_weight, heads, out_weight, out_grad, seq_lengths[None, :], seq_owner[None, :]
    )
    return (
        mixed,
        in_grad,
        dinw,
        dgain[:, 0],
        dconv[:26, :4],
        dconv[:26, 4],
        dheads[0],
        dheads[1],
        dheads[2],
        dinner[:KOUT, 5],
        doutw,
    )


def solution(mesh):
    rows, line, whole = P("fsdp", None), P("fsdp"), P()
    return jax.shard_map(
        body,
        mesh=mesh,
        in_specs=(rows, rows, line, rows, line, whole, whole, whole, line, rows, rows, whole, whole),
        out_specs=(rows, rows, rows, line, rows, line, whole, whole, whole, line, rows),
        check_vma=False,
    )
```

time: 226 us -> 173 us (0.77)
  Pallas kernels: 202 us -> 159 us
  other arithmetic: 10.8 us -> 2.52 us
  local copies, waits for them, and re-layouts: 12 us -> 9.55 us
    pallas_call x6 -> x1, Pallas kernels: 202 us -> 159 us  [layer(): pl.pallas_call(layer_kernel, name='layer', out_shape=OUT_SHAPES, in_specs...]
    unnamed x5 -> x30, local copies, waits for them, and re-layouts: 1.39 us -> 6.85 us
where the time goes in v2:
time: 173 us; the launch traced here: 172 us
  Pallas kernels  159 us (92%)
  local copies, waits for them, and re-layouts  9.55 us (6%)
  other arithmetic  2.52 us (1%)
    pallas_call x1, Pallas kernels, layer(): pl.pallas_call(layer_kernel, name='layer', out_shape=OUT_SHAPES, in_specs...  159 us
    unnamed x30, local copies, waits for them, and re-layouts  6.85 us

profile of v2, /device:TPU:1, one launch (start us, length us, event | category | flops | bytes accessed | tf_op | source)
XLA Modules:
  0.0 172.2 jit_solution(18059946946185358477)
XLA Ops:
  0.6 0.0 copy-start.6
  0.7 0.0 copy-start.7
  0.7 0.0 copy-start.8
  0.7 0.6 copy-done.6
  1.3 0.0 copy-done.7
  1.3 0.0 copy-done.8
  1.3 0.0 copy-start.9
  1.3 0.0 copy-start.10
  1.3 0.0 copy-start.11
  1.3 0.6 maximum_bitcast_fusion.vectors
  1.9 0.1 copy-done.9
  2.0 0.0 copy-done.10
  2.0 0.0 copy-done.11
  2.0 0.0 copy-start.5
  2.0 0.6 select_maximum_fusion.heads_in
  2.6 0.1 copy-done.5
  2.7 0.7 copy.26.taps
  3.4 159.4 %layer.1 = (bf16[128,1536]{1,0:T(8,128)(2,1)}, bf16[128,1536]{1,0:T(8,128)(2,1)}, f32[12,6448]{1,0:T(8,128)}, f32[12,1]{1,0:T(8,128)}, f32[32,8]{1,0:T(8,128)}, ...) custom-call(bf16[128,1536]{1,0:T(8,128)(2,1)} %hid.1, bf16[12,6448]{1,0:T(8,128)(2,1)} %inw.1, ...), custom_call_target="tpu_custom_call" | custom-call | tf_op jit(solution)/shard_map/layer/pallas_call | solution.py:859
  162.8 0.0 copy-start.4
  162.9 0.0 copy-start.3
  162.9 1.3 reduce
  164.2 0.0 copy-done.4
  164.2 0.7 slice_reduce_fusion.1
  164.9 0.0 copy-done.3
  164.9 0.7 slice_reduce_fusion
  165.6 1.3 slice_bitcast_fusion
  166.9 0.7 copy.27
  167.6 0.0 copy-start.1
  167.6 1.8 %copy.32 = bf16[128,1536]{1,0:T(8,128)(2,1)} copy(bf16[128,1536]{1,0:T(8,128)(2,1)} %get-tuple-element.63) | data formatting | bytes 786432
  169.4 0.0 copy-done.1
  169.4 0.0 copy-start
  169.4 0.7 copy.33
  170.1 0.4 copy-done
  170.5 0.0 copy-start.2
  170.5 0.8 copy.34
  171.3 0.3 copy-done.2
  171.6 0.7 copy.35
  (1 shorter events, 0.0 us)
Async XLA Ops:
  0.6 0.7 copy-start.6
  0.7 0.7 copy-start.7
  0.7 0.7 copy-start.8
  1.3 0.7 copy-start.9
  1.3 0.7 copy-start.10
  1.3 0.7 copy-start.11
  2.0 0.7 copy-start.5
  162.8 1.4 copy-start.4
  162.9 2.0 %copy-start.3 = (f32[32,8]{1,0:T(8,128)S(1)}, f32[32,8]{1,0:T(8,128)}, u32[]{:S(2)}) copy-start(f32[32,8]{1,0:T(8,128)} %get-tuple-element.23) | copy-start | bytes 3076
  167.6 1.8 %copy-start.1 = (bf16[128,1536]{1,0:T(8,128)(2,1)S(1)}, bf16[128,1536]{1,0:T(8,128)(2,1)}, u32[]{:S(2)}) copy-start(bf16[128,1536]{1,0:T(8,128)(2,1)} %get-tuple-element.64) | copy-start | bytes 1179652
  169.4 1.1 copy-start
  170.5 1.0 copy-start.2

commit v3 on v2

v3 whole, which is shorter than its diff:
```python
import functools

import jax
import jax.numpy as jnp
from jax import lax
from jax.experimental import pallas as pl
from jax.experimental.pallas import tpu as pltpu
from jax.sharding import PartitionSpec as P

MESH = pl.DeviceIdType.MESH
F32, BF16 = jnp.float32, jnp.bfloat16
HIGHEST = lax.Precision.HIGHEST
EPSILON = 1e-05

D = 1536
INNER = 3072
CONVD = 3328
HEADS = 48
SEQ = 128
GROUP = 8
ROWS = SEQ * GROUP
GW = INNER // GROUP
OWN = HEADS // GROUP
CW = GW + 128
GA, COLS = CW, CW + GW
ST = COLS
KIN = D // 128
KOUT = INNER // 128
STEP = 2 * INNER + 256
FOLD = D + D // 2
WIDE = FOLD // 2
VMEM_LIMIT = 60 * 2**20


def iota(shape, dim):
    return lax.broadcasted_iota(jnp.int32, shape, dim)


def ones(condition, kind=BF16):
    return jnp.where(condition, 1.0, 0.0).astype(kind)


def dot(a, b, precision=None):
    return lax.dot_general(a, b, (((1,), (0,)), ((), ())), precision=precision, preferred_element_type=F32)


def dot_nt(a, b, precision=None):
    return lax.dot_general(a, b, (((1,), (1,)), ((), ())), precision=precision, preferred_element_type=F32)


def dot_tn(a, b, precision=None):
    return lax.dot_general(a, b, (((0,), (0,)), ((), ())), precision=precision, preferred_element_type=F32)


def sigmoid(v):
    return 1.0 / (1.0 + jnp.exp(-v))


def softplus(v):
    return jnp.maximum(v, 0.0) + jnp.log1p(jnp.exp(-jnp.abs(v)))


def later(v, k):
    if k == 0:
        return v
    return jnp.where(iota(v.shape, 0) >= k, pltpu.roll(v, k, 0), 0.0)


def earlier(v, k):
    if k == 0:
        return v
    return jnp.where(iota(v.shape, 0) < v.shape[0] - k, pltpu.roll(v, v.shape[0] - k, 0), 0.0)


def place():
    me = lax.axis_index("fsdp")
    return me // 32, (me // 8) % 4, (me // 2) % 4, me % 2


def index(z, x, y, c):
    return ((z * 4 + x) * 4 + y) * 2 + c


def group_partner(k):
    z, x, y, c = place()
    rank = (y * 2 + c + k) % GROUP
    return index(z, x, rank // 2, rank % 2), rank


def on_z(k):
    z, x, y, c = place()
    return index((z + k) % 4, x, y, c)


def on_x(k):
    z, x, y, c = place()
    return index(z, (x + k) % 4, y, c)


def on_y(k):
    z, x, y, c = place()
    return index(z, x, (y + k) % 4, c)


def sibling():
    z, x, y, c = place()
    return index(z, x, y, 1 - c)


def swap_to():
    z, x, y, c = place()
    return index(y, x % 2 * 2 + c, z, x // 2)


def swap_from():
    z, x, y, c = place()
    return index(y, c * 2 + x // 2, z, x % 2)


def signal(target):
    pl.semaphore_signal(pltpu.get_barrier_semaphore(), inc=1, device_id=(target,), device_id_type=MESH)


def remote(src, dst, send, recv, target):
    return pltpu.make_async_remote_copy(
        src_ref=src, dst_ref=dst, send_sem=send, recv_sem=recv, device_id=(target,), device_id_type=MESH
    )


def plane_partners():
    return [on_z(k) for k in (1, 2, 3)] + [on_x(k) for k in (1, 2, 3)]


def group_partners():
    return [group_partner(k)[0] for k in range(1, GROUP)]


class PlaneGather:
    def __init__(self, buf, own, send, recv, halves):
        self.buf, self.own, self.send, self.recv, self.halves = buf, own, send, recv, halves
        self.z, self.x, _, _ = place()

    def slot(self, half, first, second):
        a, b = (first, second) if half == 0 else (second, first)
        return self.buf.at[(self.z + a) % 4, (self.x + b) % 4, half]

    def along(self, half, stage, k):
        return on_z(k) if (half == 0) == (stage == 0) else on_x(k)

    def copy(self, half, first, stage, k):
        src = self.own(half) if first == 0 else self.slot(half, first, 0)
        at = (4 - k, 0) if stage == 0 else (first, 4 - k)
        return remote(
            src,
            self.slot(half, first, 0),
            self.send.at[half, first if stage else 4, k],
            self.recv.at[half, at[0], at[1]],
            self.along(half, stage, k),
        )

    def relayed(self, half, first):
        came, k = (3, 1) if first < 2 else (1, 3)
        here = self.slot(half, first, came)
        return remote(here, here, self.send.at[half, first, 2], self.recv.at[half, first, 2], self.along(half, 1, k))

    def arrival(self, half, first, second):
        here = self.slot(half, first, second)
        return remote(here, here, self.send.at[half, 4, 0], self.recv.at[half, first, second], on_z(1))

    def start(self):
        for k in (1, 3, 2):
            for half in range(self.halves):
                self.copy(half, 0, 0, k).start()
        for k in (1, 3):
            for half in range(self.halves):
                self.copy(half, 0, 1, k).start()

    def forward(self):
        for first in (1, 3, 2):
            for half in range(self.halves):
                self.arrival(half, first, 0).wait_recv()
                for k in (1, 3):
                    self.copy(half, first, 1, k).start()

    def relay(self):
        for first in (0, 3, 1, 2):
            for half in range(self.halves):
                self.arrival(half, first, 3 if first < 2 else 1).wait_recv()
                self.relayed(half, first).start()

    def finish(self):
        for first in range(4):
            for half in range(self.halves):
                self.arrival(half, first, 1 if first < 2 else 3).wait_recv()
        for first in range(4):
            for half in range(self.halves):
                self.arrival(half, first, 2).wait_recv()

    def sent(self):
        for half in range(self.halves):
            for k in (1, 2, 3):
                self.copy(half, 0, 0, k).wait_send()
            for first in range(4):
                for k in (1, 3):
                    self.copy(half, first, 1, k).wait_send()
                self.relayed(half, first).wait_send()


class GroupGather:
    def __init__(self, buf, own, send, recv):
        self.buf, self.own, self.send, self.recv = buf, own, send, recv
        _, _, self.y, self.c = place()

    def along(self, k):
        return remote(self.own, self.buf.at[self.y, self.c], self.send.at[0, k], self.recv.at[0, 4 - k], on_y(k))

    def half(self, k):
        return pl.ds(0, SEQ // 2) if k == 3 else pl.ds(SEQ // 2, SEQ // 2)

    def relayed(self, k):
        here = self.buf.at[(self.y + k) % 4, self.c, self.half(k)]
        at = 2 if k == 3 else 0
        return remote(here, here, self.send.at[0, at], self.recv.at[0, at], on_y(4 - k))

    def across(self, k):
        src = self.own if k == 0 else self.buf.at[(self.y + k) % 4, self.c]
        dst = self.buf.at[(self.y + k) % 4, self.c]
        return remote(src, dst, self.send.at[1, k], self.recv.at[1, k], sibling())

    def start(self):
        for k in (1, 3):
            self.along(k).start()
        self.across(0).start()

    def forward(self, k):
        if k == 2:
            for came in (3, 1):
                here = self.buf.at[(self.y + 2) % 4, self.c, self.half(came)]
                at = 2 if came == 3 else 0
                remote(here, here, self.send.at[0, at], self.recv.at[0, at], sibling()).wait_recv()
        else:
            here = self.buf.at[(self.y + k) % 4, self.c]
            remote(here, here, self.send.at[0, k], self.recv.at[0, k], sibling()).wait_recv()
            self.relayed(k).start()
        self.across(k).start()

    def arrived(self, k):
        here = self.buf.at[(self.y + k) % 4, 1 - self.c]
        remote(here, here, self.send.at[1, k], self.recv.at[1, k], sibling()).wait_recv()

    def sent(self):
        for k in (1, 3):
            self.along(k).wait_send()
            self.relayed(k).wait_send()
        for k in range(4):
            self.across(k).wait_send()


def unpack_params(raw, rank, core, par, step_rows):
    row = iota((512, 1), 0)
    device = (row // 4).astype(F32)
    tap = row % 4
    values = raw[...].reshape(512, 384)

    def spots(span, first, count, channel):
        owner = jnp.floor((channel + 0.5) * (1.0 / count))
        lane = channel - owner * count + first
        pick = ones(iota((128, channel.shape[1]), 0).astype(F32) == lane)
        return jnp.where(device == owner, dot(values[:, span], pick), 0.0)

    def only(k, at):
        return jnp.sum(jnp.where(tap == k, at, 0.0), axis=0, keepdims=True)

    def lanes(n):
        return iota((1, n), 1).astype(F32)

    start = rank.astype(F32) * GW
    conv = lanes(CW)
    conv = jnp.where(conv < GW, conv + start, conv - GW + INNER + 128 * core.astype(F32))
    low, high, last = slice(0, 128), slice(128, 256), slice(256, 384)
    par[...] = jnp.zeros_like(par)
    par[0:1, :] = only(0, spots(high, 0, KIN, lanes(D)))
    taps = spots(low, 0, 26, conv)
    for k in range(4):
        par[k + 1 : k + 2, 0:CW] = only(k, taps)
    par[5:6, 0:CW] = only(0, spots(high, KIN, 26, conv))
    par[6:7, 0:GW] = only(0, spots(high, KIN + 26, KOUT, lanes(GW) + start))
    four, two = spots(last, 0, KIN, lanes(D)), spots(last, 16, KIN, lanes(D))
    rows = [only(k, four) for k in range(4)] + [only(k, two) for k in range(2)] + [jnp.zeros((122, D), F32)]
    step_rows[...] = jnp.concatenate(rows, axis=0).astype(BF16)


def own_heads(raw, rank, head, skip):
    row = iota((128, 128), 0)
    col = iota((128, 128), 1)
    given = raw[...]
    mine = dot(given, ones(jnp.logical_and(row == col + OWN * rank, col < OWN), F32), HIGHEST)
    head[...] = jnp.where(iota((8, 128), 0) == 1, -jnp.exp(mine), mine)
    wide = iota((128, GW), 0) == iota((128, GW), 1) // 64 + OWN * rank
    skip[...] = dot(given, ones(wide, F32), HIGHEST)[2:3]


def unfold_out_weight(raw, ow):
    row, col = iota((GW, 256), 0), iota((GW, 256), 1)
    device, line = row // KOUT, row % KOUT
    base = (device % 8 // 2 * 4 + device // 8 * 2 + device % 2) * 16
    top = ones(jnp.logical_and(line < 16, col == base + line))
    low_left = ones(jnp.logical_and(line >= 16, col == base + line - 16))
    low_right = ones(jnp.logical_and(line >= 16, col == base + line - 8))
    first = raw[:, :, 0].reshape(256, WIDE)
    second = raw[:, :, 1].reshape(256, WIDE)
    half, split = D // 2, WIDE - D // 2
    left, right_a = first[:, 0:half], first[:, half:]
    right_b, tail = second[:, 0 : half - split], second[:, half - split :]
    ow[:, 0:half] = (dot(top, left) + dot(low_left, tail)).astype(BF16)
    ow[:, half : half + split] = (dot(top, right_a) + dot(low_right, tail[:, 0:split])).astype(BF16)
    ow[:, half + split :] = (dot(top, right_b) + dot(low_right, tail[:, split:])).astype(BF16)


def convolve(raw, par, at, width):
    out = par[5:6, at : at + width] + raw * par[4:5, at : at + width]
    for k in range(3):
        out = out + later(raw, 3 - k) * par[k + 1 : k + 2, at : at + width]
    return out


def steps_of(raw, head):
    step = softplus(raw + head[0:1, :])
    decay = head[1:2, :] * step
    lower = ones(iota((SEQ, SEQ), 0) >= iota((SEQ, SEQ), 1), F32)
    total = dot(lower, decay, HIGHEST)
    return step, decay, total


def mix_forward(b, proj, act, par, head, skip, heads_out):
    row, col = iota((SEQ, SEQ), 0), iota((SEQ, SEQ), 1)
    causal = row >= col
    rows = pl.ds(pl.multiple_of(b * SEQ, SEQ), SEQ)
    write, read = act[0, rows, :], act[1, rows, :]
    step, _, total = steps_of(proj[rows, ST:], head)
    total_t, step_t = total.T, step.T
    scores = dot_nt(read, write, HIGHEST)
    for p in range(3):
        at = p * 128
        values = convolve(proj[rows, at : at + 128], par, at, 128)
        values = values * sigmoid(values)
        values_low = values.astype(BF16)
        parts = []
        for h in (2 * p, 2 * p + 1):
            decays = jnp.exp(jnp.where(causal, total[:, h : h + 1] - total_t[h : h + 1, :], -1e30))
            mix = (decays * scores * step_t[h : h + 1, :]).astype(BF16)
            parts.append(dot(mix, values_low))
        heads_out[rows, at : at + 128] = jnp.where(col < 64, parts[0], parts[1]) + skip[0:1, at : at + 128] * values


def norm_sums(b, proj, par, heads_out, dgated, acc):
    rows = pl.ds(pl.multiple_of(b * SEQ, SEQ), SEQ)
    gate = proj[rows, GA:COLS]
    product = heads_out[rows, :] * gate * sigmoid(gate)
    squares = jnp.sum(product * product, axis=1, keepdims=True)
    crosses = jnp.sum(product * dgated[rows, :] * par[6:7, 0:GW], axis=1, keepdims=True)
    col = iota((SEQ, SEQ), 1)
    return jnp.where(col == b, squares, jnp.where(col == b + 8, crosses, acc))


def norm_back(b, proj, par, wide, heads_out, dgated, gated, dproj, small):
    rows = pl.ds(pl.multiple_of(b * SEQ, SEQ), SEQ)
    col = iota((SEQ, SEQ), 1)
    square = jnp.sum(jnp.where(col == b, wide[...], 0.0), axis=1, keepdims=True)
    cross = jnp.sum(jnp.where(col == b + 8, wide[...], 0.0), axis=1, keepdims=True)
    inverse = lax.rsqrt(square * (1.0 / INNER) + EPSILON)
    mean = cross * inverse * (1.0 / INNER)
    out = heads_out[rows, :]
    gate = proj[rows, GA:COLS]
    s = sigmoid(gate)
    silu = gate * s
    unit = out * silu * inverse
    dg = dgated[rows, :]
    gain = par[6:7, 0:GW]
    gated[rows, :] = (unit * gain).astype(BF16)
    small[5:6, 0:GW] += jnp.sum(dg * unit, axis=0, keepdims=True)
    d_product = (dg * gain - unit * mean) * inverse
    dproj[rows, GA:COLS] = (d_product * out * (s * (1.0 + gate * (1.0 - s)))).astype(BF16)
    dgated[rows, :] = d_product * silu


def conv_back(d_act, raw, v, s, par, small, at):
    d_conv = d_act * s * (1.0 + v * (1.0 - s))
    span = slice(at, at + 128)
    back = d_conv * par[4:5, span]
    small[3:4, span] += jnp.sum(d_conv * raw, axis=0, keepdims=True)
    for k in range(3):
        back = back + earlier(d_conv, 3 - k) * par[k + 1 : k + 2, span]
        small[k : k + 1, span] += jnp.sum(d_conv * later(raw, 3 - k), axis=0, keepdims=True)
    small[4:5, span] += jnp.sum(d_conv, axis=0, keepdims=True)
    return back


def mix_back(b, core, proj, act, par, head, skip, d_heads, dproj, d_steps, small, d_mine, d_other):
    row, col = iota((SEQ, SEQ), 0), iota((SEQ, SEQ), 1)
    later_ok = col >= row
    left, right = col < 64, col >= 64
    suffix = ones(row >= col)
    before = row < col
    rows = pl.ds(pl.multiple_of(b * SEQ, SEQ), SEQ)

    write, read = act[0, rows, :], act[1, rows, :]
    raw_step = proj[rows, ST:]
    step, decay, total = steps_of(raw_step, head)
    total_t = total.T
    scores_t = dot_nt(write, read, HIGHEST)
    d_scores = jnp.zeros((SEQ, SEQ), F32)
    direct = jnp.zeros((SEQ, SEQ), F32)
    lines = []
    for p in range(3):
        at = p * 128
        span = slice(at, at + 128)
        d_out = d_heads[rows, span]
        raw = proj[rows, span]
        pre = convolve(raw, par, at, 128)
        sig = sigmoid(pre)
        values = pre * sig
        small[6:7, span] += jnp.sum(d_out * values, axis=0, keepdims=True)
        values_low = values.astype(BF16)
        d_low = d_out.astype(BF16)
        parts = []
        for i, h in enumerate((2 * p, 2 * p + 1)):
            decays = jnp.exp(jnp.where(later_ok, total_t[h : h + 1, :] - total[:, h : h + 1], -1e30))
            size = step[:, h : h + 1]
            own = jnp.where(left if i == 0 else right, d_out, 0.0).astype(BF16)
            d_mix = decays * dot_nt(values_low, own)
            d_scores = d_scores + d_mix * size
            per_step = (d_mix * scores_t).astype(BF16)
            tail = dot(per_step, suffix)
            direct = jnp.where(col == h, tail[:, 0:1], direct)
            lines.append(jnp.sum(jnp.where(before, tail * size, 0.0), axis=0, keepdims=True))
            mix = (decays * scores_t * size).astype(BF16)
            parts.append(dot(mix, d_low))
        d_values = jnp.where(left, parts[0], parts[1]) + skip[0:1, span] * d_out
        dproj[rows, span] = conv_back(d_values, raw, pre, sig, par, small, at).astype(BF16)
    d_decay = jnp.concatenate(lines + [jnp.zeros((SEQ - OWN, SEQ), F32)], axis=0).T
    d_step = direct + head[1:2, :] * d_decay
    d_raw = d_step * sigmoid(raw_step + head[0:1, :])
    small[7:8, 0:128] += jnp.sum(d_raw, axis=0, keepdims=True)
    small[7:8, 128:256] += jnp.sum(d_decay * decay, axis=0, keepdims=True)
    d_low = d_scores.astype(BF16)
    d_write = dot(d_low, read.astype(BF16))
    d_read = dot_tn(d_low, write.astype(BF16))
    d_mine[rows, :] = jnp.where(core == 0, d_write, d_read)
    d_other[rows, :] = jnp.where(core == 0, d_read, d_write)
    d_steps[rows, :] = d_raw.astype(BF16)


def vector_forward(b, core, proj, act, par):
    rows = pl.ds(pl.multiple_of(b * SEQ, SEQ), SEQ)
    v = convolve(proj[rows, GW:CW], par, GW, 128)
    act[core, rows, :] = v * sigmoid(v)


def vector_back(b, proj, par, d_mine, d_in, dproj, small):
    rows = pl.ds(pl.multiple_of(b * SEQ, SEQ), SEQ)
    raw = proj[rows, GW:CW]
    v = convolve(raw, par, GW, 128)
    d = d_mine[rows, :] + d_in[rows, :]
    dproj[rows, GW:CW] = conv_back(d, raw, v, sigmoid(v), par, small, GW).astype(BF16)


class PlaneReduce:
    def __init__(self, terms, got, mid, last, out, send, recv, halves=2):
        self.terms, self.got, self.mid, self.last, self.out = terms, got, mid, last, out
        self.send, self.recv, self.halves = send, recv, halves
        self.z, self.x, _, _ = place()

    def line(self, half, k):
        return self.terms.at[:, (self.x + k) % 4, 0] if half == 0 else self.terms.at[(self.z + k) % 4, :, 1]

    def first(self, half, k):
        target = on_x(k) if half == 0 else on_z(k)
        return remote(self.line(half, k), self.got.at[half, k - 1], self.send.at[half, 0, k], self.recv.at[half, 0, k], target)

    def second(self, half, k):
        target = on_z(k) if half == 0 else on_x(k)
        return remote(self.mid.at[half, k - 1], self.last.at[half, k - 1], self.send.at[half, 1, k], self.recv.at[half, 1, k], target)

    def start(self):
        for k in (2, 1, 3):
            for half in range(self.halves):
                self.first(half, k).start()

    def middle(self):
        for half in range(self.halves):
            for k in (1, 2, 3):
                self.first(half, k).wait_recv()
            for k in (2, 1, 3, 0):
                if half == 0:
                    at = (self.z + k) % 4
                    total = self.terms[at, self.x, 0].astype(F32)
                else:
                    at = (self.x + k) % 4
                    total = self.terms[self.z, at, 1].astype(F32)
                for j in range(3):
                    total = total + self.got[half, j, at].astype(F32)
                if k:
                    self.mid[half, k - 1] = total.astype(BF16)
                    self.second(half, k).start()
                else:
                    self.out[half] = total

    def end(self):
        for half in range(self.halves):
            for k in (1, 2, 3):
                self.second(half, k).wait_recv()
            total = self.out[half]
            for j in range(3):
                total = total + self.last[half, j].astype(F32)
            self.out[half] = total

    def finish(self):
        for half in range(self.halves):
            for k in (1, 2, 3):
                self.first(half, k).wait_send()
                self.second(half, k).wait_send()


class GroupReduce:
    def __init__(self, terms, got, mid, last, out, send, recv):
        self.terms, self.got, self.mid, self.last, self.out = terms, got, mid, last, out
        self.send, self.recv = send, recv
        _, _, self.y, self.c = place()

    def across(self, k):
        src = self.terms.at[(self.y + k) % 4, 1 - self.c]
        return remote(src, self.got.at[k], self.send.at[0, k], self.recv.at[0, k], sibling())

    def along(self, k):
        return remote(self.mid.at[k - 1], self.last.at[k - 1], self.send.at[1, k], self.recv.at[1, k], on_y(k))

    def half(self, k):
        self.across(k).wait_recv()
        return self.terms[(self.y + k) % 4, self.c].astype(F32) + self.got[k].astype(F32)

    def pass_on(self, k):
        self.mid[k - 1] = self.half(k).astype(BF16)
        self.along(k).start()

    def keep(self):
        self.out[...] = self.half(0)

    def end(self):
        for k in (1, 2, 3):
            self.along(k).wait_recv()
        total = self.out[...]
        for j in range(3):
            total = total + self.last[j].astype(F32)
        self.out[...] = total

    def finish(self):
        for k in range(4):
            self.across(k).wait_send()
            if k:
                self.along(k).wait_send()


class Members:
    def __init__(self, src, dst, send, recv):
        self.src, self.dst, self.send, self.recv = src, dst, send, recv
        _, _, y, c = place()
        self.rank = y * 2 + c

    def copy(self, k):
        target, q = group_partner(k)
        return remote(self.src(q), self.dst(self.rank), self.send.at[k], self.recv.at[k], target)

    def arrival(self, k):
        _, q = group_partner(k)
        return remote(self.dst(q), self.dst(q), self.send.at[k], self.recv.at[GROUP - k], sibling())

    def start(self):
        for k in range(1, GROUP):
            self.copy(k).start()

    def finish(self):
        for k in range(1, GROUP):
            self.arrival(k).wait_recv()

    def sent(self):
        for k in range(1, GROUP):
            self.copy(k).wait_send()


def layer_kernel(
    hid, inw, gain_in, taps, bias_in, dt_in, a_in, skip_in, inner_in, outw, grd, lengths, owners,
    mixed, in_grad, dinw, dvecs, doutw,
    vectors, heads_in, tap_rows,
    split, joined, block, gblock, params, outl, placed, live_grd,
    wx, wg, praw, plane, hall, gall, low, proj, act, step_rows, heads_out, dgated, ow, par, head, skip, sums, slots, wide,
    gated, dproj, d_steps, d_mine, d_other, d_in, d_low, dwx, dwg, dow, dws, small,
    gb, mb, lb, fb, gd, md, ld, fd, gx, mx, lx, fx, gg, mg, lg, fg, gl, ml, ll, fl, gs, ms, ls, fs,
    swapped, cut, rows_in, gcut, grows_in, zs, xs, part, small_all,
    a_s, a_r, wx_s, wx_r, wg_s, wg_r, p_s, p_r, l_s, l_r, h_s, h_r, g_s, g_r, n_s, n_r, v_s, v_r, u_s, u_r,
    b_s, b_r, d_s, d_r, rx_s, rx_r, rg_s, rg_r, rl_s, rl_r, rs_s, rs_r, rr_s, rr_r, rq_s, rq_r,
    sz_s, sz_r, sx_s, sx_r, sg_s, sg_r, swap_s, swap_r,
):
    z, x, y, c = place()
    rank = y * 2 + c
    me = lax.axis_index("fsdp")
    partners = plane_partners() + group_partners()
    moves = swap_to() != me
    for p in partners:
        signal(p)

    @pl.when(moves)
    def _():
        signal(swap_to())
        signal(swap_from())

    vectors[...] = jnp.zeros_like(vectors)
    heads_in[...] = jnp.zeros_like(heads_in)
    tap_rows[...] = jnp.zeros_like(tap_rows)
    vectors[0:1, 0:KIN] = gain_in[...].astype(F32)[None, :]
    vectors[0:1, KIN : KIN + 26] = bias_in[...].astype(F32)[None, :]
    vectors[0:1, KIN + 26 : KIN + 26 + KOUT] = inner_in[...].astype(F32)[None, :]
    for i, line in enumerate((dt_in, a_in, skip_in)):
        heads_in[i : i + 1, 0:HEADS] = line[...][None, :]
    tap_rows[0:4, 0:26] = taps[...].astype(F32)
    col_steps = inw[:, STEP : STEP + HEADS]
    steps_low = dot_tn(col_steps, ones(iota((KIN, 128), 0) == iota((KIN, 128), 1)))
    steps_high = dot_tn(col_steps, ones(iota((KIN, 128), 0) + 16 == iota((KIN, 128), 1)))
    rest = jnp.zeros((4, 128), F32)

    def padded(span, extra):
        return jnp.concatenate([inw[:, span].astype(F32), extra], axis=0).astype(BF16)

    vector_cols = [padded(slice(2 * INNER + 128 * i, 2 * INNER + 128 * (i + 1)), rest) for i in range(2)]
    for q in range(GROUP):
        at = q * OWN
        two = jnp.concatenate([steps_high[at + 4 : at + OWN], jnp.zeros((2, 128), F32)], axis=0)
        extra = jnp.concatenate([tap_rows[0:4], vectors[0:4], steps_low[at : at + 4] + two], axis=1)
        split[q, :, 0:GW] = padded(slice(INNER + q * GW, INNER + (q + 1) * GW), extra)
        split[q, :, GW:CW] = vector_cols[q % 2]
        split[q, :, GA:COLS] = padded(slice(q * GW, (q + 1) * GW), jnp.zeros((4, GW), F32))
    end = outw[16:24, :].astype(F32)
    tail = jnp.concatenate([end[:, 0 : D // 2], end[:, D // 2 :]], axis=0).astype(BF16)
    outl[0] = outw[0:16, 0:WIDE]
    outl[1, :, 0 : D - WIDE] = outw[0:16, WIDE:D]
    outl[1, :, D - WIDE :] = tail

    @pl.when(moves)
    def _():
        pl.semaphore_wait(pltpu.get_barrier_semaphore(), len(partners) + 2)

    @pl.when(jnp.logical_not(moves))
    def _():
        pl.semaphore_wait(pltpu.get_barrier_semaphore(), len(partners))

    cuts = Members(lambda q: split.at[q], lambda q: joined.at[q], a_s, a_r)
    cuts.start()
    swap = remote(outl, placed, swap_s.at[0], swap_r.at[0], swap_to())
    swap_back = remote(fl, swapped, swap_s.at[1], swap_r.at[1], swap_from())

    @pl.when(moves)
    def _():
        swap.start()

    joined[rank] = split[rank]
    length = jnp.sum(jnp.where(owners[...][None, :] == me, lengths[...][None, :], 0), axis=1, keepdims=True)
    live = iota((SEQ, 1), 0) < length
    live_grd[...] = jnp.where(live, grd[...].astype(F32), 0.0).astype(BF16)
    own_heads(heads_in, rank, head, skip)

    hidden = GroupGather(hall, hid, h_s, h_r)
    grads = GroupGather(gall, live_grd, g_s, g_r)
    first_w = PlaneGather(wx, lambda h: block.at[h], wx_s, wx_r, 2)
    gate_w = PlaneGather(wg, lambda h: gblock.at[h], wg_s, wg_r, 2)
    vecs = PlaneGather(praw, lambda h: params, p_s, p_r, 1)
    lines = PlaneGather(plane, lambda h: placed.at[h], l_s, l_r, 2)

    cuts.finish()
    hidden.start()
    row, col = iota((128, 128), 0), iota((128, 128), 1)
    member, line = col // 16, col % 16
    spot = jnp.where(line < KIN, member * KIN + line, 96 + member * 4 + line - KIN)
    both = dot(ones(spot == row), joined[...].reshape(128, COLS)).astype(BF16)
    for h in range(2):
        block[h] = both[48 * h : 48 * h + 48, 0:GA]
        gblock[h] = both[48 * h : 48 * h + 48, GA:COLS]
    params[...] = both[96:128, 0:384]
    vecs.start()
    first_w.start()
    wx[z, x] = block[...]
    wg[z, x] = gblock[...]
    praw[z, x, 0] = params[...]
    hall[y, c] = hid[...]
    gall[y, c] = live_grd[...]
    vecs.forward()
    first_w.forward()
    vecs.relay()
    first_w.relay()
    gate_w.start()

    @pl.when(moves)
    def _():
        swap.wait_recv()

    @pl.when(jnp.logical_not(moves))
    def _():
        placed[...] = outl[...]

    lines.start()
    plane[z, x] = placed[...]
    vecs.finish()
    unpack_params(praw, rank, c, par, step_rows)
    gate_w.forward()
    lines.forward()
    hidden.forward(1)
    hidden.forward(3)
    grads.start()
    first_w.finish()
    gate_w.relay()
    lines.relay()

    def chunk(i):
        return pl.ds(pl.multiple_of(i * 256, 256), 256)

    def in_turn(i):
        return (y + i + i // 2 * (5 - 2 * i)) % 4

    def vector_copy(i):
        here = act.at[c, chunk(in_turn(i))]
        return remote(here, here, v_s.at[i], v_r.at[i], sibling())

    def vector_arrival(i):
        here = act.at[1 - c, chunk(in_turn(i))]
        return remote(here, here, v_s.at[i], v_r.at[i], sibling())

    def forward(i, carry):
        @pl.when(i == 0)
        def _():
            hidden.arrived(0)

        @pl.when(i == 1)
        def _():
            hidden.arrived(1)

        @pl.when(i == 2)
        def _():
            hidden.arrived(3)
            hidden.forward(2)

        @pl.when(i == 3)
        def _():
            hidden.arrived(2)

        @pl.when(i < 4)
        def _():
            at = in_turn(i)
            for core in range(2):
                h = hall[at, core].astype(F32)
                scale = lax.rsqrt(jnp.mean(h * h, axis=1, keepdims=True) + EPSILON)
                rows = pl.ds(pl.multiple_of(at * 256 + core * SEQ, SEQ), SEQ)
                low[rows, :] = (h * scale * par[0:1, :]).astype(BF16)
            rows = chunk(at)
            proj[rows, 0:GA] = dot(low[rows, :], wx[...].reshape(D, GA))
            proj[rows, ST:] = dot_nt(low[rows, :], step_rows[...])
            for core in range(2):
                vector_forward(at * 2 + core, c, proj, act, par)
            vector_copy(i).start()

        @pl.when(i > 0)
        def _():
            vector_arrival(i - 1).wait_recv()
            at = in_turn(i - 1)
            for core in range(2):
                mix_forward(at * 2 + core, proj, act, par, head, skip, heads_out)

        return carry

    lax.fori_loop(0, 5, forward, 0)
    gate_w.finish()

    def project_gate(i, carry):
        proj[chunk(i), GA:COLS] = dot(low[chunk(i), :], wg[...].reshape(D, GW))
        return carry

    lax.fori_loop(0, ROWS // 256, project_gate, 0)
    grads.forward(1)
    grads.forward(3)
    lines.finish()
    unfold_out_weight(plane, ow)
    grads.arrived(0)

    def pull(i, carry):
        @pl.when(i == 1)
        def _():
            grads.arrived(1)

        @pl.when(i == 2)
        def _():
            grads.arrived(3)
            grads.forward(2)

        @pl.when(i == 3)
        def _():
            grads.arrived(2)

        at = in_turn(i)
        dgated[chunk(at), :] = dot_nt(gall[at].reshape(256, D), ow[...])
        return carry

    lax.fori_loop(0, 4, pull, 0)
    acc = lax.fori_loop(
        0, GROUP, lambda b, acc: norm_sums(b, proj, par, heads_out, dgated, acc), jnp.zeros((SEQ, SEQ), F32)
    )
    sums[...] = acc.T[0:16, :]
    norms = Members(lambda q: sums, lambda q: slots.at[q], n_s, n_r)
    norms.start()
    slots[rank] = sums[...]
    small[...] = jnp.zeros_like(small)
    norms.finish()
    total = slots[0]
    for q in range(1, GROUP):
        total = total + slots[q]
    wide[...] = jnp.concatenate([total, jnp.zeros((SEQ - 16, SEQ), F32)], axis=0).T

    def norms_back(b, carry):
        norm_back(b, proj, par, wide, heads_out, dgated, gated, dproj, small)
        return carry

    lax.fori_loop(0, GROUP, norms_back, 0)

    hidden.sent()
    branch = hall
    branches = GroupReduce(branch, gb, mb, lb, fb, b_s, b_r)
    lowers = GroupReduce(d_low, gd, md, ld, fd, d_s, d_r)
    sums_x = PlaneReduce(dwx, gx, mx, lx, fx, rx_s, rx_r)
    sums_g = PlaneReduce(dwg, gg, mg, lg, fg, rg_s, rg_r)
    sums_l = PlaneReduce(dow, gl, ml, ll, fl, rl_s, rl_r)
    sums_s = PlaneReduce(dws, gs, ms, ls, fs, rs_s, rs_r, 1)
    cut_rows = Members(lambda q: cut.at[q], lambda q: rows_in.at[q], rr_s, rr_r)
    gate_rows = Members(lambda q: gcut.at[q], lambda q: grows_in.at[q], rq_s, rq_r)
    all_small = Members(lambda q: small_all.at[rank], lambda q: small_all.at[q], sg_s, sg_r)

    def small_z(k):
        return remote(small, zs.at[z], sz_s.at[k], sz_r.at[k], on_z(k))

    def small_x(k):
        return remote(part, xs.at[x], sx_s.at[k], sx_r.at[k], on_x(k))

    def slab(k, span):
        at = (z + k) % 4
        own = low[:, pl.ds(pl.multiple_of(at * GW, GW), GW)]
        return at, dot_tn(own, dproj[:, span]).astype(BF16).reshape(4, 2, 48, span.stop - span.start)

    def out_term(i, carry):
        at = (y + 3 - i) % 4
        branch[at] = dot(gated[chunk(at), :], ow[...]).astype(BF16).reshape(2, SEQ, D)
        branches.across((3 - i) % 4).start()
        return carry

    lax.fori_loop(0, 4, out_term, 0)
    for k in (2, 1, 3, 0):
        at, rows = slab(k, slice(GA, COLS))
        dwg[at] = rows
        if k:
            sums_g.first(1, k).start()
    for k in (2, 1, 3):
        sums_g.first(0, k).start()
    out = dot_tn(gated[...], gall[...].reshape(ROWS, D))
    for j in range(16):
        piece = out[j * KOUT : (j + 1) * KOUT]
        tail = jnp.concatenate([piece[16:24, 0 : D // 2], piece[16:24, D // 2 :]], axis=0)
        fold = jnp.concatenate([piece[0:16], tail], axis=1).astype(BF16)
        for h in range(2):
            dow[j % 8 // 2, j // 8 * 2 + j % 2, h] = fold[:, h * WIDE : (h + 1) * WIDE]
    sums_l.start()

    def other_copy(i):
        rows = chunk((y + i + 1) % 4)
        return remote(d_other.at[rows], d_in.at[rows], u_s.at[i], u_r.at[i], sibling())

    def backward(i, carry):
        @pl.when(i < 4)
        def _():
            at = (y + i + 1) % 4
            for core in range(2):
                mix_back(at * 2 + core, c, proj, act, par, head, skip, dgated, dproj, d_steps, small, d_mine, d_other)
            other_copy(i).start()

        @pl.when(i == 0)
        def _():
            for k in (3, 2, 1):
                branches.pass_on(k)
            branches.keep()

        @pl.when(i == 1)
        def _():
            sums_g.middle()

        @pl.when(i == 2)
        def _():
            sums_l.middle()

        @pl.when(jnp.logical_and(i > 0, i < 5))
        def _():
            other_copy(i - 1).wait_recv()
            at = (y + i) % 4
            for core in range(2):
                vector_back(at * 2 + core, proj, par, d_mine, d_in, dproj, small)
            rows = chunk(at)
            back = dot_nt(dproj[rows, 0:GA], wx[...].reshape(D, GA))
            back = back + dot_nt(dproj[rows, GA:COLS], wg[...].reshape(D, GW))
            back = back + dot(d_steps[rows, :], step_rows[...])
            d_low[at] = back.astype(BF16).reshape(2, SEQ, D)
            lowers.across(i % 4).start()

        @pl.when(jnp.logical_and(i > 1, i < 5))
        def _():
            lowers.pass_on(i - 1)

        return carry

    lax.fori_loop(0, 5, backward, 0)
    for k in (1, 2, 3):
        small_z(k).start()
    zs[z] = small[...]
    for k in (2, 1, 3, 0):
        at, rows = slab(k, slice(0, GA))
        dwx[at] = rows
        if k:
            sums_x.first(1, k).start()
    for k in (2, 1, 3):
        sums_x.first(0, k).start()
    steps_back = dot_tn(d_steps[...], low[...])
    for r in range(16):
        own = jnp.concatenate([steps_back[0:16, r * 96 : (r + 1) * 96], jnp.zeros((16, 32), F32)], axis=1)
        dws[r // 4, r % 4, 0] = own.astype(BF16)
    sums_s.start()
    for k in (1, 2, 3):
        small_z(k).wait_recv()
    part[...] = ((zs[0] + zs[1]) + zs[2]) + zs[3]
    xs[x] = part[...]
    for k in (1, 2, 3):
        small_x(k).start()
    sums_x.middle()
    sums_s.middle()
    lowers.keep()
    sums_g.end()
    for q in range(GROUP):
        gcut[q] = jnp.zeros((16, GW), BF16)
        gcut[q, 0:KIN, :] = fg[q // 4, q % 4 * KIN : (q % 4 + 1) * KIN, :].astype(BF16)
    gate_rows.start()
    grows_in[rank] = gcut[rank]
    sums_l.end()

    @pl.when(moves)
    def _():
        swap_back.start()

    for k in (1, 2, 3):
        small_x(k).wait_recv()
    small_all[rank] = ((xs[0] + xs[1]) + xs[2]) + xs[3]
    all_small.start()
    branches.end()
    h32 = hid[...].astype(F32)
    mixed[...] = (h32 + jnp.where(live, fb[...], 0.0)).astype(BF16)
    sums_s.end()
    sums_x.end()
    step_cols = dot_tn(fs[0, 0:8], ones(iota((8, 128), 0) == iota((8, 128), 1), F32), HIGHEST)
    for q in range(GROUP):
        at = q % 4 * KIN
        cut[q] = jnp.zeros((16, CW + 128), BF16)
        cut[q, 0:KIN, 0:CW] = fx[q // 4, at : at + KIN, :].astype(BF16)
        cut[q, 0:KIN, CW:] = step_cols[q * KIN : (q + 1) * KIN].astype(BF16)
    cut_rows.start()
    rows_in[rank] = cut[rank]
    all_small.finish()
    finish_small(small_all, dvecs)

    @pl.when(moves)
    def _():
        swap_back.wait_recv()

    @pl.when(jnp.logical_not(moves))
    def _():
        swapped[...] = fl[...]

    doutw[0:16, 0:WIDE] = swapped[0]
    doutw[0:16, WIDE:D] = swapped[1, :, 0 : D - WIDE]
    doutw[16:24, 0 : D // 2] = swapped[1, 0:8, D - WIDE :]
    doutw[16:24, D // 2 : D] = swapped[1, 8:16, D - WIDE :]
    lowers.end()
    scale = lax.rsqrt(jnp.mean(h32 * h32, axis=1, keepdims=True) + EPSILON)
    normed = h32 * scale
    d_normed = fd[...] * par[0:1, :]
    through = scale * (d_normed - normed * jnp.mean(d_normed * normed, axis=1, keepdims=True))
    in_grad[...] = (grd[...].astype(F32) + through).astype(BF16)
    gate_rows.finish()
    cut_rows.finish()
    finish_rows(rows_in, grows_in, inw, vectors, dinw, dvecs)
    for gone in (grads, first_w, gate_w, vecs, lines, cuts, norms, cut_rows, gate_rows, all_small):
        gone.sent()
    for gone in (branches, lowers, sums_x, sums_g, sums_l, sums_s):
        gone.finish()
    for k in (1, 2, 3):
        small_z(k).wait_send()
        small_x(k).wait_send()
    for i in range(4):
        vector_copy(i).wait_send()
        other_copy(i).wait_send()

    @pl.when(moves)
    def _():
        swap.wait_send()
        swap_back.wait_send()


def finish_small(small, dvecs):
    me = lax.axis_index("fsdp")
    conv = jnp.zeros((8, 128), F32)
    inner = jnp.zeros((8, 128), F32)
    common = [jnp.zeros((8, 128), F32), jnp.zeros((8, 128), F32)]
    row, col = iota((GW, 128), 0), iota((GW, 128), 1)
    heads = ones(row // 64 == col, F32)
    dvecs[...] = jnp.zeros_like(dvecs)
    for q in range(GROUP):
        part = small[q, :, 0:GW]
        conv = conv + dot(part, ones(row + q * GW == col + 26 * me, F32), HIGHEST)
        inner = inner + dot(part, ones(row + q * GW == col + KOUT * me, F32), HIGHEST)
        common[q % 2] = common[q % 2] + small[q, :, GW:CW]
        span = slice(q * OWN, (q + 1) * OWN)
        dvecs[3:4, span] = small[q, 7:8, 0:OWN]
        dvecs[4:5, span] = small[q, 7:8, 128 : 128 + OWN]
        dvecs[5:6, span] = dot(part, heads, HIGHEST)[6:7, 0:OWN]
    row, col = iota((256, 128), 0), iota((256, 128), 1)
    conv = conv + dot(jnp.concatenate(common, axis=1), ones(row + INNER == col + 26 * me, F32), HIGHEST)
    dvecs[1:2] = conv[4:5]
    dvecs[2:3] = inner[5:6]
    dvecs[8:12] = conv[0:4]


def finish_rows(rows, gate_rows, inw, vectors, dinw, dvecs):
    shared = [jnp.zeros((KIN, 128), F32), jnp.zeros((KIN, 128), F32)]
    for q in range(GROUP):
        own = rows[q].astype(F32)[0:KIN]
        dinw[:, INNER + q * GW : INNER + (q + 1) * GW] = own[:, 0:GW]
        dinw[:, q * GW : (q + 1) * GW] = gate_rows[q].astype(F32)[0:KIN]
        dinw[:, STEP + q * OWN : STEP + (q + 1) * OWN] = own[:, CW : CW + OWN]
        shared[q % 2] = shared[q % 2] + own[:, GW:CW]
    dinw[:, 2 * INNER : 2 * INNER + 128] = shared[0]
    dinw[:, 2 * INNER + 128 : STEP] = shared[1]
    total = jnp.sum(dinw[...] * inw[...].astype(F32), axis=1, keepdims=True)
    spread = jnp.where(iota((KIN, 128), 0) == iota((KIN, 128), 1), total, 0.0)
    gain = jnp.where(iota((1, 128), 1) < KIN, vectors[0:1], 1.0)
    dvecs[0:1] = jnp.sum(spread, axis=0, keepdims=True) / gain


def emit_kernel(mixed, in_grad, dinw, doutw, dvecs, *outs):
    (mixed_out, grad_out, dinw_out, dgain, conv_out, dbias, ddt, da_log, dskip, dinner, doutw_out) = outs
    for given, out in ((mixed, mixed_out), (in_grad, grad_out), (dinw, dinw_out), (doutw, doutw_out)):
        out[...] = given[...]
    for i, line in enumerate((dgain, dbias, dinner, ddt, da_log, dskip)):
        line[...] = dvecs[i, 0 : line.shape[0]]
    conv_out[...] = dvecs[8:12, 0:26]


def emit(*given):
    vmem = pl.BlockSpec(memory_space=pltpu.VMEM)
    shape = jax.ShapeDtypeStruct
    line = [shape((n,), F32) for n in (KIN, 26, HEADS, HEADS, HEADS, KOUT)]
    return pl.pallas_call(
        emit_kernel,
        name="emit",
        out_shape=(*OUT_SHAPES[0:3], line[0], shape((4, 26), F32), *line[1:], OUT_SHAPES[4]),
        in_specs=[vmem] * 5,
        out_specs=(vmem,) * 11,
        compiler_params=pltpu.CompilerParams(vmem_limit_bytes=VMEM_LIMIT),
    )(*given)


def layer(*given):
    vmem, vm = pl.BlockSpec(memory_space=pltpu.VMEM), pltpu.VMEM

    def dma(*dims):
        return pltpu.SemaphoreType.DMA(dims)

    def plane_reduce(halves, rows, cols):
        block = (rows, cols)
        return [
            vm((halves, 3, 4) + block, BF16), vm((halves, 3) + block, BF16), vm((halves, 3) + block, BF16),
            vm((halves,) + block, F32),
        ]

    seven, pair, four = [dma(GROUP)] * 2, [dma(2, 4)] * 2, [dma(4)] * 2
    group_reduce = [vm((4, SEQ, D), BF16), vm((3, SEQ, D), BF16), vm((3, SEQ, D), BF16), vm((SEQ, D), F32)]
    gather = [dma(2, 5, 4), dma(2, 4, 4)]
    return pl.pallas_call(
        layer_kernel,
        name="layer",
        out_shape=OUT_SHAPES,
        in_specs=[vmem] * len(given),
        out_specs=(vmem,) * len(OUT_SHAPES),
        scratch_shapes=[
            vm((8, 128), F32), vm((8, 128), F32), vm((8, 128), F32),
            vm((GROUP, 16, COLS), BF16), vm((GROUP, 16, COLS), BF16), vm((2, 48, GA), BF16), vm((2, 48, GW), BF16),
            vm((32, 384), BF16), vm((2, 16, WIDE), BF16), vm((2, 16, WIDE), BF16), vm((SEQ, D), BF16),
            vm((4, 4, 2, 48, GA), BF16), vm((4, 4, 2, 48, GW), BF16), vm((4, 4, 1, 32, 384), BF16),
            vm((4, 4, 2, 16, WIDE), BF16), vm((4, 2, SEQ, D), BF16), vm((4, 2, SEQ, D), BF16),
            vm((ROWS, D), BF16), vm((ROWS, COLS + 128), F32), vm((2, ROWS, 128), F32), vm((128, D), BF16),
            vm((ROWS, GW), F32), vm((ROWS, GW), F32), vm((GW, D), BF16),
            vm((8, D), F32), vm((8, 128), F32), vm((1, GW), F32),
            vm((16, SEQ), F32), vm((GROUP, 16, SEQ), F32), vm((SEQ, SEQ), F32),
            vm((ROWS, GW), BF16), vm((ROWS, COLS), BF16), vm((ROWS, 128), BF16),
            vm((ROWS, 128), F32), vm((ROWS, 128), F32), vm((ROWS, 128), F32), vm((4, 2, SEQ, D), BF16),
            vm((4, 4, 2, 48, GA), BF16), vm((4, 4, 2, 48, GW), BF16), vm((4, 4, 2, 16, WIDE), BF16),
            vm((4, 4, 1, 16, 128), BF16), vm((8, CW), F32),
            *group_reduce, *group_reduce, *plane_reduce(2, 48, GA), *plane_reduce(2, 48, GW),
            *plane_reduce(2, 16, WIDE), *plane_reduce(1, 16, 128),
            vm((2, 16, WIDE), F32), vm((GROUP, 16, CW + 128), BF16), vm((GROUP, 16, CW + 128), BF16),
            vm((GROUP, 16, GW), BF16), vm((GROUP, 16, GW), BF16),
            vm((4, 8, CW), F32), vm((4, 8, CW), F32), vm((8, CW), F32), vm((GROUP, 8, CW), F32),
            *seven, *gather, *gather, dma(1, 5, 4), dma(1, 4, 4), *gather,
            *pair, *pair, *seven, *four, *four,
            *pair, *pair, *[dma(2, 2, 4)] * 6, *[dma(1, 2, 4)] * 2, *seven, *seven,
            *four, *four, *seven, dma(2), dma(2),
        ],
        compiler_params=pltpu.CompilerParams(collective_id=0, has_side_effects=True, vmem_limit_bytes=VMEM_LIMIT),
    )(*given)


OUT_SHAPES = (
    jax.ShapeDtypeStruct((SEQ, D), BF16),
    jax.ShapeDtypeStruct((SEQ, D), BF16),
    jax.ShapeDtypeStruct((KIN, STEP + HEADS), F32),
    jax.ShapeDtypeStruct((16, 128), F32),
    jax.ShapeDtypeStruct((KOUT, D), F32),
)


def body(
    hidden, in_weight, norm_gain, conv_weight, conv_bias, dt_bias, a_log, skip, inner_gain, out_weight, out_grad,
    seq_lengths, seq_owner,
):
    mixed, in_grad, dinw, dvecs, doutw = layer(
        hidden, in_weight, norm_gain, conv_weight.T, conv_bias, dt_bias, a_log, skip, inner_gain, out_weight, out_grad,
        seq_lengths, seq_owner,
    )
    outs = list(emit(mixed, in_grad, dinw, doutw, dvecs))
    outs[4] = outs[4].T
    return tuple(outs)


def solution(mesh):
    rows, line, whole = P("fsdp", None), P("fsdp"), P()
    return jax.shard_map(
        body,
        mesh=mesh,
        in_specs=(rows, rows, line, rows, line, whole, whole, whole, line, rows, rows, whole, whole),
        out_specs=(rows, rows, rows, line, rows, line, whole, whole, whole, line, rows),
        check_vma=False,
    )
```

time: 173 us -> 138 us (0.80)
  Pallas kernels: 159 us -> 137 us
  local copies, waits for them, and re-layouts: 9.55 us -> 0 us
  other arithmetic: 2.52 us -> 0 us
    pallas_call x1, Pallas kernels: 159 us -> 134 us  [layer(): pl.pallas_call(layer_kernel, name='layer', out_shape=OUT_SHAPES, in_specs...]
    unnamed x30 -> x0, local copies, waits for them, and re-layouts: 6.85 us -> none
    pallas_call x0 -> x1, Pallas kernels: none -> 2.42 us  [emit(): pl.pallas_call(emit_kernel, name='emit', out_shape=(*OUT_SHAPES[0:3], lin...]
where the time goes in v3:
time: 138 us; the launch traced here: 137 us
  Pallas kernels  137 us (99%)
    pallas_call x1, Pallas kernels, layer(): pl.pallas_call(layer_kernel, name='layer', out_shape=OUT_SHAPES, in_specs...  134 us

profile of v3, /device:TPU:1, one launch (start us, length us, event | category | flops | bytes accessed | tf_op | source)
XLA Modules:
  0.0 137.4 jit_solution(5144284384460038101)
XLA Ops:
  0.6 134.1 %layer.1 = (bf16[128,1536]{1,0:T(8,128)(2,1)}, bf16[128,1536]{1,0:T(8,128)(2,1)}, f32[12,6448]{1,0:T(8,128)}, f32[16,128]{1,0:T(8,128)}, f32[24,1536]{1,0:T(8,128)}) custom-call(bf16[128,1536]{1,0:T(8,128)(2,1)} %hid.1, bf16[12,6448]{1,0:T(8,128)(2,1)} %inw.1, bf16[12]{0:T(256)(128)(2,1)} %gain_in.1, bf16[4,26]{1,0:T(4,128)(2,1)} %bitcast.2, ...), custom_call_target="tpu_custom_call" | custom-call | tf_op jit(solution)/shard_map/layer/pallas_call | solution.py:1096
  134.8 2.4 %emit.1 = (bf16[128,1536]{1,0:T(8,128)(2,1)}, bf16[128,1536]{1,0:T(8,128)(2,1)}, f32[12,6448]{1,0:T(8,128)}, f32[12]{0:T(128)}, f32[4,26]{1,0:T(4,128)}, /*index...) custom-call(bf16[128,1536]{1,0:T(8,128)(2,1)} %get-tuple-element.27.mixed, ...), custom_call_target="tpu_custom_call" | custom-call | tf_op jit(solution)/shard_map/emit/pallas_call | solution.py:1070

commit v4 on v3

--- a/solution.py
+++ b/solution.py
@@ -147,25 +147,32 @@
     def along(self, half, stage, k):
         return on_z(k) if (half == 0) == (stage == 0) else on_x(k)
 
+    def came(self, first):
+        return 3 if first < 2 else 1
+
+    def mark(self, half, first, second):
+        if second == 0:
+            return self.recv.at[half, first - 1]
+        return self.recv.at[half, 3 + first if second == self.came(first) else 7]
+
     def copy(self, half, first, stage, k):
         src = self.own(half) if first == 0 else self.slot(half, first, 0)
         at = (4 - k, 0) if stage == 0 else (first, 4 - k)
         return remote(
-            src,
-            self.slot(half, first, 0),
-            self.send.at[half, first if stage else 4, k],
-            self.recv.at[half, at[0], at[1]],
-            self.along(half, stage, k),
+            src, self.slot(half, first, 0), self.send.at[half, stage], self.mark(half, *at), self.along(half, stage, k)
         )
 
     def relayed(self, half, first):
-        came, k = (3, 1) if first < 2 else (1, 3)
+        came = self.came(first)
         here = self.slot(half, first, came)
-        return remote(here, here, self.send.at[half, first, 2], self.recv.at[half, first, 2], self.along(half, 1, k))
+        return remote(here, here, self.send.at[half, 1], self.mark(half, first, 2), self.along(half, 1, 4 - came))
 
     def arrival(self, half, first, second):
         here = self.slot(half, first, second)
-        return remote(here, here, self.send.at[half, 4, 0], self.recv.at[half, first, second], on_z(1))
+        return remote(here, here, self.send.at[half, 0], self.mark(half, first, second), on_z(1))
+
+    def some(self, rows, count, half):
+        return self.buf.at[pl.ds(0, rows), pl.ds(0, count), half]
 
     def start(self):
         for k in (1, 3, 2):
@@ -185,25 +192,18 @@
     def relay(self):
         for first in (0, 3, 1, 2):
             for half in range(self.halves):
-                self.arrival(half, first, 3 if first < 2 else 1).wait_recv()
+                self.arrival(half, first, self.came(first)).wait_recv()
                 self.relayed(half, first).start()
 
     def finish(self):
-        for first in range(4):
-            for half in range(self.halves):
-                self.arrival(half, first, 1 if first < 2 else 3).wait_recv()
-        for first in range(4):
-            for half in range(self.halves):
-                self.arrival(half, first, 2).wait_recv()
+        for half in range(self.halves):
+            here = self.some(4, 2, half)
+            remote(here, here, self.send.at[half, 0], self.recv.at[half, 7], on_z(1)).wait_recv()
 
     def sent(self):
         for half in range(self.halves):
-            for k in (1, 2, 3):
-                self.copy(half, 0, 0, k).wait_send()
-            for first in range(4):
-                for k in (1, 3):
-                    self.copy(half, first, 1, k).wait_send()
-                self.relayed(half, first).wait_send()
+            for stage, here in ((0, self.some(1, 3, half)), (1, self.some(4, 3, half))):
+                remote(here, here, self.send.at[half, stage], self.recv.at[half, 7], on_z(1)).wait_send()
 
 
 class GroupGather:
@@ -212,20 +212,19 @@
         _, _, self.y, self.c = place()
 
     def along(self, k):
-        return remote(self.own, self.buf.at[self.y, self.c], self.send.at[0, k], self.recv.at[0, 4 - k], on_y(k))
+        return remote(self.own, self.buf.at[self.y, self.c], self.send.at[0], self.recv.at[4 - k], on_y(k))
 
     def half(self, k):
         return pl.ds(0, SEQ // 2) if k == 3 else pl.ds(SEQ // 2, SEQ // 2)
 
     def relayed(self, k):
         here = self.buf.at[(self.y + k) % 4, self.c, self.half(k)]
-        at = 2 if k == 3 else 0
-        return remote(here, here, self.send.at[0, at], self.recv.at[0, at], on_y(4 - k))
+        return remote(here, here, self.send.at[0], self.recv.at[2], on_y(4 - k))
 
     def across(self, k):
         src = self.own if k == 0 else self.buf.at[(self.y + k) % 4, self.c]
         dst = self.buf.at[(self.y + k) % 4, self.c]
-        return remote(src, dst, self.send.at[1, k], self.recv.at[1, k], sibling())
+        return remote(src, dst, self.send.at[1], self.recv.at[4 + k], sibling())
 
     def start(self):
         for k in (1, 3):
@@ -233,27 +232,19 @@
         self.across(0).start()
 
     def forward(self, k):
-        if k == 2:
-            for came in (3, 1):
-                here = self.buf.at[(self.y + 2) % 4, self.c, self.half(came)]
-                at = 2 if came == 3 else 0
-                remote(here, here, self.send.at[0, at], self.recv.at[0, at], sibling()).wait_recv()
-        else:
-            here = self.buf.at[(self.y + k) % 4, self.c]
-            remote(here, here, self.send.at[0, k], self.recv.at[0, k], sibling()).wait_recv()
+        here = self.buf.at[(self.y + k) % 4, self.c]
+        remote(here, here, self.send.at[0], self.recv.at[k], sibling()).wait_recv()
+        if k != 2:
             self.relayed(k).start()
         self.across(k).start()
 
     def arrived(self, k):
         here = self.buf.at[(self.y + k) % 4, 1 - self.c]
-        remote(here, here, self.send.at[1, k], self.recv.at[1, k], sibling()).wait_recv()
+        remote(here, here, self.send.at[0], self.recv.at[4 + k], sibling()).wait_recv()
 
     def sent(self):
-        for k in (1, 3):
-            self.along(k).wait_send()
-            self.relayed(k).wait_send()
-        for k in range(4):
-            self.across(k).wait_send()
+        for at, here in ((0, self.buf.at[pl.ds(0, 3), 0]), (1, self.buf.at[:, 0])):
+            remote(here, here, self.send.at[at], self.recv.at[0], sibling()).wait_send()
 
 
 def unpack_params(raw, rank, core, par, step_rows):
@@ -353,6 +344,16 @@
         heads_out[rows, at : at + 128] = jnp.where(col < 64, parts[0], parts[1]) + skip[0:1, at : at + 128] * values
 
 
+def weigh(b, proj, par, heads_out, gated):
+    rows = pl.ds(pl.multiple_of(b * SEQ, SEQ), SEQ)
+    gate = proj[rows, GA:COLS]
+    gated[rows, :] = (heads_out[rows, :] * gate * sigmoid(gate) * par[6:7, 0:GW]).astype(BF16)
+
+
+def column(at, values):
+    return jnp.sum(jnp.where(iota((SEQ, SEQ), 1) == at, values, 0.0), axis=1, keepdims=True)
+
+
 def norm_sums(b, proj, par, heads_out, dgated, acc):
     rows = pl.ds(pl.multiple_of(b * SEQ, SEQ), SEQ)
     gate = proj[rows, GA:COLS]
@@ -365,10 +366,8 @@
 
 def norm_back(b, proj, par, wide, heads_out, dgated, gated, dproj, small):
     rows = pl.ds(pl.multiple_of(b * SEQ, SEQ), SEQ)
-    col = iota((SEQ, SEQ), 1)
-    square = jnp.sum(jnp.where(col == b, wide[...], 0.0), axis=1, keepdims=True)
-    cross = jnp.sum(jnp.where(col == b + 8, wide[...], 0.0), axis=1, keepdims=True)
-    inverse = lax.rsqrt(square * (1.0 / INNER) + EPSILON)
+    cross = column(b + 8, wide[...])
+    inverse = lax.rsqrt(column(b, wide[...]) * (1.0 / INNER) + EPSILON)
     mean = cross * inverse * (1.0 / INNER)
     out = heads_out[rows, :]
     gate = proj[rows, GA:COLS]
@@ -476,21 +475,23 @@
 
     def first(self, half, k):
         target = on_x(k) if half == 0 else on_z(k)
-        return remote(self.line(half, k), self.got.at[half, k - 1], self.send.at[half, 0, k], self.recv.at[half, 0, k], target)
+        return remote(self.line(half, k), self.got.at[half, k - 1], self.send.at[half, 0], self.recv.at[half, 0], target)
 
     def second(self, half, k):
         target = on_z(k) if half == 0 else on_x(k)
-        return remote(self.mid.at[half, k - 1], self.last.at[half, k - 1], self.send.at[half, 1, k], self.recv.at[half, 1, k], target)
+        return remote(self.mid.at[half, k - 1], self.last.at[half, k - 1], self.send.at[half, 1], self.recv.at[half, 1], target)
+
+    def stage(self, half, at, like):
+        return remote(like.at[half], like.at[half], self.send.at[half, at], self.recv.at[half, at], on_z(1))
 
     def start(self):
         for k in (2, 1, 3):
-            for half in range(self.halves):
+            for half in reversed(range(self.halves)):
                 self.first(half, k).start()
 
     def middle(self):
-        for half in range(self.halves):
-            for k in (1, 2, 3):
-                self.first(half, k).wait_recv()
+        for half in reversed(range(self.halves)):
+            self.stage(half, 0, self.got).wait_recv()
             for k in (2, 1, 3, 0):
                 if half == 0:
                     at = (self.z + k) % 4
@@ -507,85 +508,93 @@
                     self.out[half] = total
 
     def end(self):
-        for half in range(self.halves):
-            for k in (1, 2, 3):
-                self.second(half, k).wait_recv()
+        for half in reversed(range(self.halves)):
+            self.stage(half, 1, self.last).wait_recv()
             total = self.out[half]
             for j in range(3):
                 total = total + self.last[half, j].astype(F32)
             self.out[half] = total
 
     def finish(self):
-        for half in range(self.halves):
-            for k in (1, 2, 3):
-                self.first(half, k).wait_send()
-                self.second(half, k).wait_send()
+        for half in reversed(range(self.halves)):
+            self.stage(half, 0, self.got).wait_send()
+            self.stage(half, 1, self.mid).wait_send()
 
 
 class GroupReduce:
-    def __init__(self, terms, got, mid, last, out, send, recv):
-        self.terms, self.got, self.mid, self.last, self.out = terms, got, mid, last, out
+    def __init__(self, terms, got, mid, relay, last, out, send, recv):
+        self.terms, self.got, self.mid, self.relay, self.last, self.out = terms, got, mid, relay, last, out
         self.send, self.recv = send, recv
         _, _, self.y, self.c = place()
 
     def across(self, k):
         src = self.terms.at[(self.y + k) % 4, 1 - self.c]
-        return remote(src, self.got.at[k], self.send.at[0, k], self.recv.at[0, k], sibling())
+        return remote(src, self.got.at[k], self.send.at[0], self.recv.at[k], sibling())
 
     def along(self, k):
-        return remote(self.mid.at[k - 1], self.last.at[k - 1], self.send.at[1, k], self.recv.at[1, k], on_y(k))
+        at = (k - 1) // 2
+        return remote(self.mid.at[k - 1], self.last.at[at], self.send.at[1], self.recv.at[6], on_y(k))
+
+    def far(self, at):
+        src = self.mid.at[1, pl.ds(at * (SEQ // 2), SEQ // 2)]
+        return remote(src, self.relay.at[at], self.send.at[1], self.recv.at[4 + at], on_y(3 if at else 1))
 
     def half(self, k):
         self.across(k).wait_recv()
         return self.terms[(self.y + k) % 4, self.c].astype(F32) + self.got[k].astype(F32)
 
+    def pass_far(self):
+        self.mid[1] = self.half(2).astype(BF16)
+        for at in range(2):
+            self.far(at).start()
+
     def pass_on(self, k):
-        self.mid[k - 1] = self.half(k).astype(BF16)
+        at = (k - 1) // 2
+        total = self.half(k)
+        self.far(at).wait_recv()
+        came = self.relay[at].astype(F32)
+        upper, lower = total[0 : SEQ // 2], total[SEQ // 2 :]
+        if at == 0:
+            upper = upper + came
+        else:
+            lower = lower + came
+        self.mid[k - 1, 0 : SEQ // 2] = upper.astype(BF16)
+        self.mid[k - 1, SEQ // 2 :] = lower.astype(BF16)
         self.along(k).start()
 
     def keep(self):
         self.out[...] = self.half(0)
 
     def end(self):
-        for k in (1, 2, 3):
-            self.along(k).wait_recv()
         total = self.out[...]
-        for j in range(3):
-            total = total + self.last[j].astype(F32)
-        self.out[...] = total
+        remote(self.last, self.last, self.send.at[1], self.recv.at[6], sibling()).wait_recv()
+        self.out[...] = total + self.last[0].astype(F32) + self.last[1].astype(F32)
 
     def finish(self):
-        for k in range(4):
-            self.across(k).wait_send()
-            if k:
-                self.along(k).wait_send()
+        for at, here in ((0, self.got), (1, self.mid)):
+            remote(here, here, self.send.at[at], self.recv.at[6], sibling()).wait_send()
 
 
 class Members:
-    def __init__(self, src, dst, send, recv):
-        self.src, self.dst, self.send, self.recv = src, dst, send, recv
+    def __init__(self, src, buf, send, recv):
+        self.src, self.buf, self.send, self.recv = src, buf, send.at[0], recv.at[0]
         _, _, y, c = place()
         self.rank = y * 2 + c
 
-    def copy(self, k):
-        target, q = group_partner(k)
-        return remote(self.src(q), self.dst(self.rank), self.send.at[k], self.recv.at[k], target)
-
-    def arrival(self, k):
-        _, q = group_partner(k)
-        return remote(self.dst(q), self.dst(q), self.send.at[k], self.recv.at[GROUP - k], sibling())
-
     def start(self):
         for k in range(1, GROUP):
-            self.copy(k).start()
+            target, q = group_partner(k)
+            remote(self.src(q), self.buf.at[self.rank], self.send, self.recv, target).start()
+
+    def others(self):
+        here = self.buf.at[pl.ds(0, GROUP - 1)]
+        return remote(here, here, self.send, self.recv, sibling())
 
     def finish(self):
-        for k in range(1, GROUP):
-            self.arrival(k).wait_recv()
+        self.others().wait_recv()
 
     def sent(self):
-        for k in range(1, GROUP):
-            self.copy(k).wait_send()
+        self.others().wait_send()
 
 
 def layer_kernel(
@@ -595,7 +604,7 @@
     split, joined, block, gblock, params, outl, placed, live_grd,
     wx, wg, praw, plane, hall, gall, low, proj, act, step_rows, heads_out, dgated, ow, par, head, skip, sums, slots, wide,
     gated, dproj, d_steps, d_mine, d_other, d_in, d_low, dwx, dwg, dow, dws, small,
-    gb, mb, lb, fb, gd, md, ld, fd, gx, mx, lx, fx, gg, mg, lg, fg, gl, ml, ll, fl, gs, ms, ls, fs,
+    gb, mb, tb, lb, fb, gd, md, td, ld, fd, gx, mx, lx, fx, gg, mg, lg, fg, gl, ml, ll, fl, gs, ms, ls, fs,
     swapped, cut, rows_in, gcut, grows_in, zs, xs, part, small_all,
     a_s, a_r, wx_s, wx_r, wg_s, wg_r, p_s, p_r, l_s, l_r, h_s, h_r, g_s, g_r, n_s, n_r, v_s, v_r, u_s, u_r,
     b_s, b_r, d_s, d_r, rx_s, rx_r, rg_s, rg_r, rl_s, rl_r, rs_s, rs_r, rr_s, rr_r, rq_s, rq_r,
@@ -653,7 +662,7 @@
     def _():
         pl.semaphore_wait(pltpu.get_barrier_semaphore(), len(partners))
 
-    cuts = Members(lambda q: split.at[q], lambda q: joined.at[q], a_s, a_r)
+    cuts = Members(lambda q: split.at[q], joined, a_s, a_r)
     cuts.start()
     swap = remote(outl, placed, swap_s.at[0], swap_r.at[0], swap_to())
     swap_back = remote(fl, swapped, swap_s.at[1], swap_r.at[1], swap_from())
@@ -675,8 +684,8 @@
     vecs = PlaneGather(praw, lambda h: params, p_s, p_r, 1)
     lines = PlaneGather(plane, lambda h: placed.at[h], l_s, l_r, 2)
 
+    hidden.start()
     cuts.finish()
-    hidden.start()
     row, col = iota((128, 128), 0), iota((128, 128), 1)
     member, line = col // 16, col % 16
     spot = jnp.where(line < KIN, member * KIN + line, 96 + member * 4 + line - KIN)
@@ -694,8 +703,6 @@
     gall[y, c] = live_grd[...]
     vecs.forward()
     first_w.forward()
-    vecs.relay()
-    first_w.relay()
     gate_w.start()
 
     @pl.when(moves)
@@ -708,30 +715,33 @@
 
     lines.start()
     plane[z, x] = placed[...]
+    hidden.forward(1)
+    hidden.forward(3)
+    grads.start()
+    vecs.relay()
+    first_w.relay()
     vecs.finish()
     unpack_params(praw, rank, c, par, step_rows)
     gate_w.forward()
     lines.forward()
-    hidden.forward(1)
-    hidden.forward(3)
-    grads.start()
     first_w.finish()
-    gate_w.relay()
-    lines.relay()
 
     def chunk(i):
         return pl.ds(pl.multiple_of(i * 256, 256), 256)
 
+    def turn(i):
+        return i + i // 2 * (5 - 2 * i)
+
     def in_turn(i):
-        return (y + i + i // 2 * (5 - 2 * i)) % 4
+        return (y + turn(i)) % 4
 
     def vector_copy(i):
         here = act.at[c, chunk(in_turn(i))]
-        return remote(here, here, v_s.at[i], v_r.at[i], sibling())
+        return remote(here, here, v_s.at[0], v_r.at[i], sibling())
 
     def vector_arrival(i):
         here = act.at[1 - c, chunk(in_turn(i))]
-        return remote(here, here, v_s.at[i], v_r.at[i], sibling())
+        return remote(here, here, v_s.at[0], v_r.at[i], sibling())
 
     def forward(i, carry):
         @pl.when(i == 0)
@@ -741,15 +751,22 @@
         @pl.when(i == 1)
         def _():
             hidden.arrived(1)
+            hidden.forward(2)
 
         @pl.when(i == 2)
         def _():
             hidden.arrived(3)
-            hidden.forward(2)
+            gate_w.relay()
 
         @pl.when(i == 3)
         def _():
             hidden.arrived(2)
+            lines.relay()
+
+        @pl.when(i == 4)
+        def _():
+            grads.forward(1)
+            grads.forward(3)
 
         @pl.when(i < 4)
         def _():
@@ -783,10 +800,26 @@
         return carry
 
     lax.fori_loop(0, ROWS // 256, project_gate, 0)
-    grads.forward(1)
-    grads.forward(3)
+
+    def weighed(b, carry):
+        weigh(b, proj, par, heads_out, gated)
+        return carry
+
+    lax.fori_loop(0, GROUP, weighed, 0)
     lines.finish()
     unfold_out_weight(plane, ow)
+    hidden.sent()
+    branch = hall
+    branches = GroupReduce(branch, gb, mb, tb, lb, fb, b_s, b_r)
+
+    def out_term(i, carry):
+        at = in_turn(3 - i)
+        branch[at] = dot(gated[chunk(at), :], ow[...]).astype(BF16).reshape(2, SEQ, D)
+        branches.across(turn(3 - i)).start()
+        return carry
+
+    lax.fori_loop(0, 4, out_term, 0)
+    grads.forward(2)
     grads.arrived(0)
 
     def pull(i, carry):
@@ -797,7 +830,6 @@
         @pl.when(i == 2)
         def _():
             grads.arrived(3)
-            grads.forward(2)
 
         @pl.when(i == 3)
         def _():
@@ -812,10 +844,11 @@
         0, GROUP, lambda b, acc: norm_sums(b, proj, par, heads_out, dgated, acc), jnp.zeros((SEQ, SEQ), F32)
     )
     sums[...] = acc.T[0:16, :]
-    norms = Members(lambda q: sums, lambda q: slots.at[q], n_s, n_r)
+    norms = Members(lambda q: sums, slots, n_s, n_r)
     norms.start()
     slots[rank] = sums[...]
     small[...] = jnp.zeros_like(small)
+    branches.pass_far()
     norms.finish()
     total = slots[0]
     for q in range(1, GROUP):
@@ -828,36 +861,31 @@
 
     lax.fori_loop(0, GROUP, norms_back, 0)
 
-    hidden.sent()
-    branch = hall
-    branches = GroupReduce(branch, gb, mb, lb, fb, b_s, b_r)
-    lowers = GroupReduce(d_low, gd, md, ld, fd, d_s, d_r)
+    lowers = GroupReduce(d_low, gd, md, td, ld, fd, d_s, d_r)
     sums_x = PlaneReduce(dwx, gx, mx, lx, fx, rx_s, rx_r)
     sums_g = PlaneReduce(dwg, gg, mg, lg, fg, rg_s, rg_r)
     sums_l = PlaneReduce(dow, gl, ml, ll, fl, rl_s, rl_r)
     sums_s = PlaneReduce(dws, gs, ms, ls, fs, rs_s, rs_r, 1)
-    cut_rows = Members(lambda q: cut.at[q], lambda q: rows_in.at[q], rr_s, rr_r)
-    gate_rows = Members(lambda q: gcut.at[q], lambda q: grows_in.at[q], rq_s, rq_r)
-    all_small = Members(lambda q: small_all.at[rank], lambda q: small_all.at[q], sg_s, sg_r)
+    cut_rows = Members(lambda q: cut.at[q], rows_in, rr_s, rr_r)
+    gate_rows = Members(lambda q: gcut.at[q], grows_in, rq_s, rq_r)
+    all_small = Members(lambda q: small_all.at[rank], small_all, sg_s, sg_r)
 
     def small_z(k):
-        return remote(small, zs.at[z], sz_s.at[k], sz_r.at[k], on_z(k))
+        return remote(small, zs.at[z], sz_s.at[0], sz_r.at[0], on_z(k))
 
     def small_x(k):
-        return remote(part, xs.at[x], sx_s.at[k], sx_r.at[k], on_x(k))
+        return remote(part, xs.at[x], sx_s.at[0], sx_r.at[0], on_x(k))
+
+    def small_all_of(buf, send, recv):
+        here = buf.at[pl.ds(0, 3)]
+        return remote(here, here, send.at[0], recv.at[0], on_z(1))
+
 
     def slab(k, span):
         at = (z + k) % 4
         own = low[:, pl.ds(pl.multiple_of(at * GW, GW), GW)]
         return at, dot_tn(own, dproj[:, span]).astype(BF16).reshape(4, 2, 48, span.stop - span.start)
 
-    def out_term(i, carry):
-        at = (y + 3 - i) % 4
-        branch[at] = dot(gated[chunk(at), :], ow[...]).astype(BF16).reshape(2, SEQ, D)
-        branches.across((3 - i) % 4).start()
-        return carry
-
-    lax.fori_loop(0, 4, out_term, 0)
     for k in (2, 1, 3, 0):
         at, rows = slab(k, slice(GA, COLS))
         dwg[at] = rows
@@ -875,47 +903,58 @@
     sums_l.start()
 
     def other_copy(i):
-        rows = chunk((y + i + 1) % 4)
-        return remote(d_other.at[rows], d_in.at[rows], u_s.at[i], u_r.at[i], sibling())
+        rows = chunk(in_turn(3 - i))
+        return remote(d_other.at[rows], d_in.at[rows], u_s.at[0], u_r.at[i], sibling())
+
+    def lower_back(k):
+        at = (y + k) % 4
+        rows = chunk(at)
+        back = dot_nt(dproj[rows, 0:GA], wx[...].reshape(D, GA))
+        back = back + dot_nt(dproj[rows, GA:COLS], wg[...].reshape(D, GW))
+        back = back + dot(d_steps[rows, :], step_rows[...])
+        d_low[at] = back.astype(BF16).reshape(2, SEQ, D)
+        lowers.across(k).start()
 
     def backward(i, carry):
         @pl.when(i < 4)
         def _():
-            at = (y + i + 1) % 4
+            at = in_turn(3 - i)
             for core in range(2):
                 mix_back(at * 2 + core, c, proj, act, par, head, skip, dgated, dproj, d_steps, small, d_mine, d_other)
             other_copy(i).start()
 
         @pl.when(i == 0)
         def _():
-            for k in (3, 2, 1):
-                branches.pass_on(k)
+            branches.pass_on(3)
+            branches.pass_on(1)
             branches.keep()
 
-        @pl.when(i == 1)
+        @pl.when(i == 3)
         def _():
             sums_g.middle()
 
-        @pl.when(i == 2)
+        @pl.when(i == 4)
         def _():
             sums_l.middle()
 
-        @pl.when(jnp.logical_and(i > 0, i < 5))
+        @pl.when(i > 0)
         def _():
             other_copy(i - 1).wait_recv()
-            at = (y + i) % 4
+            at = in_turn(4 - i)
             for core in range(2):
                 vector_back(at * 2 + core, proj, par, d_mine, d_in, dproj, small)
-            rows = chunk(at)
-            back = dot_nt(dproj[rows, 0:GA], wx[...].reshape(D, GA))
-            back = back + dot_nt(dproj[rows, GA:COLS], wg[...].reshape(D, GW))
-            back = back + dot(d_steps[rows, :], step_rows[...])
-            d_low[at] = back.astype(BF16).reshape(2, SEQ, D)
-            lowers.across(i % 4).start()
-
-        @pl.when(jnp.logical_and(i > 1, i < 5))
-        def _():
-            lowers.pass_on(i - 1)
+
+        @pl.when(jnp.logical_and(i > 0, i < 3))
+        def _():
+            lower_back(turn(4 - i))
+
+        @pl.when(i == 2)
+        def _():
+            lowers.pass_far()
+
+        @pl.when(i == 4)
+        def _():
+            lowers.pass_on(3)
 
         return carry
 
@@ -935,12 +974,13 @@
         own = jnp.concatenate([steps_back[0:16, r * 96 : (r + 1) * 96], jnp.zeros((16, 32), F32)], axis=1)
         dws[r // 4, r % 4, 0] = own.astype(BF16)
     sums_s.start()
-    for k in (1, 2, 3):
-        small_z(k).wait_recv()
+    lax.fori_loop(0, 2, lambda i, carry: (lower_back(1 - i), carry)[1], 0)
+    small_all_of(zs, sz_s, sz_r).wait_recv()
     part[...] = ((zs[0] + zs[1]) + zs[2]) + zs[3]
     xs[x] = part[...]
     for k in (1, 2, 3):
         small_x(k).start()
+    lowers.pass_on(1)
     sums_x.middle()
     sums_s.middle()
     lowers.keep()
@@ -956,13 +996,13 @@
     def _():
         swap_back.start()
 
-    for k in (1, 2, 3):
-        small_x(k).wait_recv()
+    small_all_of(xs, sx_s, sx_r).wait_recv()
     small_all[rank] = ((xs[0] + xs[1]) + xs[2]) + xs[3]
     all_small.start()
     branches.end()
     h32 = hid[...].astype(F32)
-    mixed[...] = (h32 + jnp.where(live, fb[...], 0.0)).astype(BF16)
+    inverse = lax.rsqrt(column(rank, wide[...]) * (1.0 / INNER) + EPSILON)
+    mixed[...] = (h32 + jnp.where(live, inverse * fb[...], 0.0)).astype(BF16)
     sums_s.end()
     sums_x.end()
     step_cols = dot_tn(fs[0, 0:8], ones(iota((8, 128), 0) == iota((8, 128), 1), F32), HIGHEST)
@@ -1001,12 +1041,10 @@
         gone.sent()
     for gone in (branches, lowers, sums_x, sums_g, sums_l, sums_s):
         gone.finish()
-    for k in (1, 2, 3):
-        small_z(k).wait_send()
-        small_x(k).wait_send()
-    for i in range(4):
-        vector_copy(i).wait_send()
-        other_copy(i).wait_send()
+    small_all_of(zs, sz_s, sz_r).wait_send()
+    small_all_of(xs, sx_s, sx_r).wait_send()
+    remote(act.at[c], act.at[c], v_s.at[0], v_r.at[0], sibling()).wait_send()
+    remote(d_other, d_other, u_s.at[0], u_r.at[0], sibling()).wait_send()
 
     @pl.when(moves)
     def _():
@@ -1090,9 +1128,11 @@
             vm((halves,) + block, F32),
         ]
 
-    seven, pair, four = [dma(GROUP)] * 2, [dma(2, 4)] * 2, [dma(4)] * 2
-    group_reduce = [vm((4, SEQ, D), BF16), vm((3, SEQ, D), BF16), vm((3, SEQ, D), BF16), vm((SEQ, D), F32)]
-    gather = [dma(2, 5, 4), dma(2, 4, 4)]
+    one, group = [dma(1)] * 2, [dma(2), dma(8)]
+    group_reduce = [
+        vm((4, SEQ, D), BF16), vm((3, SEQ, D), BF16), vm((2, SEQ // 2, D), BF16), vm((2, SEQ, D), BF16), vm((SEQ, D), F32)
+    ]
+    gather, two = [dma(2, 2), dma(2, 8)], [dma(2, 2)] * 2
     return pl.pallas_call(
         layer_kernel,
         name="layer",
@@ -1118,10 +1158,8 @@
             vm((2, 16, WIDE), F32), vm((GROUP, 16, CW + 128), BF16), vm((GROUP, 16, CW + 128), BF16),
             vm((GROUP, 16, GW), BF16), vm((GROUP, 16, GW), BF16),
             vm((4, 8, CW), F32), vm((4, 8, CW), F32), vm((8, CW), F32), vm((GROUP, 8, CW), F32),
-            *seven, *gather, *gather, dma(1, 5, 4), dma(1, 4, 4), *gather,
-            *pair, *pair, *seven, *four, *four,
-            *pair, *pair, *[dma(2, 2, 4)] * 6, *[dma(1, 2, 4)] * 2, *seven, *seven,
-            *four, *four, *seven, dma(2), dma(2),
+            *one, *gather, *gather, dma(1, 2), dma(1, 8), *gather, *group, *group, *one, dma(1), dma(4), dma(1), dma(4),
+            *group, *group, *two, *two, *two, dma(1, 2), dma(1, 2), *one, *one, *one, *one, *one, dma(2), dma(2),
         ],
         compiler_params=pltpu.CompilerParams(collective_id=0, has_side_effects=True, vmem_limit_bytes=VMEM_LIMIT),
     )(*given)

time: 138 us -> 123 us (0.89)
  Pallas kernels: 137 us -> 122 us
    pallas_call x1, Pallas kernels: 134 us -> 120 us  [layer(): pl.pallas_call(layer_kernel, name='layer', out_shape=OUT_SHAPES, in_specs...]
where the time goes in v4:
time: 123 us
  Pallas kernels  122 us (99%)
    pallas_call x1, Pallas kernels, layer(): pl.pallas_call(layer_kernel, name='layer', out_shape=OUT_SHAPES, in_specs...  120 us

profile of v4, /device:TPU:1, one launch (start us, length us, event | category | flops | bytes accessed | tf_op | source)
XLA Modules:
  0.0 122.8 jit_solution(6172375063375145774)
XLA Ops:
  0.6 119.6 %layer.1 = (bf16[128,1536]{1,0:T(8,128)(2,1)}, bf16[128,1536]{1,0:T(8,128)(2,1)}, f32[12,6448]{1,0:T(8,128)}, f32[16,128]{1,0:T(8,128)}, f32[24,1536]{1,0:T(8,128)}) custom-call(bf16[128,1536]{1,0:T(8,128)(2,1)} %hid.1, bf16[12,6448]{1,0:T(8,128)(2,1)} %inw.1, bf16[12]{0:T(256)(128)(2,1)} %gain_in.1, bf16[4,26]{1,0:T(4,128)(2,1)} %bitcast.2, ...), custom_call_target="tpu_custom_call" | custom-call | tf_op jit(solution)/shard_map/layer/pallas_call | solution.py:1136
  120.2 2.4 %emit.1 = (bf16[128,1536]{1,0:T(8,128)(2,1)}, bf16[128,1536]{1,0:T(8,128)(2,1)}, f32[12,6448]{1,0:T(8,128)}, f32[12]{0:T(128)}, f32[4,26]{1,0:T(4,128)}, /*index...) custom-call(bf16[128,1536]{1,0:T(8,128)(2,1)} %get-tuple-element.27.mixed, ...), custom_call_target="tpu_custom_call" | custom-call | tf_op jit(solution)/shard_map/emit/pallas_call | solution.py:1108

commit v5 on v4

--- a/solution.py
+++ b/solution.py
@@ -315,33 +315,39 @@
     return out
 
 
-def steps_of(raw, head):
-    step = softplus(raw + head[0:1, :])
-    decay = head[1:2, :] * step
+def steps_forward(b, proj, head, steps, totals):
+    rows = pl.ds(pl.multiple_of(b * SEQ, SEQ), SEQ)
+    step = softplus(proj[rows, ST:] + head[0:1, :])
     lower = ones(iota((SEQ, SEQ), 0) >= iota((SEQ, SEQ), 1), F32)
-    total = dot(lower, decay, HIGHEST)
-    return step, decay, total
-
-
-def mix_forward(b, proj, act, par, head, skip, heads_out):
+    steps[rows, :] = step
+    totals[rows, :] = dot(lower, head[1:2, :] * step, HIGHEST)
+
+
+def activate(v, out, slope):
+    s = sigmoid(v)
+    out[...] = v * s
+    slope[...] = s * (1.0 + v * (1.0 - s))
+
+
+def mix_forward(b, proj, act, par, skip, steps, totals, values, slopes, scores, heads_out):
     row, col = iota((SEQ, SEQ), 0), iota((SEQ, SEQ), 1)
     causal = row >= col
     rows = pl.ds(pl.multiple_of(b * SEQ, SEQ), SEQ)
-    write, read = act[0, rows, :], act[1, rows, :]
-    step, _, total = steps_of(proj[rows, ST:], head)
-    total_t, step_t = total.T, step.T
-    scores = dot_nt(read, write, HIGHEST)
+    total = totals[rows, :]
+    total_t, step_t = total.T, steps[rows, :].T
+    score = dot_nt(act[1, rows, :], act[0, rows, :], HIGHEST)
+    scores[b] = score
     for p in range(3):
-        at = p * 128
-        values = convolve(proj[rows, at : at + 128], par, at, 128)
-        values = values * sigmoid(values)
-        values_low = values.astype(BF16)
+        span = slice(p * 128, p * 128 + 128)
+        activate(convolve(proj[rows, span], par, p * 128, 128), values.at[rows, span], slopes.at[rows, span])
+        value = values[rows, span]
+        value_low = value.astype(BF16)
         parts = []
         for h in (2 * p, 2 * p + 1):
             decays = jnp.exp(jnp.where(causal, total[:, h : h + 1] - total_t[h : h + 1, :], -1e30))
-            mix = (decays * scores * step_t[h : h + 1, :]).astype(BF16)
-            parts.append(dot(mix, values_low))
-        heads_out[rows, at : at + 128] = jnp.where(col < 64, parts[0], parts[1]) + skip[0:1, at : at + 128] * values
+            mix = (decays * score * step_t[h : h + 1, :]).astype(BF16)
+            parts.append(dot(mix, value_low))
+        heads_out[rows, span] = jnp.where(col < 64, parts[0], parts[1]) + skip[0:1, span] * value
 
 
 def weigh(b, proj, par, heads_out, gated):
@@ -383,51 +389,47 @@
     dgated[rows, :] = d_product * silu
 
 
-def conv_back(d_act, raw, v, s, par, small, at):
-    d_conv = d_act * s * (1.0 + v * (1.0 - s))
+def conv_back(d_conv, raw, par, small, at):
     span = slice(at, at + 128)
     back = d_conv * par[4:5, span]
     small[3:4, span] += jnp.sum(d_conv * raw, axis=0, keepdims=True)
     for k in range(3):
-        back = back + earlier(d_conv, 3 - k) * par[k + 1 : k + 2, span]
-        small[k : k + 1, span] += jnp.sum(d_conv * later(raw, 3 - k), axis=0, keepdims=True)
+        ahead = earlier(d_conv, 3 - k)
+        back = back + ahead * par[k + 1 : k + 2, span]
+        small[k : k + 1, span] += jnp.sum(ahead * raw, axis=0, keepdims=True)
     small[4:5, span] += jnp.sum(d_conv, axis=0, keepdims=True)
     return back
 
 
-def mix_back(b, core, proj, act, par, head, skip, d_heads, dproj, d_steps, small, d_mine, d_other):
+def mix_back(
+    b, core, proj, act, par, head, skip, steps, totals, values, slopes, scores, d_heads, dproj, d_steps, small, d_mine,
+    d_other,
+):
     row, col = iota((SEQ, SEQ), 0), iota((SEQ, SEQ), 1)
     later_ok = col >= row
     left, right = col < 64, col >= 64
     suffix = ones(row >= col)
     before = row < col
     rows = pl.ds(pl.multiple_of(b * SEQ, SEQ), SEQ)
-
-    write, read = act[0, rows, :], act[1, rows, :]
-    raw_step = proj[rows, ST:]
-    step, decay, total = steps_of(raw_step, head)
+    step, total = steps[rows, :], totals[rows, :]
     total_t = total.T
-    scores_t = dot_nt(write, read, HIGHEST)
+    scores_t = scores[b].T
     d_scores = jnp.zeros((SEQ, SEQ), F32)
     direct = jnp.zeros((SEQ, SEQ), F32)
     lines = []
     for p in range(3):
-        at = p * 128
-        span = slice(at, at + 128)
+        span = slice(p * 128, p * 128 + 128)
         d_out = d_heads[rows, span]
-        raw = proj[rows, span]
-        pre = convolve(raw, par, at, 128)
-        sig = sigmoid(pre)
-        values = pre * sig
-        small[6:7, span] += jnp.sum(d_out * values, axis=0, keepdims=True)
-        values_low = values.astype(BF16)
+        value = values[rows, span]
+        small[6:7, span] += jnp.sum(d_out * value, axis=0, keepdims=True)
+        value_low = value.astype(BF16)
         d_low = d_out.astype(BF16)
         parts = []
         for i, h in enumerate((2 * p, 2 * p + 1)):
             decays = jnp.exp(jnp.where(later_ok, total_t[h : h + 1, :] - total[:, h : h + 1], -1e30))
             size = step[:, h : h + 1]
             own = jnp.where(left if i == 0 else right, d_out, 0.0).astype(BF16)
-            d_mix = decays * dot_nt(values_low, own)
+            d_mix = decays * dot_nt(value_low, own)
             d_scores = d_scores + d_mix * size
             per_step = (d_mix * scores_t).astype(BF16)
             tail = dot(per_step, suffix)
@@ -436,32 +438,30 @@
             mix = (decays * scores_t * size).astype(BF16)
             parts.append(dot(mix, d_low))
         d_values = jnp.where(left, parts[0], parts[1]) + skip[0:1, span] * d_out
-        dproj[rows, span] = conv_back(d_values, raw, pre, sig, par, small, at).astype(BF16)
+        d_conv = d_values * slopes[rows, span]
+        dproj[rows, span] = conv_back(d_conv, proj[rows, span], par, small, p * 128).astype(BF16)
     d_decay = jnp.concatenate(lines + [jnp.zeros((SEQ - OWN, SEQ), F32)], axis=0).T
     d_step = direct + head[1:2, :] * d_decay
-    d_raw = d_step * sigmoid(raw_step + head[0:1, :])
+    d_raw = d_step * sigmoid(proj[rows, ST:] + head[0:1, :])
     small[7:8, 0:128] += jnp.sum(d_raw, axis=0, keepdims=True)
-    small[7:8, 128:256] += jnp.sum(d_decay * decay, axis=0, keepdims=True)
+    small[7:8, 128:256] += jnp.sum(d_decay * head[1:2, :] * step, axis=0, keepdims=True)
     d_low = d_scores.astype(BF16)
-    d_write = dot(d_low, read.astype(BF16))
-    d_read = dot_tn(d_low, write.astype(BF16))
+    d_write = dot(d_low, act[1, rows, :].astype(BF16))
+    d_read = dot_tn(d_low, act[0, rows, :].astype(BF16))
     d_mine[rows, :] = jnp.where(core == 0, d_write, d_read)
     d_other[rows, :] = jnp.where(core == 0, d_read, d_write)
     d_steps[rows, :] = d_raw.astype(BF16)
 
 
-def vector_forward(b, core, proj, act, par):
+def vector_forward(b, core, proj, act, slopes, par):
     rows = pl.ds(pl.multiple_of(b * SEQ, SEQ), SEQ)
-    v = convolve(proj[rows, GW:CW], par, GW, 128)
-    act[core, rows, :] = v * sigmoid(v)
-
-
-def vector_back(b, proj, par, d_mine, d_in, dproj, small):
+    activate(convolve(proj[rows, GW:CW], par, GW, 128), act.at[core, rows, :], slopes.at[rows, GW:CW])
+
+
+def vector_back(b, proj, par, slopes, d_mine, d_in, dproj, small):
     rows = pl.ds(pl.multiple_of(b * SEQ, SEQ), SEQ)
-    raw = proj[rows, GW:CW]
-    v = convolve(raw, par, GW, 128)
-    d = d_mine[rows, :] + d_in[rows, :]
-    dproj[rows, GW:CW] = conv_back(d, raw, v, sigmoid(v), par, small, GW).astype(BF16)
+    d_conv = (d_mine[rows, :] + d_in[rows, :]) * slopes[rows, GW:CW]
+    dproj[rows, GW:CW] = conv_back(d_conv, proj[rows, GW:CW], par, small, GW).astype(BF16)
 
 
 class PlaneReduce:
@@ -602,8 +602,8 @@
     mixed, in_grad, dinw, dvecs, doutw,
     vectors, heads_in, tap_rows,
     split, joined, block, gblock, params, outl, placed, live_grd,
-    wx, wg, praw, plane, hall, gall, low, proj, act, step_rows, heads_out, dgated, ow, par, head, skip, sums, slots, wide,
-    gated, dproj, d_steps, d_mine, d_other, d_in, d_low, dwx, dwg, dow, dws, small,
+    wx, wg, praw, plane, hall, gall, low, proj, act, step_rows, steps, totals, values, slopes, scores, heads_out, dgated, ow, par, head, skip, sums, slots, wide,
+    gated, dproj, d_steps, d_mine, d_other, d_in, dwx, dwg, dow, dws, small,
     gb, mb, tb, lb, fb, gd, md, td, ld, fd, gx, mx, lx, fx, gg, mg, lg, fg, gl, ml, ll, fl, gs, ms, ls, fs,
     swapped, cut, rows_in, gcut, grows_in, zs, xs, part, small_all,
     a_s, a_r, wx_s, wx_r, wg_s, wg_r, p_s, p_r, l_s, l_r, h_s, h_r, g_s, g_r, n_s, n_r, v_s, v_r, u_s, u_r,
@@ -696,6 +696,7 @@
     params[...] = both[96:128, 0:384]
     vecs.start()
     first_w.start()
+    grads.start()
     wx[z, x] = block[...]
     wg[z, x] = gblock[...]
     praw[z, x, 0] = params[...]
@@ -717,14 +718,12 @@
     plane[z, x] = placed[...]
     hidden.forward(1)
     hidden.forward(3)
-    grads.start()
     vecs.relay()
     first_w.relay()
     vecs.finish()
     unpack_params(praw, rank, c, par, step_rows)
     gate_w.forward()
     lines.forward()
-    first_w.finish()
 
     def chunk(i):
         return pl.ds(pl.multiple_of(i * 256, 256), 256)
@@ -743,11 +742,17 @@
         here = act.at[1 - c, chunk(in_turn(i))]
         return remote(here, here, v_s.at[0], v_r.at[i], sibling())
 
+    def prepare(at):
+        for core in range(2):
+            h = hall[at, core].astype(F32)
+            scale = lax.rsqrt(jnp.mean(h * h, axis=1, keepdims=True) + EPSILON)
+            rows = pl.ds(pl.multiple_of(at * 256 + core * SEQ, SEQ), SEQ)
+            low[rows, :] = (h * scale * par[0:1, :]).astype(BF16)
+        proj[chunk(at), ST:] = dot_nt(low[chunk(at), :], step_rows[...])
+        for core in range(2):
+            steps_forward(at * 2 + core, proj, head, steps, totals)
+
     def forward(i, carry):
-        @pl.when(i == 0)
-        def _():
-            hidden.arrived(0)
-
         @pl.when(i == 1)
         def _():
             hidden.arrived(1)
@@ -762,25 +767,20 @@
         def _():
             hidden.arrived(2)
             lines.relay()
-
-        @pl.when(i == 4)
-        def _():
             grads.forward(1)
             grads.forward(3)
 
+        @pl.when(jnp.logical_and(i > 0, i < 4))
+        def _():
+            prepare(in_turn(i))
+
         @pl.when(i < 4)
         def _():
             at = in_turn(i)
-            for core in range(2):
-                h = hall[at, core].astype(F32)
-                scale = lax.rsqrt(jnp.mean(h * h, axis=1, keepdims=True) + EPSILON)
-                rows = pl.ds(pl.multiple_of(at * 256 + core * SEQ, SEQ), SEQ)
-                low[rows, :] = (h * scale * par[0:1, :]).astype(BF16)
             rows = chunk(at)
             proj[rows, 0:GA] = dot(low[rows, :], wx[...].reshape(D, GA))
-            proj[rows, ST:] = dot_nt(low[rows, :], step_rows[...])
             for core in range(2):
-                vector_forward(at * 2 + core, c, proj, act, par)
+                vector_forward(at * 2 + core, c, proj, act, slopes, par)
             vector_copy(i).start()
 
         @pl.when(i > 0)
@@ -788,10 +788,13 @@
             vector_arrival(i - 1).wait_recv()
             at = in_turn(i - 1)
             for core in range(2):
-                mix_forward(at * 2 + core, proj, act, par, head, skip, heads_out)
+                mix_forward(at * 2 + core, proj, act, par, skip, steps, totals, values, slopes, scores, heads_out)
 
         return carry
 
+    hidden.arrived(0)
+    prepare(y)
+    first_w.finish()
     lax.fori_loop(0, 5, forward, 0)
     gate_w.finish()
 
@@ -808,17 +811,6 @@
     lax.fori_loop(0, GROUP, weighed, 0)
     lines.finish()
     unfold_out_weight(plane, ow)
-    hidden.sent()
-    branch = hall
-    branches = GroupReduce(branch, gb, mb, tb, lb, fb, b_s, b_r)
-
-    def out_term(i, carry):
-        at = in_turn(3 - i)
-        branch[at] = dot(gated[chunk(at), :], ow[...]).astype(BF16).reshape(2, SEQ, D)
-        branches.across(turn(3 - i)).start()
-        return carry
-
-    lax.fori_loop(0, 4, out_term, 0)
     grads.forward(2)
     grads.arrived(0)
 
@@ -848,7 +840,17 @@
     norms.start()
     slots[rank] = sums[...]
     small[...] = jnp.zeros_like(small)
-    branches.pass_far()
+    hidden.sent()
+    branch = hall
+    branches = GroupReduce(branch, gb, mb, tb, lb, fb, b_s, b_r)
+
+    def out_term(i, carry):
+        at = in_turn(3 - i)
+        branch[at] = dot(gated[chunk(at), :], ow[...]).astype(BF16).reshape(2, SEQ, D)
+        branches.across(turn(3 - i)).start()
+        return carry
+
+    lax.fori_loop(0, 4, out_term, 0)
     norms.finish()
     total = slots[0]
     for q in range(1, GROUP):
@@ -860,7 +862,9 @@
         return carry
 
     lax.fori_loop(0, GROUP, norms_back, 0)
-
+    branches.pass_far()
+
+    d_low = gall
     lowers = GroupReduce(d_low, gd, md, td, ld, fd, d_s, d_r)
     sums_x = PlaneReduce(dwx, gx, mx, lx, fx, rx_s, rx_r)
     sums_g = PlaneReduce(dwg, gg, mg, lg, fg, rg_s, rg_r)
@@ -879,7 +883,6 @@
     def small_all_of(buf, send, recv):
         here = buf.at[pl.ds(0, 3)]
         return remote(here, here, send.at[0], recv.at[0], on_z(1))
-
 
     def slab(k, span):
         at = (z + k) % 4
@@ -901,6 +904,7 @@
         for h in range(2):
             dow[j % 8 // 2, j // 8 * 2 + j % 2, h] = fold[:, h * WIDE : (h + 1) * WIDE]
     sums_l.start()
+    grads.sent()
 
     def other_copy(i):
         rows = chunk(in_turn(3 - i))
@@ -920,7 +924,10 @@
         def _():
             at = in_turn(3 - i)
             for core in range(2):
-                mix_back(at * 2 + core, c, proj, act, par, head, skip, dgated, dproj, d_steps, small, d_mine, d_other)
+                mix_back(
+                    at * 2 + core, c, proj, act, par, head, skip, steps, totals, values, slopes, scores, dgated, dproj,
+                    d_steps, small, d_mine, d_other,
+                )
             other_copy(i).start()
 
         @pl.when(i == 0)
@@ -929,32 +936,20 @@
             branches.pass_on(1)
             branches.keep()
 
-        @pl.when(i == 3)
-        def _():
-            sums_g.middle()
-
-        @pl.when(i == 4)
-        def _():
-            sums_l.middle()
-
         @pl.when(i > 0)
         def _():
             other_copy(i - 1).wait_recv()
             at = in_turn(4 - i)
             for core in range(2):
-                vector_back(at * 2 + core, proj, par, d_mine, d_in, dproj, small)
-
-        @pl.when(jnp.logical_and(i > 0, i < 3))
-        def _():
-            lower_back(turn(4 - i))
-
-        @pl.when(i == 2)
+                vector_back(at * 2 + core, proj, par, slopes, d_mine, d_in, dproj, small)
+
+        @pl.when(i == 1)
+        def _():
+            lower_back(2)
+
+        @pl.when(i == 3)
         def _():
             lowers.pass_far()
-
-        @pl.when(i == 4)
-        def _():
-            lowers.pass_on(3)
 
         return carry
 
@@ -969,18 +964,26 @@
             sums_x.first(1, k).start()
     for k in (2, 1, 3):
         sums_x.first(0, k).start()
+    sums_g.middle()
+    sums_l.middle()
     steps_back = dot_tn(d_steps[...], low[...])
     for r in range(16):
         own = jnp.concatenate([steps_back[0:16, r * 96 : (r + 1) * 96], jnp.zeros((16, 32), F32)], axis=1)
         dws[r // 4, r % 4, 0] = own.astype(BF16)
     sums_s.start()
-    lax.fori_loop(0, 2, lambda i, carry: (lower_back(1 - i), carry)[1], 0)
+
+    def lower_backs(i, carry):
+        lower_back(turn(2 - i))
+        return carry
+
+    lax.fori_loop(0, 3, lower_backs, 0)
+    lowers.pass_on(3)
+    lowers.pass_on(1)
     small_all_of(zs, sz_s, sz_r).wait_recv()
     part[...] = ((zs[0] + zs[1]) + zs[2]) + zs[3]
     xs[x] = part[...]
     for k in (1, 2, 3):
         small_x(k).start()
-    lowers.pass_on(1)
     sums_x.middle()
     sums_s.middle()
     lowers.keep()
@@ -1035,9 +1038,10 @@
     through = scale * (d_normed - normed * jnp.mean(d_normed * normed, axis=1, keepdims=True))
     in_grad[...] = (grd[...].astype(F32) + through).astype(BF16)
     gate_rows.finish()
+    gate_total = finish_gate(grows_in, inw, dinw)
     cut_rows.finish()
-    finish_rows(rows_in, grows_in, inw, vectors, dinw, dvecs)
-    for gone in (grads, first_w, gate_w, vecs, lines, cuts, norms, cut_rows, gate_rows, all_small):
+    finish_rows(rows_in, gate_total, inw, vectors, dinw, dvecs)
+    for gone in (first_w, gate_w, vecs, lines, cuts, norms, cut_rows, gate_rows, all_small):
         gone.sent()
     for gone in (branches, lowers, sums_x, sums_g, sums_l, sums_s):
         gone.finish()
@@ -1076,17 +1080,22 @@
     dvecs[8:12] = conv[0:4]
 
 
-def finish_rows(rows, gate_rows, inw, vectors, dinw, dvecs):
+def finish_gate(gate_rows, inw, dinw):
+    for q in range(GROUP):
+        dinw[:, q * GW : (q + 1) * GW] = gate_rows[q].astype(F32)[0:KIN]
+    return jnp.sum(dinw[:, 0:INNER] * inw[:, 0:INNER].astype(F32), axis=1, keepdims=True)
+
+
+def finish_rows(rows, gate_total, inw, vectors, dinw, dvecs):
     shared = [jnp.zeros((KIN, 128), F32), jnp.zeros((KIN, 128), F32)]
     for q in range(GROUP):
         own = rows[q].astype(F32)[0:KIN]
         dinw[:, INNER + q * GW : INNER + (q + 1) * GW] = own[:, 0:GW]
-        dinw[:, q * GW : (q + 1) * GW] = gate_rows[q].astype(F32)[0:KIN]
         dinw[:, STEP + q * OWN : STEP + (q + 1) * OWN] = own[:, CW : CW + OWN]
         shared[q % 2] = shared[q % 2] + own[:, GW:CW]
     dinw[:, 2 * INNER : 2 * INNER + 128] = shared[0]
     dinw[:, 2 * INNER + 128 : STEP] = shared[1]
-    total = jnp.sum(dinw[...] * inw[...].astype(F32), axis=1, keepdims=True)
+    total = gate_total + jnp.sum(dinw[:, INNER:] * inw[:, INNER:].astype(F32), axis=1, keepdims=True)
     spread = jnp.where(iota((KIN, 128), 0) == iota((KIN, 128), 1), total, 0.0)
     gain = jnp.where(iota((1, 128), 1) < KIN, vectors[0:1], 1.0)
     dvecs[0:1] = jnp.sum(spread, axis=0, keepdims=True) / gain
@@ -1146,11 +1155,12 @@
             vm((4, 4, 2, 48, GA), BF16), vm((4, 4, 2, 48, GW), BF16), vm((4, 4, 1, 32, 384), BF16),
             vm((4, 4, 2, 16, WIDE), BF16), vm((4, 2, SEQ, D), BF16), vm((4, 2, SEQ, D), BF16),
             vm((ROWS, D), BF16), vm((ROWS, COLS + 128), F32), vm((2, ROWS, 128), F32), vm((128, D), BF16),
+            vm((ROWS, 128), F32), vm((ROWS, 128), F32), vm((ROWS, GW), F32), vm((ROWS, CW), F32), vm((GROUP, SEQ, SEQ), F32),
             vm((ROWS, GW), F32), vm((ROWS, GW), F32), vm((GW, D), BF16),
             vm((8, D), F32), vm((8, 128), F32), vm((1, GW), F32),
             vm((16, SEQ), F32), vm((GROUP, 16, SEQ), F32), vm((SEQ, SEQ), F32),
             vm((ROWS, GW), BF16), vm((ROWS, COLS), BF16), vm((ROWS, 128), BF16),
-            vm((ROWS, 128), F32), vm((ROWS, 128), F32), vm((ROWS, 128), F32), vm((4, 2, SEQ, D), BF16),
+            vm((ROWS, 128), F32), vm((ROWS, 128), F32), vm((ROWS, 128), F32),
             vm((4, 4, 2, 48, GA), BF16), vm((4, 4, 2, 48, GW), BF16), vm((4, 4, 2, 16, WIDE), BF16),
             vm((4, 4, 1, 16, 128), BF16), vm((8, CW), F32),
             *group_reduce, *group_reduce, *plane_reduce(2, 48, GA), *plane_reduce(2, 48, GW),

time: 123 us -> 118 us (0.959)
  Pallas kernels: 122 us -> 117 us
    pallas_call x1, Pallas kernels: 120 us -> 115 us  [layer(): pl.pallas_call(layer_kernel, name='layer', out_shape=OUT_SHAPES, in_specs...]
where the time goes in v5:
time: 118 us
  Pallas kernels  117 us (99%)
    pallas_call x1, Pallas kernels, layer(): pl.pallas_call(layer_kernel, name='layer', out_shape=OUT_SHAPES, in_specs...  115 us
    pallas_call x1, Pallas kernels, emit(): pl.pallas_call(emit_kernel, name='emit', out_shape=(*OUT_SHAPES[0:3], lin...  2.42 us

profile of v5, /device:TPU:1, one launch (start us, length us, event | category | flops | bytes accessed | tf_op | source)
XLA Modules:
  0.0 118.0 jit_solution(6111400137274107490)
XLA Ops:
  0.6 114.8 %layer.1 = (bf16[128,1536]{1,0:T(8,128)(2,1)}, bf16[128,1536]{1,0:T(8,128)(2,1)}, f32[12,6448]{1,0:T(8,128)}, f32[16,128]{1,0:T(8,128)}, f32[24,1536]{1,0:T(8,128)}) custom-call(bf16[128,1536]{1,0:T(8,128)(2,1)} %hid.1, bf16[12,6448]{1,0:T(8,128)(2,1)} %inw.1, bf16[12]{0:T(256)(128)(2,1)} %gain_in.1, bf16[4,26]{1,0:T(4,128)(2,1)} %bitcast.2, ...), custom_call_target="tpu_custom_call" | custom-call | tf_op jit(solution)/shard_map/layer/pallas_call | solution.py:1145
  115.4 2.4 %emit.1 = (bf16[128,1536]{1,0:T(8,128)(2,1)}, bf16[128,1536]{1,0:T(8,128)(2,1)}, f32[12,6448]{1,0:T(8,128)}, f32[12]{0:T(128)}, f32[4,26]{1,0:T(4,128)}, /*index...) custom-call(bf16[128,1536]{1,0:T(8,128)(2,1)} %get-tuple-element.27.mixed, ...), custom_call_target="tpu_custom_call" | custom-call | tf_op jit(solution)/shard_map/emit/pallas_call | solution.py:1117

commit v6 on v5

--- a/solution.py
+++ b/solution.py
@@ -350,24 +350,23 @@
         heads_out[rows, span] = jnp.where(col < 64, parts[0], parts[1]) + skip[0:1, span] * value
 
 
-def weigh(b, proj, par, heads_out, gated):
-    rows = pl.ds(pl.multiple_of(b * SEQ, SEQ), SEQ)
-    gate = proj[rows, GA:COLS]
-    gated[rows, :] = (heads_out[rows, :] * gate * sigmoid(gate) * par[6:7, 0:GW]).astype(BF16)
-
-
-def column(at, values):
-    return jnp.sum(jnp.where(iota((SEQ, SEQ), 1) == at, values, 0.0), axis=1, keepdims=True)
-
-
-def norm_sums(b, proj, par, heads_out, dgated, acc):
+def weigh(b, proj, par, heads_out, gated, acc):
     rows = pl.ds(pl.multiple_of(b * SEQ, SEQ), SEQ)
     gate = proj[rows, GA:COLS]
     product = heads_out[rows, :] * gate * sigmoid(gate)
+    gated[rows, :] = (product * par[6:7, 0:GW]).astype(BF16)
     squares = jnp.sum(product * product, axis=1, keepdims=True)
-    crosses = jnp.sum(product * dgated[rows, :] * par[6:7, 0:GW], axis=1, keepdims=True)
-    col = iota((SEQ, SEQ), 1)
-    return jnp.where(col == b, squares, jnp.where(col == b + 8, crosses, acc))
+    return jnp.where(iota((SEQ, SEQ), 1) == b, squares, acc)
+
+
+def column(at, values):
+    return jnp.sum(jnp.where(iota((SEQ, SEQ), 1) == at, values, 0.0), axis=1, keepdims=True)
+
+
+def norm_sums(b, gated, dgated, acc):
+    rows = pl.ds(pl.multiple_of(b * SEQ, SEQ), SEQ)
+    crosses = jnp.sum(gated[rows, :].astype(F32) * dgated[rows, :], axis=1, keepdims=True)
+    return jnp.where(iota((SEQ, SEQ), 1) == b + 8, crosses, acc)
 
 
 def norm_back(b, proj, par, wide, heads_out, dgated, gated, dproj, small):
@@ -804,11 +803,10 @@
 
     lax.fori_loop(0, ROWS // 256, project_gate, 0)
 
-    def weighed(b, carry):
-        weigh(b, proj, par, heads_out, gated)
-        return carry
-
-    lax.fori_loop(0, GROUP, weighed, 0)
+    def weighed(b, acc):
+        return weigh(b, proj, par, heads_out, gated, acc)
+
+    wide[...] = lax.fori_loop(0, GROUP, weighed, jnp.zeros((SEQ, SEQ), F32))
     lines.finish()
     unfold_out_weight(plane, ow)
     grads.forward(2)
@@ -832,9 +830,7 @@
         return carry
 
     lax.fori_loop(0, 4, pull, 0)
-    acc = lax.fori_loop(
-        0, GROUP, lambda b, acc: norm_sums(b, proj, par, heads_out, dgated, acc), jnp.zeros((SEQ, SEQ), F32)
-    )
+    acc = lax.fori_loop(0, GROUP, lambda b, acc: norm_sums(b, gated, dgated, acc), wide[...])
     sums[...] = acc.T[0:16, :]
     norms = Members(lambda q: sums, slots, n_s, n_r)
     norms.start()
@@ -861,8 +857,8 @@
         norm_back(b, proj, par, wide, heads_out, dgated, gated, dproj, small)
         return carry
 
+    branches.pass_far()
     lax.fori_loop(0, GROUP, norms_back, 0)
-    branches.pass_far()
 
     d_low = gall
     lowers = GroupReduce(d_low, gd, md, td, ld, fd, d_s, d_r)
@@ -889,13 +885,6 @@
         own = low[:, pl.ds(pl.multiple_of(at * GW, GW), GW)]
         return at, dot_tn(own, dproj[:, span]).astype(BF16).reshape(4, 2, 48, span.stop - span.start)
 
-    for k in (2, 1, 3, 0):
-        at, rows = slab(k, slice(GA, COLS))
-        dwg[at] = rows
-        if k:
-            sums_g.first(1, k).start()
-    for k in (2, 1, 3):
-        sums_g.first(0, k).start()
     out = dot_tn(gated[...], gall[...].reshape(ROWS, D))
     for j in range(16):
         piece = out[j * KOUT : (j + 1) * KOUT]
@@ -904,6 +893,13 @@
         for h in range(2):
             dow[j % 8 // 2, j // 8 * 2 + j % 2, h] = fold[:, h * WIDE : (h + 1) * WIDE]
     sums_l.start()
+    for k in (2, 1, 3, 0):
+        at, rows = slab(k, slice(GA, COLS))
+        dwg[at] = rows
+        if k:
+            sums_g.first(1, k).start()
+    for k in (2, 1, 3):
+        sums_g.first(0, k).start()
     grads.sent()
 
     def other_copy(i):
@@ -942,6 +938,10 @@
             at = in_turn(4 - i)
             for core in range(2):
                 vector_back(at * 2 + core, proj, par, slopes, d_mine, d_in, dproj, small)
+
+        @pl.when(i == 4)
+        def _():
+            sums_l.middle()
 
         @pl.when(i == 1)
         def _():
@@ -965,7 +965,6 @@
     for k in (2, 1, 3):
         sums_x.first(0, k).start()
     sums_g.middle()
-    sums_l.middle()
     steps_back = dot_tn(d_steps[...], low[...])
     for r in range(16):
         own = jnp.concatenate([steps_back[0:16, r * 96 : (r + 1) * 96], jnp.zeros((16, 32), F32)], axis=1)

time: 118 us -> 117 us (level)
    pallas_call x1, Pallas kernels: 115 us -> 113 us  [layer(): pl.pallas_call(layer_kernel, name='layer', out_shape=OUT_SHAPES, in_specs...]
where the time goes in v6:
time: 117 us; the launch traced here: 116 us
  Pallas kernels  116 us (99%)
    pallas_call x1, Pallas kernels, layer(): pl.pallas_call(layer_kernel, name='layer', out_shape=OUT_SHAPES, in_specs...  113 us
    pallas_call x1, Pallas kernels, emit(): pl.pallas_call(emit_kernel, name='emit', out_shape=(*OUT_SHAPES[0:3], lin...  2.42 us

profile of v6, /device:TPU:1, one launch (start us, length us, event | category | flops | bytes accessed | tf_op | source)
XLA Modules:
  0.0 116.4 jit_solution(142066737453263552)
XLA Ops:
  0.6 113.1 %layer.1 = (bf16[128,1536]{1,0:T(8,128)(2,1)}, bf16[128,1536]{1,0:T(8,128)(2,1)}, f32[12,6448]{1,0:T(8,128)}, f32[16,128]{1,0:T(8,128)}, f32[24,1536]{1,0:T(8,128)}) custom-call(bf16[128,1536]{1,0:T(8,128)(2,1)} %hid.1, bf16[12,6448]{1,0:T(8,128)(2,1)} %inw.1, bf16[12]{0:T(256)(128)(2,1)} %gain_in.1, bf16[4,26]{1,0:T(4,128)(2,1)} %bitcast.2, ...), custom_call_target="tpu_custom_call" | custom-call | tf_op jit(solution)/shard_map/layer/pallas_call | solution.py:1144
  113.8 2.4 %emit.1 = (bf16[128,1536]{1,0:T(8,128)(2,1)}, bf16[128,1536]{1,0:T(8,128)(2,1)}, f32[12,6448]{1,0:T(8,128)}, f32[12]{0:T(128)}, f32[4,26]{1,0:T(4,128)}, /*index...) custom-call(bf16[128,1536]{1,0:T(8,128)(2,1)} %get-tuple-element.27.mixed, ...), custom_call_target="tpu_custom_call" | custom-call | tf_op jit(solution)/shard_map/emit/pallas_call | solution.py:1116

commit v7 on v6

--- a/solution.py
+++ b/solution.py
@@ -943,14 +943,6 @@
         def _():
             sums_l.middle()
 
-        @pl.when(i == 1)
-        def _():
-            lower_back(2)
-
-        @pl.when(i == 3)
-        def _():
-            lowers.pass_far()
-
         return carry
 
     lax.fori_loop(0, 5, backward, 0)
@@ -972,10 +964,15 @@
     sums_s.start()
 
     def lower_backs(i, carry):
-        lower_back(turn(2 - i))
+        lower_back(turn(3 - i))
+
+        @pl.when(i == 1)
+        def _():
+            lowers.pass_far()
+
         return carry
 
-    lax.fori_loop(0, 3, lower_backs, 0)
+    lax.fori_loop(0, 4, lower_backs, 0)
     lowers.pass_on(3)
     lowers.pass_on(1)
     small_all_of(zs, sz_s, sz_r).wait_recv()

time: 117 us -> 122 us (1.043)
  Pallas kernels: 116 us -> 121 us
    pallas_call x1, Pallas kernels: 113 us -> 119 us  [layer(): pl.pallas_call(layer_kernel, name='layer', out_shape=OUT_SHAPES, in_specs...]
where the time goes in v7:
time: 122 us
  Pallas kernels  121 us (99%)
    pallas_call x1, Pallas kernels, layer(): pl.pallas_call(layer_kernel, name='layer', out_shape=OUT_SHAPES, in_specs...  119 us

profile of v7, /device:TPU:1, one launch (start us, length us, event | category | flops | bytes accessed | tf_op | source)
XLA Modules:
  0.0 121.9 jit_solution(12995820738908254132)
XLA Ops:
  0.6 118.6 %layer.1 = (bf16[128,1536]{1,0:T(8,128)(2,1)}, bf16[128,1536]{1,0:T(8,128)(2,1)}, f32[12,6448]{1,0:T(8,128)}, f32[16,128]{1,0:T(8,128)}, f32[24,1536]{1,0:T(8,128)}) custom-call(bf16[128,1536]{1,0:T(8,128)(2,1)} %hid.1, bf16[12,6448]{1,0:T(8,128)(2,1)} %inw.1, bf16[12]{0:T(256)(128)(2,1)} %gain_in.1, bf16[4,26]{1,0:T(4,128)(2,1)} %bitcast.2, ...), custom_call_target="tpu_custom_call" | custom-call | tf_op jit(solution)/shard_map/layer/pallas_call | solution.py:1141
  119.3 2.4 %emit.1 = (bf16[128,1536]{1,0:T(8,128)(2,1)}, bf16[128,1536]{1,0:T(8,128)(2,1)}, f32[12,6448]{1,0:T(8,128)}, f32[12]{0:T(128)}, f32[4,26]{1,0:T(4,128)}, /*index...) custom-call(bf16[128,1536]{1,0:T(8,128)(2,1)} %get-tuple-element.27.mixed, ...), custom_call_target="tpu_custom_call" | custom-call | tf_op jit(solution)/shard_map/emit/pallas_call | solution.py:1113
